TPU v7x, 32 devices: a whole 2x2x4 slice. The times are simulated.
32 devices in a mesh: seq: 8 (over z, x), batch: 4 (over y, core).
Axes of the slice: x: 2, y: 2, z: 4, core: 2. Of those that a mesh axis runs over, the one named last changes fastest.
Arguments:
- tokens: bfloat16 [8, 2048, 1024], P('batch', 'seq'), may hold values from -6 to 6
- starts: int32 [8, 2048], P('batch', 'seq'), may hold values from 0 to 1, as said below
- entry_gain: float32 [1024], replicated, may hold values from 0.25 to 1.75
- query_weight: bfloat16 [1024, 1024], P('seq'), may hold values from -0.1875 to 0.1875
- key_weight: bfloat16 [1024, 1024], P('seq'), may hold values from -0.1875 to 0.1875
- value_weight: bfloat16 [1024, 1024], P('seq'), may hold values from -0.1875 to 0.1875
- gate_weight: bfloat16 [1024, 1024], P('seq'), may hold values from -0.1875 to 0.1875
- head_gain: float32 [1024], replicated, may hold values from 0.25 to 1.75
- output_weight: bfloat16 [1024, 1024], P('seq'), may hold values from -0.375 to 0.375
- middle_gain: float32 [1024], replicated, may hold values from 0.25 to 1.75
- left_weight: bfloat16 [1024, 2816], P('seq'), may hold values from -0.1875 to 0.1875
- right_weight: bfloat16 [1024, 2816], P('seq'), may hold values from -0.1875 to 0.1875
- down_weight: bfloat16 [2816, 1024], P(None, 'seq'), may hold values from -0.109375 to 0.109375
- cotangent: bfloat16 [8, 2048, 1024], P('batch', 'seq'), may hold values from -6 to 6
Outputs:
- mixed: bfloat16 [8, 2048, 1024], P('batch', 'seq')
- input_gradient: float32 [8, 2048, 1024], P('batch', 'seq')
- entry_gradient: float32 [1024], P('seq')
- query_gradient: float32 [1024, 1024], P('seq')
- key_gradient: float32 [1024, 1024], P('seq')
- value_gradient: float32 [1024, 1024], P('seq')
- gate_gradient: float32 [1024, 1024], P('seq')
- head_gradient: float32 [1024], P('seq')
- output_gradient: float32 [1024, 1024], P('seq')
- middle_gradient: float32 [1024], P('seq')
- left_gradient: float32 [1024, 2816], P('seq')
- right_gradient: float32 [1024, 2816], P('seq')
- down_gradient: float32 [2816, 1024], P(None, 'seq')
Inputs may be any that keep to these rules, and one draw needn't show every extreme that they name: `starts`: A row's first position never holds a start.
All inputs are finite; a program needn't handle non-finite values.
Results may differ from a plain program's by a relative error of at most 0.019.
Values may be sent and summed in bfloat16 or wider, within the bound.
No kernel may reach another device: no remote copies, remote signals or barrier semaphores. Data moves between devices by JAX's collectives and lax.ppermute only.
A program may use at most 256 MiB of HBM per device.

v0:
```python
import jax
import jax.numpy as jnp
from jax import lax
from jax.sharding import PartitionSpec as P

HEADS = 16
HEAD = 64


EPSILON = 1e-06


def inverse_rms(values):
    return lax.rsqrt(jnp.mean(values * values, axis=-1, keepdims=True) + EPSILON)


def project(left, right):
    return jnp.dot(left, right, preferred_element_type=jnp.float32)


def contract_rows(left, right):
    return lax.dot_general(
        left, right, (((0,), (0,)), ((), ())), preferred_element_type=jnp.float32
    )


def project_back(left, right):
    return lax.dot_general(
        left, right, (((1,), (1,)), ((), ())), preferred_element_type=jnp.float32
    )


def norm_back(upstream, values, inverse, gain):
    scaled = upstream * gain
    gain_part = jnp.sum(upstream * values * inverse, axis=0)
    cubed = inverse * inverse * inverse
    return (
        inverse * scaled - values * cubed * jnp.mean(scaled * values, axis=-1, keepdims=True),
        gain_part,
    )


def row_mask(segment_row):
    order = jnp.arange(segment_row.shape[0])
    return (
        (segment_row[:, None] == segment_row[None, :]) & (order[:, None] >= order[None, :])
    ).astype(jnp.float32)


def row_weights(query_row, keys_row, allowed):
    scores = jnp.einsum("thd,shd->hts", query_row, keys_row, preferred_element_type=jnp.float32)
    return (scores * allowed[None]).astype(jnp.bfloat16)


def forward_row(item):
    query_row, keys_row, values_row, segment_row, state_low = item
    weights_low = row_weights(query_row, keys_row, row_mask(segment_row))
    inside = jnp.einsum("hts,shd->thd", weights_low, values_row, preferred_element_type=jnp.float32)
    inherit = (segment_row == 0).astype(jnp.bfloat16)[:, None, None]
    carried = jnp.einsum(
        "thd,hde->the", query_row * inherit, state_low, preferred_element_type=jnp.float32
    )
    return inside + carried


def backward_row(item):
    query_row, keys_row, values_row, segment_row, state_low, after_low, upstream_row = item
    allowed = row_mask(segment_row)
    weights_low = row_weights(query_row, keys_row, allowed)
    inherit = (segment_row == 0).astype(jnp.bfloat16)[:, None, None]
    tail = segment_row == segment_row[-1]
    tail_values = values_row * tail.astype(jnp.bfloat16)[:, None, None]
    score_back = (
        jnp.einsum("the,she->hts", upstream_row, values_row, preferred_element_type=jnp.float32)
        * allowed[None]
    ).astype(jnp.bfloat16)
    values_back = jnp.einsum(
        "hts,thd->shd", weights_low, upstream_row, preferred_element_type=jnp.float32
    )
    values_back = (
        values_back
        + jnp.einsum("hde,shd->she", after_low, keys_row, preferred_element_type=jnp.float32)
        * tail.astype(jnp.float32)[:, None, None]
    )
    query_back = jnp.einsum(
        "hts,shd->thd", score_back, keys_row, preferred_element_type=jnp.float32
    )
    query_back = query_back + jnp.einsum(
        "the,hde->thd", upstream_row * inherit, state_low, preferred_element_type=jnp.float32
    )
    keys_back = jnp.einsum(
        "hts,thd->shd", score_back, query_row, preferred_element_type=jnp.float32
    )
    keys_back = keys_back + jnp.einsum(
        "hde,she->shd", after_low, tail_values, preferred_element_type=jnp.float32
    )
    return (query_back, keys_back, values_back)


def shards(
    tokens,
    starts,
    entry_gain,
    query_weight,
    key_weight,
    value_weight,
    gate_weight,
    head_gain,
    output_weight,
    middle_gain,
    left_weight,
    right_weight,
    down_weight,
    cotangent,
):
    query_full, key_full, value_full, gate_full, output_full, left_full, right_full, down_full = (
        lax.all_gather(query_weight, "seq", axis=0, tiled=True),
        lax.all_gather(key_weight, "seq", axis=0, tiled=True),
        lax.all_gather(value_weight, "seq", axis=0, tiled=True),
        lax.all_gather(gate_weight, "seq", axis=0, tiled=True),
        lax.all_gather(output_weight, "seq", axis=0, tiled=True),
        lax.all_gather(left_weight, "seq", axis=0, tiled=True),
        lax.all_gather(right_weight, "seq", axis=0, tiled=True),
        lax.all_gather(down_weight, "seq", axis=1, tiled=True),
    )
    rows_here, span, width = tokens.shape
    count = rows_here * span
    source = tokens.reshape(count, width).astype(jnp.float32)
    inverse_in = inverse_rms(source)
    normed_in = (source * inverse_in * entry_gain).astype(jnp.bfloat16)
    query_linear = project(normed_in, query_full)
    key_linear = project(normed_in, key_full)
    value_linear = project(normed_in, value_full)
    gate_linear = project(normed_in, gate_full)
    shaped = (rows_here, span, HEADS, HEAD)
    query = jax.nn.softplus(query_linear).astype(jnp.bfloat16).reshape(shaped)
    keys = jax.nn.softplus(key_linear).astype(jnp.bfloat16).reshape(shaped)
    values = value_linear.astype(jnp.bfloat16).reshape(shaped)
    gate = jax.nn.sigmoid(gate_linear)
    segment = jnp.cumsum(starts, axis=1)
    last = segment[:, span - 1 :]
    tail = (segment == last).astype(jnp.bfloat16)
    keep = (last[:, 0] == 0).astype(jnp.float32)
    inherit = (segment == 0).astype(jnp.bfloat16)[:, :, None, None]
    fresh = jnp.einsum(
        "rshd,rshe->rhde", keys, values * tail[:, :, None, None], preferred_element_type=jnp.float32
    )
    every_keep = lax.all_gather(keep[None], "seq", axis=0, tiled=True)
    position = lax.axis_index("seq")
    resets = jnp.cumsum(1.0 - every_keep, axis=0)
    mine = lax.dynamic_index_in_dim(resets, position, 0, keepdims=False)
    device = jnp.arange(every_keep.shape[0])[:, None]
    forward_factor = (
        (device < position) & (mine[None] - (1.0 - keep)[None] - resets == 0.0)
    ).astype(jnp.float32)
    backward_factor = (
        (device > position) & (resets - (1.0 - every_keep) - mine[None] == 0.0)
    ).astype(jnp.float32)
    share = forward_factor
    prior_state = jnp.sum(
        lax.all_gather(fresh[None], "seq", axis=0, tiled=True) * share[:, :, None, None, None],
        axis=0,
    )
    state_low = prior_state.astype(jnp.bfloat16)
    attended = lax.map(forward_row, (query, keys, values, segment, state_low))
    inverse_head = inverse_rms(attended)
    head_shaped = head_gain.reshape(HEADS, HEAD)
    headed = (attended * inverse_head * head_shaped).reshape(count, width)
    gated = (headed * gate).astype(jnp.bfloat16)
    middle = source + project(gated, output_full)
    inverse_mid = inverse_rms(middle)
    normed_mid = (middle * inverse_mid * middle_gain).astype(jnp.bfloat16)
    left = project(normed_mid, left_full)
    right = project(normed_mid, right_full)
    joined = (left * right).astype(jnp.bfloat16)
    mixed = (middle + project(joined, down_full)).astype(jnp.bfloat16).reshape(tokens.shape)
    upstream = cotangent.reshape(count, width)
    down_term = contract_rows(joined, upstream)
    joined_back = project_back(upstream, down_full)
    left_back = (joined_back * right).astype(jnp.bfloat16)
    right_back = (joined_back * left).astype(jnp.bfloat16)
    left_term = contract_rows(normed_mid, left_back)
    right_term = contract_rows(normed_mid, right_back)
    normed_mid_back = project_back(left_back, left_full) + project_back(right_back, right_full)
    middle_back, middle_term = norm_back(normed_mid_back, middle, inverse_mid, middle_gain)
    middle_back = middle_back + upstream.astype(jnp.float32)
    branch_back = middle_back.astype(jnp.bfloat16)
    output_term = contract_rows(gated, branch_back)
    gated_back = project_back(branch_back, output_full)
    gate_linear_back = (gated_back * headed * gate * (1.0 - gate)).astype(jnp.bfloat16)
    attended_flat = attended.reshape(count, HEADS, HEAD)
    attended_grad, head_part = norm_back(
        (gated_back * gate).reshape(count, HEADS, HEAD),
        attended_flat,
        inverse_head.reshape(count, HEADS, 1),
        head_shaped,
    )
    head_term = head_part.reshape(width)
    attended_back = attended_grad.astype(jnp.bfloat16).reshape(shaped)
    direct = jnp.einsum(
        "rthd,rthe->rhde", query * inherit, attended_back, preferred_element_type=jnp.float32
    )
    share = backward_factor
    after_state = jnp.sum(
        lax.all_gather(direct[None], "seq", axis=0, tiled=True) * share[:, :, None, None, None],
        axis=0,
    )
    after_low = after_state.astype(jnp.bfloat16)
    query_back, keys_back, values_back = lax.map(
        backward_row, (query, keys, values, segment, state_low, after_low, attended_back)
    )
    query_linear_back = (query_back.reshape(count, width) * jax.nn.sigmoid(query_linear)).astype(
        jnp.bfloat16
    )
    key_linear_back = (keys_back.reshape(count, width) * jax.nn.sigmoid(key_linear)).astype(
        jnp.bfloat16
    )
    value_linear_back = values_back.reshape(count, width).astype(jnp.bfloat16)
    query_term = contract_rows(normed_in, query_linear_back)
    key_term = contract_rows(normed_in, key_linear_back)
    value_term = contract_rows(normed_in, value_linear_back)
    gate_term = contract_rows(normed_in, gate_linear_back)
    normed_in_back = project_back(query_linear_back, query_full) + project_back(
        key_linear_back, key_full
    )
    normed_in_back = (
        normed_in_back
        + project_back(value_linear_back, value_full)
        + project_back(gate_linear_back, gate_full)
    )
    input_back, entry_term = norm_back(normed_in_back, source, inverse_in, entry_gain)
    input_gradient = (input_back + middle_back).reshape(tokens.shape)
    shares = (
        lax.psum_scatter(entry_term, "seq", scatter_dimension=0, tiled=True),
        lax.psum_scatter(query_term, "seq", scatter_dimension=0, tiled=True),
        lax.psum_scatter(key_term, "seq", scatter_dimension=0, tiled=True),
        lax.psum_scatter(value_term, "seq", scatter_dimension=0, tiled=True),
        lax.psum_scatter(gate_term, "seq", scatter_dimension=0, tiled=True),
        lax.psum_scatter(head_term, "seq", scatter_dimension=0, tiled=True),
        lax.psum_scatter(output_term, "seq", scatter_dimension=0, tiled=True),
        lax.psum_scatter(middle_term, "seq", scatter_dimension=0, tiled=True),
        lax.psum_scatter(left_term, "seq", scatter_dimension=0, tiled=True),
        lax.psum_scatter(right_term, "seq", scatter_dimension=0, tiled=True),
        lax.psum_scatter(down_term, "seq", scatter_dimension=1, tiled=True),
    )
    (
        entry_total,
        query_total,
        key_total,
        value_total,
        gate_total,
        head_total,
        output_total,
        middle_total,
        left_total,
        right_total,
        down_total,
    ) = (
        lax.psum(shares[0].astype(jnp.bfloat16), "batch").astype(jnp.float32),
        lax.psum(shares[1].astype(jnp.bfloat16), "batch").astype(jnp.float32),
        lax.psum(shares[2].astype(jnp.bfloat16), "batch").astype(jnp.float32),
        lax.psum(shares[3].astype(jnp.bfloat16), "batch").astype(jnp.float32),
        lax.psum(shares[4].astype(jnp.bfloat16), "batch").astype(jnp.float32),
        lax.psum(shares[5].astype(jnp.bfloat16), "batch").astype(jnp.float32),
        lax.psum(shares[6].astype(jnp.bfloat16), "batch").astype(jnp.float32),
        lax.psum(shares[7].astype(jnp.bfloat16), "batch").astype(jnp.float32),
        lax.psum(shares[8].astype(jnp.bfloat16), "batch").astype(jnp.float32),
        lax.psum(shares[9].astype(jnp.bfloat16), "batch").astype(jnp.float32),
        lax.psum(shares[10].astype(jnp.bfloat16), "batch").astype(jnp.float32),
    )
    return (
        mixed,
        input_gradient,
        entry_total,
        query_total,
        key_total,
        value_total,
        gate_total,
        head_total,
        output_total,
        middle_total,
        left_total,
        right_total,
        down_total,
    )


def solution(mesh):
    in_specs = (
        P("batch", "seq", None),
        P("batch", "seq"),
        P(),
        P("seq", None),
        P("seq", None),
        P("seq", None),
        P("seq", None),
        P(),
        P("seq", None),
        P(),
        P("seq", None),
        P("seq", None),
        P(None, "seq"),
        P("batch", "seq", None),
    )
    out_specs = (
        P("batch", "seq", None),
        P("batch", "seq", None),
        P("seq"),
        P("seq", None),
        P("seq", None),
        P("seq", None),
        P("seq", None),
        P("seq"),
        P("seq", None),
        P("seq"),
        P("seq", None),
        P("seq", None),
        P(None, "seq"),
    )
    return jax.shard_map(shards, mesh=mesh, in_specs=in_specs, out_specs=out_specs, check_vma=False)
```

profile of v0, /device:TPU:0, one launch (start us, length us, event | category | flops | bytes accessed | tf_op | source)
XLA Modules:
  0.0 1987.1 jit_solution(10454922949463563538)
XLA Ops:
  14.1 48.1 %all-gather.14.cloned.1.call-done = bf16[1024,1024]{1,0:T(8,128)(2,1)} async-done(((bf16[128,1024]{1,0:T(8,128)(2,1)}), bf16[1024,1024]{1,0:T(8,128)(2,1)}) %all-gather.14.cloned.1.call-update) | async-done | bytes 2097168 | tf_op jit(solution)/shard_map/all_gather | solution.py:119
  65.9 46.2 %all-gather.18.cloned.1.call-done = bf16[1024,1024]{1,0:T(8,128)(2,1)} async-done(((bf16[128,1024]{1,0:T(8,128)(2,1)}), bf16[1024,1024]{1,0:T(8,128)(2,1)}) %all-gather.18.cloned.1.call-update) | async-done | bytes 2097168 | tf_op jit(solution)/shard_map/all_gather | solution.py:118
  112.1 5.0 fusion.79
  128.9 19.4 all-reduce
  149.7 12.0 all-gather.16.cloned.1.call-done
  161.8 5.0 fusion.78
  168.8 119.5 %all-gather.30.cloned.1.call-done = f32[16,16,64,64]{3,2,1,0:T(8,128)} async-done(((f32[2,16,64,64]{3,2,1,0:T(8,128)}), f32[16,16,64,64]{3,2,1,0:T(8,128)}) %all-gather.30.cloned.1.call-update) | async-done | bytes 4194320 | tf_op jit(solution)/shard_map/all_gather | solution.py:161
  288.3 5.5 multiply_reduce_fusion.1
  295.4 9.6 while.24
  305.0 5.0 copy.144
  318.6 19.2 all-gather.20.cloned.1.call-done
  337.8 5.7 multiply_convert_fusion.10
  343.5 44.1 %all-gather.22.cloned.1.call-done = bf16[1024,1024]{1,0:T(8,128)(2,1)} async-done(((bf16[128,1024]{1,0:T(8,128)(2,1)}), bf16[1024,1024]{1,0:T(8,128)(2,1)}) %all-gather.22.cloned.1.call-update) | async-done | bytes 2097168 | tf_op jit(solution)/shard_map/all_gather | solution.py:121
  392.5 88.5 %all-gather.24.cloned.1.call-done = bf16[1024,2816]{1,0:T(8,128)(2,1)} async-done(((bf16[128,2816]{1,0:T(8,128)(2,1)}), bf16[1024,2816]{1,0:T(8,128)(2,1)}) %all-gather.24.cloned.1.call-update) | async-done | bytes 5767184 | tf_op jit(solution)/shard_map/all_gather | solution.py:122
  481.0 7.9 fusion.110
  488.9 85.1 %all-gather.26.cloned.1.call-done = bf16[1024,2816]{1,0:T(8,128)(2,1)} async-done(((bf16[128,2816]{1,0:T(8,128)(2,1)}), bf16[1024,2816]{1,0:T(8,128)(2,1)}) %all-gather.26.cloned.1.call-update) | async-done | bytes 5767184 | tf_op jit(solution)/shard_map/all_gather | solution.py:123
  574.0 8.6 fusion.111
  582.6 85.2 %all-gather.28.cloned.1.call-done = bf16[2816,1024]{1,0:T(8,128)(2,1)} async-done(((bf16[2816,128]{1,0:T(8,128)(2,1)}), bf16[2816,1024]{1,0:T(8,128)(2,1)}) %all-gather.28.cloned.1.call-update) | async-done | bytes 5767184 | tf_op jit(solution)/shard_map/all_gather | solution.py:124
  667.9 9.0 multiply_convert_fusion.3
  676.8 7.3 fusion.112
  684.2 4.8 multiply_reduce_fusion.2
  693.6 4.9 reshape.438
  703.0 5.7 multiply_reduce_fusion.3
  711.6 3.5 reshape.414
  715.2 5.3 multiply_reduce_fusion.4
  725.5 4.9 fusion.95
  731.7 4.6 fusion.119
  739.0 109.7 %all-gather.32.cloned.1.call-done = f32[16,16,64,64]{3,2,1,0:T(8,128)} async-done(((f32[2,16,64,64]{3,2,1,0:T(8,128)}), f32[16,16,64,64]{3,2,1,0:T(8,128)}) %all-gather.32.cloned.1.call-update) | async-done | bytes 4194320 | tf_op jit(solution)/shard_map/all_gather | solution.py:205
  848.7 5.5 multiply_reduce_fusion
  857.3 32.5 %while.25 = (s32[]{:T(128)}, f32[2,256,16,64]{1,3,2,0:T(8,128)}, f32[2,256,16,64]{1,3,2,0:T(8,128)}, bf16[2,256,16,64]{1,3,2,0:T(8,128)(2,1)}, bf16[2,256,16,64]...) while((s32[]{:T(128)}, f32[2,256,16,64]{1,3,2,0:T(8,128)}, ...), condition=%wide.region_13.14_spmd, body=%wide.region_12.13_spmd.sunk | while | flops 778568960 | bytes 54017900 | solution.py:209
  889.8 4.9 copy.143
  894.7 3.5 reshape.437
  906.3 3.8 copy.142
  910.1 3.5 reshape.436
  928.4 7.8 fusion.120
  936.3 7.8 fusion.121
  945.3 7.8 fusion.122
  954.7 7.8 add_convert_fusion
  966.9 63.2 %reduce-scatter.15.cloned.1.call-done = f32[128,1024]{1,0:T(8,128)} async-done(((f32[1024,1024]{1,0:T(8,128)}), f32[128,1024]{1,0:T(8,128)}) %reduce-scatter.15.cloned.1.call-update) | async-done | bytes 524304 | tf_op jit(solution)/shard_map/reduce_scatter | solution.py:238
  1031.8 89.7 %reduce-scatter.11.cloned.1.call-done = f32[128,1024]{1,0:T(8,128)} async-done(((f32[1024,1024]{1,0:T(8,128)}), f32[128,1024]{1,0:T(8,128)}) %reduce-scatter.11.cloned.1.call-update) | async-done | bytes 524304 | tf_op jit(solution)/shard_map/reduce_scatter | solution.py:236
  1123.3 89.8 %reduce-scatter.9.cloned.1.call-done = f32[128,1024]{1,0:T(8,128)} async-done(((f32[1024,1024]{1,0:T(8,128)}), f32[128,1024]{1,0:T(8,128)}) %reduce-scatter.9.cloned.1.call-update) | async-done | bytes 524304 | tf_op jit(solution)/shard_map/reduce_scatter | solution.py:235
  1214.9 89.4 %reduce-scatter.13.cloned.1.call-done = f32[128,1024]{1,0:T(8,128)} async-done(((f32[1024,1024]{1,0:T(8,128)}), f32[128,1024]{1,0:T(8,128)}) %reduce-scatter.13.cloned.1.call-update) | async-done | bytes 524304 | tf_op jit(solution)/shard_map/reduce_scatter | solution.py:237
  1306.1 194.5 %reduce-scatter.19.cloned.1.call-done = f32[128,2816]{1,0:T(8,128)} async-done(((f32[1024,2816]{1,0:T(8,128)}), f32[128,2816]{1,0:T(8,128)}) %reduce-scatter.19.cloned.1.call-update) | async-done | bytes 1441808 | tf_op jit(solution)/shard_map/reduce_scatter | solution.py:242
  1502.9 193.4 %reduce-scatter.21.cloned.1.call-done = f32[128,2816]{1,0:T(8,128)} async-done(((f32[1024,2816]{1,0:T(8,128)}), f32[128,2816]{1,0:T(8,128)}) %reduce-scatter.21.cloned.1.call-update) | async-done | bytes 1441808 | tf_op jit(solution)/shard_map/reduce_scatter | solution.py:243
  1698.7 193.7 %reduce-scatter.23.cloned.1.call-done = f32[2816,128]{1,0:T(8,128)} async-done(((f32[2816,1024]{1,0:T(8,128)}), f32[2816,128]{1,0:T(8,128)}) %reduce-scatter.23.cloned.1.call-update) | async-done | bytes 1441808 | tf_op jit(solution)/shard_map/reduce_scatter | solution.py:244
  1904.9 34.9 %all-reduce.4 = (bf16[1024]{0:T(1024)(128)(2,1)S(1)}, bf16[1024]{0:T(1024)(128)(2,1)S(1)}, bf16[1024]{0:T(1024)(128)(2,1)S(1)}) all-reduce(f32[1024]{0:T(1024)S(1)} %get-tuple-element.187, f32[1024]{0:T(1024)S(1)} %get-tuple-element.241, f32[1024]{0:T(1024)S(1)} %get-tuple-element.185), channel_id=5, replica_groups=mesh['seq'=8,'batch'=4] {'seq'}, use_global_device_ids=true, to_apply=%region_16.17.clone | all-reduce | flops 3072 | bytes 18432
  1940.0 6.1 all-reduce.5
  1951.2 19.8 all-reduce.9.cloned.1.call-done
  (306 shorter events, 173.3 us)
Async XLA Ops:
  7.2 5.9 copy-start.7
  7.2 55.0 %all-gather.14.cloned.1.call-start = ((), (), s32[]{:S(2)}) async-start(), calls=%async_computation.8 | async-start | bytes 2359296 | tf_op jit(solution)/shard_map/all_gather | solution.py:119
  7.9 104.2 %all-gather.18.cloned.1.call-start = ((), (), s32[]{:S(2)}) async-start(), calls=%async_computation.10 | async-start | bytes 2359296 | tf_op jit(solution)/shard_map/all_gather | solution.py:118
  8.7 153.1 %all-gather.16.cloned.1.call-start = ((), (), s32[]{:S(2)}) async-start(), calls=%async_computation.9 | async-start | bytes 2359296 | tf_op jit(solution)/shard_map/all_gather | solution.py:117
  9.4 278.9 %all-gather.30.cloned.1.call-start = ((), (), s32[]{:S(2)}) async-start(), calls=%async_computation.24 | async-start | bytes 9437184 | tf_op jit(solution)/shard_map/all_gather | solution.py:161
  14.0 147.7 %copy-start.10 = (bf16[512,1024]{1,0:T(8,128)(2,1)}, bf16[512,1024]{1,0:T(8,128)(2,1)S(1)}, u32[]{:S(2)}) copy-start(bf16[512,1024]{1,0:T(8,128)(2,1)S(1)} %fusion.84) | copy-start | bytes 3145732
  123.7 3.5 copy-start.57
  123.7 24.7 %copy-start.56 = (f32[1024]{0:T(1024)S(1)}, f32[1024]{0:T(1024)}, u32[]{:S(2)}) copy-start(f32[1024]{0:T(1024)} %param.25) | copy-start | bytes 12292
  123.7 214.1 %all-gather.20.cloned.1.call-start = ((), (), s32[]{:S(2)}) async-start(), calls=%async_computation.11 | async-start | bytes 2359296 | tf_op jit(solution)/shard_map/all_gather | solution.py:120
  124.3 263.3 %all-gather.22.cloned.1.call-start = ((), (), s32[]{:S(2)}) async-start(), calls=%async_computation.12 | async-start | bytes 2359296 | tf_op jit(solution)/shard_map/all_gather | solution.py:121
  124.9 356.1 %all-gather.24.cloned.1.call-start = ((), (), s32[]{:S(2)}) async-start(), calls=%async_computation.13 | async-start | bytes 6488064 | tf_op jit(solution)/shard_map/all_gather | solution.py:122
  125.7 448.4 %all-gather.26.cloned.1.call-start = ((), (), s32[]{:S(2)}) async-start(), calls=%async_computation.14 | async-start | bytes 6488064 | tf_op jit(solution)/shard_map/all_gather | solution.py:123
  126.4 541.5 %all-gather.28.cloned.1.call-start = ((), (), s32[]{:S(2)}) async-start(), calls=%async_computation.15 | async-start | bytes 6488064 | tf_op jit(solution)/shard_map/all_gather | solution.py:124
  127.1 721.6 %all-gather.32.cloned.1.call-start = ((), (), s32[]{:S(2)}) async-start(), calls=%async_computation.25 | async-start | bytes 9437184 | tf_op jit(solution)/shard_map/all_gather | solution.py:205
  318.6 69.0 %copy-start.8 = (bf16[2,256,1024]{2,1,0:T(8,128)(2,1)S(1)}, bf16[2,256,1024]{2,1,0:T(8,128)(2,1)}, u32[]{:S(2)}) copy-start(bf16[2,256,1024]{2,1,0:T(8,128)(2,1)} %param.18) | copy-start | bytes 3145732
  387.6 4.6 copy-start.55
  392.5 88.5 %copy-start.41 = (bf16[512,1024]{1,0:T(8,128)(2,1)}, bf16[512,1024]{1,0:T(8,128)(2,1)S(1)}, u32[]{:S(2)}) copy-start(bf16[512,1024]{1,0:T(8,128)(2,1)S(1)} %multiply_convert_fusion.9) | copy-start | bytes 3145732
  488.9 179.0 %copy-start.28 = (bf16[2,256,1024]{2,1,0:T(8,128)(2,1)S(1)}, bf16[2,256,1024]{2,1,0:T(8,128)(2,1)}, u32[]{:S(2)}) copy-start(bf16[2,256,1024]{2,1,0:T(8,128)(2,1)} %param.31) | copy-start | bytes 3145732
  676.8 7.4 copy-start.37
  676.8 7.4 copy-start.36
  676.8 7.4 copy-start.21
  676.8 7.4 copy-start.58
  698.5 3.0 copy-start.19
  698.5 3.5 copy-start.23
  698.5 4.5 copy-start.24
  701.4 7.3 copy-start.5
  715.2 5.4 copy-start.4
  715.2 5.4 copy-start.14
  720.6 3.4 copy-start.30
  725.4 239.7 %reduce-scatter.17.cloned.1.call-start = ((), (), s32[]{:S(2)}) async-start(), calls=%async_computation.20 | async-start | bytes 4718592 | tf_op jit(solution)/shard_map/reduce_scatter | solution.py:240
  730.4 299.7 %reduce-scatter.15.cloned.1.call-start = ((), (), s32[]{:S(2)}) async-start(), calls=%async_computation.19 | async-start | bytes 4718592 | tf_op jit(solution)/shard_map/reduce_scatter | solution.py:238
  736.3 385.2 %reduce-scatter.11.cloned.1.call-start = ((), (), s32[]{:S(2)}) async-start(), calls=%async_computation.17 | async-start | bytes 4718592 | tf_op jit(solution)/shard_map/reduce_scatter | solution.py:236
  898.2 3.2 copy-start.12
  904.7 308.4 %reduce-scatter.9.cloned.1.call-start = ((), (), s32[]{:S(2)}) async-start(), calls=%async_computation.16 | async-start | bytes 4718592 | tf_op jit(solution)/shard_map/reduce_scatter | solution.py:235
  920.0 384.3 %reduce-scatter.13.cloned.1.call-start = ((), (), s32[]{:S(2)}) async-start(), calls=%async_computation.18 | async-start | bytes 4718592 | tf_op jit(solution)/shard_map/reduce_scatter | solution.py:237
  927.2 573.5 %reduce-scatter.19.cloned.1.call-start = ((), (), s32[]{:S(2)}) async-start(), calls=%async_computation.21 | async-start | bytes 12976128 | tf_op jit(solution)/shard_map/reduce_scatter | solution.py:242
  936.2 760.1 %reduce-scatter.21.cloned.1.call-start = ((), (), s32[]{:S(2)}) async-start(), calls=%async_computation.22 | async-start | bytes 12976128 | tf_op jit(solution)/shard_map/reduce_scatter | solution.py:243
  944.1 948.3 %reduce-scatter.23.cloned.1.call-start = ((), (), s32[]{:S(2)}) async-start(), calls=%async_computation.23 | async-start | bytes 12976128 | tf_op jit(solution)/shard_map/reduce_scatter | solution.py:244
  953.1 1017.9 %all-reduce.9.cloned.1.call-start = ((), (), s32[]{:S(2)}) async-start(), calls=%async_computation.26 | async-start | bytes 6946816 | tf_op jit(solution)/shard_map/psum | solution.py:260
  954.7 7.8 copy-start.35
  954.7 7.8 copy-start.60
  1895.9 3.0 copy-start.44
  1895.9 3.0 copy-start.59
  1901.8 45.9 %copy-start.6 = (f32[512,1024]{1,0:T(8,128)S(1)}, f32[512,1024]{1,0:T(8,128)}, u32[]{:S(2)}) copy-start(f32[512,1024]{1,0:T(8,128)} %copy-done.5) | copy-start | bytes 6291460
  1971.0 3.6 copy-start.45
  1973.4 3.2 copy-start.50
  1974.6 3.7 copy-start.48
  1975.8 3.4 copy-start.47
  (39 other events, 59.5 us)
Sparse Core Ops, SparseCore 0:
  10.1 51.9 all-gather.13
  64.3 47.7 all-gather.17
  114.2 47.4 all-gather.15
  164.3 123.9 all-gather.29
  290.3 47.4 all-gather.19
  339.8 47.7 all-gather.21
  389.8 91.1 all-gather.23
  483.1 90.8 all-gather.25
  576.0 91.7 all-gather.27
  725.6 123.0 all-gather.31
  852.3 86.0 reduce-scatter.16
  942.4 87.6 reduce-scatter.14
  1033.7 87.7 reduce-scatter.10
  1125.4 87.6 reduce-scatter.8
  1216.6 87.6 reduce-scatter.12
  1308.2 192.4 reduce-scatter.18
  1504.5 191.7 reduce-scatter.20
  1700.2 192.1 reduce-scatter.22
  1896.7 74.2 all-reduce.8
where the time goes:
time: 1990 us
  waiting for transfers between devices  1600 us (80%)
  matrix products  161 us (8%)
  local copies, waits for them, and re-layouts  82.6 us (4%)
  other arithmetic  68 us (3%)
  blocking collectives  60.4 us (3%)
    reduce_scatter x1, waiting for transfers between devices, shards(): lax.psum_scatter(left_term, 'seq', scatter_dimension=0, tiled=True)  195 us
    reduce_scatter x1, waiting for transfers between devices, shards(): lax.psum_scatter(down_term, 'seq', scatter_dimension=1, tiled=True)  194 us
    reduce_scatter x1, waiting for transfers between devices, shards(): lax.psum_scatter(right_term, 'seq', scatter_dimension=0, tiled=True)  193 us
    all_gather x1, waiting for transfers between devices, shards(): lax.all_gather(fresh[None], 'seq', axis=0, tiled=True)  120 us
    all_gather x1, waiting for transfers between devices, shards(): lax.all_gather(direct[None], 'seq', axis=0, tiled=True)  110 us
    reduce_scatter x1, waiting for transfers between devices, shards(): lax.psum_scatter(query_term, 'seq', scatter_dimension=0, tiled=True)  89.8 us
    reduce_scatter x1, waiting for transfers between devices, shards(): lax.psum_scatter(key_term, 'seq', scatter_dimension=0, tiled=True)  89.7 us
    reduce_scatter x1, waiting for transfers between devices, shards(): lax.psum_scatter(value_term, 'seq', scatter_dimension=0, tiled=True)  89.4 us
  transfers between devices with their start and end apart: 19, of which 18 were waited for; matrix products, arithmetic and copies ran while one was open for 11% of the time, Pallas kernels for 0%

commit v1 on v0

v1 whole, which is shorter than its diff:
```python
import functools

import jax
import jax.numpy as jnp
from jax import lax
from jax.experimental import pallas as pl
from jax.experimental.pallas import tpu as pltpu
from jax.sharding import PartitionSpec as P

HEADS = 16
HEAD = 64
EPSILON = 1e-06
BF = jnp.bfloat16
F32 = jnp.float32
VMEM = pl.BlockSpec(memory_space=pltpu.VMEM)
SMEM = pl.BlockSpec(memory_space=pltpu.SMEM)
ANY = pl.BlockSpec(memory_space=pl.ANY)
LIMIT = 60 * 1024 * 1024


def inverse_rms(values):
    return lax.rsqrt(jnp.mean(values * values, axis=-1, keepdims=True) + EPSILON)


def dot(left, right):
    return jnp.dot(left, right, preferred_element_type=F32)


def dot_nt(left, right):
    return lax.dot_general(left, right, (((1,), (1,)), ((), ())), preferred_element_type=F32)


def dot_tn(left, right):
    return lax.dot_general(left, right, (((0,), (0,)), ((), ())), preferred_element_type=F32)


def norm_back(upstream, values, inverse, gain):
    scaled = upstream * gain
    gain_part = jnp.sum(upstream * values * inverse, axis=0)
    cubed = inverse * inverse * inverse
    return (
        inverse * scaled - values * cubed * jnp.mean(scaled * values, axis=-1, keepdims=True),
        gain_part,
    )


def swap(value, axis, bit, size):
    return lax.ppermute(value, axis, [(i, i ^ bit) for i in range(size)])


class Plan:
    def __init__(self, mesh_shape, width):
        self.seq = mesh_shape["seq"]
        self.batch = mesh_shape["batch"]
        self.rows = width // self.seq
        self.fast = self.seq == 8 and self.batch == 4
        self.place = lax.axis_index("seq")
        self.lane = lax.axis_index("batch")
        self.nz = 4 if self.fast else self.seq
        self.span = width // self.nz
        self.part = self.rows // 2 if self.fast else self.rows
        self.groups = [[z * 2 + x for z in range(self.nz)] for x in range(2)]

    def half(self, bit):
        return (self.lane // bit) % 2

    def bases(self, bit):
        if not self.fast:
            return jnp.zeros((1,), jnp.int32)
        x, b = self.place % 2, self.half(bit)
        return jnp.stack(
            [(x ^ dx) * self.rows + (b ^ db) * self.part for db in range(2) for dx in range(2)]
        ).astype(jnp.int32)

    def gather(self, shard, bit):
        if not self.fast:
            return [lax.all_gather(shard, "seq", axis=0)]
        m, _, w = shard.shape
        mine = lax.dynamic_slice(shard, (0, self.half(bit) * self.part, 0), (m, self.part, w))
        near = lax.all_gather(mine, "seq", axis=0, axis_index_groups=self.groups)
        far = swap(near, "seq", 1, self.seq)
        return [near, far, swap(near, "batch", bit, 4), swap(far, "batch", bit, 4)]

    def reduce(self, keep, send, bit):
        if not self.fast:
            mine = lax.psum_scatter(keep, "seq", scatter_dimension=0)
            return mine
        got = swap(send, "batch", bit, 4)
        near = (keep[0].astype(F32) + got[0].astype(F32)).astype(BF)
        far = (keep[1].astype(F32) + got[1].astype(F32)).astype(BF)
        got = swap(far, "seq", 1, self.seq)
        near = (near.astype(F32) + got.astype(F32)).astype(BF)
        mine = lax.psum_scatter(
            near, "seq", scatter_dimension=0, axis_index_groups=self.groups
        )
        return mine

    def join(self, mine, bit):
        other = swap(mine, "batch", bit, 4)
        first = jnp.where(self.half(bit) == 0, mine, other)
        second = jnp.where(self.half(bit) == 0, other, mine)
        return jnp.concatenate([first, second], axis=1)


def assemble(plan, bit, pieces):
    nz, m, part, w = pieces[0].shape
    nb = len(pieces)

    def body(base_ref, *refs):
        ins, outs, sems = refs[:nb], refs[nb : nb + m], refs[nb + m]
        copies = []
        for b in range(nb):
            start = pl.multiple_of(base_ref[b], 16)
            for i in range(m):
                copies.append(
                    pltpu.make_async_copy(
                        ins[b].at[:, i], outs[i].at[:, pl.ds(start, part), :], sems.at[b, i]
                    )
                )
        for c in copies:
            c.start()
        for c in copies:
            c.wait()

    outs = pl.pallas_call(
        body,
        out_shape=[jax.ShapeDtypeStruct((nz, plan.span, w), BF)] * m,
        in_specs=[SMEM] + [ANY] * nb,
        out_specs=[ANY] * m,
        scratch_shapes=[pltpu.SemaphoreType.DMA((nb, m))],
        compiler_params=pltpu.CompilerParams(vmem_limit_bytes=LIMIT),
        name="assemble",
    )(plan.bases(bit), *pieces)
    return [o.reshape(nz * plan.span, w) for o in outs]


def ff_body(plan, nb, width, first, last, base_ref, nm_ref, up_ref, *refs):
    nz, span, part = plan.nz, plan.span, plan.part
    refs = list(refs)
    pieces = [refs.pop(0) for _ in range(nb)]
    carried = None if first else [refs.pop(0) for _ in range(2)]
    outs = [refs.pop(0) for _ in range(2 if nb > 1 else 1)]
    ends = [refs.pop(0) for _ in range(4 if last else 2)]
    weight, nm_t, up_t, grads, joined_s, left_s, right_s = [refs.pop(0) for _ in range(7)]
    totals = [refs.pop(0) for _ in range(2)] if last else ends
    in_sem, out_sem = refs
    mixed_ref, back_ref = totals
    d = nm_ref.shape[1]
    count = nm_ref.shape[0]
    starts = [pl.multiple_of(base_ref[b], 16) for b in range(nb)]
    tiles = [(s, min(256, width - s)) for s in range(0, width, 256)]

    def copy_in(t, b):
        cols = pl.ds(*tiles[t])
        return pltpu.make_async_copy(
            pieces[b].at[:, :, :, cols],
            weight.at[:, :, pl.ds(starts[b], part), cols],
            in_sem.at[t, b],
        )

    def copy_out(t, b):
        cols = pl.ds(*tiles[t])
        return pltpu.make_async_copy(
            grads.at[t % 2, :, :, pl.ds(starts[b], part), pl.ds(0, tiles[t][1])],
            outs[b // 2].at[b % 2, :, :, :, cols],
            out_sem.at[t % 2, b],
        )

    for t in range(len(tiles)):
        for b in range(nb):
            copy_in(t, b).start()

    def turn(i, _):
        rows = pl.ds(pl.multiple_of(i * 256, 256), 256)
        nm_t[:, rows] = nm_ref[rows, :].T
        up_t[:, rows] = up_ref[rows, :].T
        return 0

    lax.fori_loop(0, count // 256, turn, 0)

    for t, (start, size) in enumerate(tiles):
        cols = slice(start, start + size)
        for b in range(nb):
            copy_in(t, b).wait()

        def tokens(i, _, t=t, cols=cols, size=size):
            rows = pl.ds(pl.multiple_of(i * 256, 256), 256)
            left_w = weight[:, 0, :, cols].reshape(d, size)
            right_w = weight[:, 1, :, cols].reshape(d, size)
            down_w = weight[:, 2, :, cols].reshape(d, size)
            left = dot(nm_ref[rows, :], left_w)
            right = dot(nm_ref[rows, :], right_w)
            joined = (left * right).astype(BF)
            joined_back = dot(up_ref[rows, :], down_w)
            left_back = (joined_back * right).astype(BF)
            right_back = (joined_back * left).astype(BF)
            joined_s[rows, :size] = joined
            left_s[rows, :size] = left_back
            right_s[rows, :size] = right_back
            mixed = dot_nt(joined, down_w)
            back = dot_nt(left_back, left_w) + dot_nt(right_back, right_w)
            if t == 0 and first:
                mixed_ref[rows, :] = mixed
                back_ref[rows, :] = back
            elif t == 0:
                mixed_ref[rows, :] = carried[0][rows, :] + mixed
                back_ref[rows, :] = carried[1][rows, :] + back
            else:
                mixed_ref[rows, :] += mixed
                back_ref[rows, :] += back
            return 0

        lax.fori_loop(0, count // 256, tokens, 0)
        if t >= 2:
            for b in range(nb):
                copy_out(t - 2, b).wait()

        def features(i, _, t=t, size=size):
            rows = pl.ds(pl.multiple_of(i * 256, 256), 256)
            slabs = 256 // span
            at = pl.ds(i * slabs, slabs)
            nm_rows, up_rows = nm_t[rows, :], up_t[rows, :]
            for k, value in enumerate(
                (
                    dot(nm_rows, left_s[:, :size]),
                    dot(nm_rows, right_s[:, :size]),
                    dot(up_rows, joined_s[:, :size]),
                )
            ):
                grads[t % 2, at, k, :, :size] = value.astype(BF).reshape(slabs, span, size)
            return 0

        lax.fori_loop(0, d // 256, features, 0)
        for b in range(nb):
            copy_out(t, b).start()
    for t in range(max(0, len(tiles) - 2), len(tiles)):
        for b in range(nb):
            copy_out(t, b).wait()
    if last:
        half = count // 2
        for k in range(2):
            ends[2 * k][...] = totals[k][:half, :]
            ends[2 * k + 1][...] = totals[k][half:, :].astype(BF)


def feed_forward(plan, bit, pieces, nm, up, carry, last):
    nz, three, part, width = pieces[0].shape
    nb = len(pieces)
    count, d = nm.shape
    first = carry is None
    tiles = -(-width // 256)
    out_shape = [
        jax.ShapeDtypeStruct((2 if nb > 1 else 1, nz, three, part, width), BF)
    ] * (2 if nb > 1 else 1)
    if last:
        ends = [
            jax.ShapeDtypeStruct((count // 2, d), F32),
            jax.ShapeDtypeStruct((count // 2, d), BF),
        ] * 2
    else:
        ends = [jax.ShapeDtypeStruct((count, d), F32)] * 2
    scratch = [
        pltpu.VMEM((nz, three, plan.span, width), BF),
        pltpu.VMEM((d, count), BF),
        pltpu.VMEM((d, count), BF),
        pltpu.VMEM((2, nz, three, plan.span, 256), BF),
        pltpu.VMEM((count, 256), BF),
        pltpu.VMEM((count, 256), BF),
        pltpu.VMEM((count, 256), BF),
    ]
    if last:
        scratch += [pltpu.VMEM((count, d), F32)] * 2
    scratch += [pltpu.SemaphoreType.DMA((tiles, nb)), pltpu.SemaphoreType.DMA((2, nb))]
    got = pl.pallas_call(
        functools.partial(ff_body, plan, nb, width, first, last),
        out_shape=out_shape + ends,
        in_specs=[SMEM, VMEM, VMEM] + [ANY] * nb + ([] if first else [VMEM] * 2),
        out_specs=[ANY] * len(out_shape) + [VMEM] * len(ends),
        scratch_shapes=scratch,
        compiler_params=pltpu.CompilerParams(vmem_limit_bytes=LIMIT),
        cost_estimate=pl.CostEstimate(
            flops=18 * count * d * width, bytes_accessed=12 * d * width + 16 * d * count, transcendentals=0
        ),
        name="feed_forward",
    )(plan.bases(bit), nm, up, *pieces, *(carry or ()))
    return got[: len(out_shape)], got[len(out_shape) :]


def row_mask(segment_row):
    order = jnp.arange(segment_row.shape[0])
    return (
        (segment_row[:, None] == segment_row[None, :]) & (order[:, None] >= order[None, :])
    ).astype(F32)


def row_weights(query_row, keys_row, allowed):
    scores = jnp.einsum("thd,shd->hts", query_row, keys_row, preferred_element_type=F32)
    return (scores * allowed[None]).astype(BF)


def forward_row(item):
    query_row, keys_row, values_row, segment_row, state_low = item
    weights_low = row_weights(query_row, keys_row, row_mask(segment_row))
    inside = jnp.einsum("hts,shd->thd", weights_low, values_row, preferred_element_type=F32)
    inherit = (segment_row == 0).astype(BF)[:, None, None]
    carried = jnp.einsum("thd,hde->the", query_row * inherit, state_low, preferred_element_type=F32)
    return inside + carried


def backward_row(item):
    query_row, keys_row, values_row, segment_row, state_low, after_low, upstream_row = item
    allowed = row_mask(segment_row)
    weights_low = row_weights(query_row, keys_row, allowed)
    inherit = (segment_row == 0).astype(BF)[:, None, None]
    tail = segment_row == segment_row[-1]
    tail_values = values_row * tail.astype(BF)[:, None, None]
    score_back = (
        jnp.einsum("the,she->hts", upstream_row, values_row, preferred_element_type=F32)
        * allowed[None]
    ).astype(BF)
    values_back = jnp.einsum("hts,thd->shd", weights_low, upstream_row, preferred_element_type=F32)
    values_back = (
        values_back
        + jnp.einsum("hde,shd->she", after_low, keys_row, preferred_element_type=F32)
        * tail.astype(F32)[:, None, None]
    )
    query_back = jnp.einsum("hts,shd->thd", score_back, keys_row, preferred_element_type=F32)
    query_back = query_back + jnp.einsum(
        "the,hde->thd", upstream_row * inherit, state_low, preferred_element_type=F32
    )
    keys_back = jnp.einsum("hts,thd->shd", score_back, query_row, preferred_element_type=F32)
    keys_back = keys_back + jnp.einsum(
        "hde,she->shd", after_low, tail_values, preferred_element_type=F32
    )
    return (query_back, keys_back, values_back)


def chain(own, keep, order, size):
    shape = keep.shape + (1,) * (own.ndim - 1)
    total, before, all_kept, between = own, jnp.zeros_like(own), keep, jnp.ones_like(keep)
    step = 1
    while step < size:
        pairs = [
            (i, i + order * step) for i in range(size) if 0 <= i + order * step < size
        ]
        got = lax.ppermute(total.astype(BF), "seq", pairs).astype(F32)
        got_kept = lax.ppermute(all_kept, "seq", pairs)
        before = before + between.reshape(shape) * got
        if step * 2 < size:
            total = total + all_kept.reshape(shape) * got
        between = between * got_kept
        all_kept = all_kept * got_kept
        step *= 2
    return before


def shards(
    mesh_shape,
    tokens,
    starts,
    entry_gain,
    query_weight,
    key_weight,
    value_weight,
    gate_weight,
    head_gain,
    output_weight,
    middle_gain,
    left_weight,
    right_weight,
    down_weight,
    cotangent,
):
    rows_here, span, width = tokens.shape
    count = rows_here * span
    hidden = left_weight.shape[1]
    plan = Plan(mesh_shape, width)
    seq = plan.seq
    core = plan.half(1)

    pair_kv = plan.gather(jnp.stack([key_weight, value_weight]), 1)
    pair_qg = plan.gather(jnp.stack([query_weight, gate_weight]), 1)
    one_o = plan.gather(output_weight[None], 1)
    mine = hidden // 2
    cuts = [0, 768, mine]
    stack = lax.dynamic_slice(
        jnp.stack([left_weight, right_weight, down_weight.T]),
        (0, 0, core * mine),
        (3, plan.rows, mine),
    )
    ff_pieces = [plan.gather(stack[:, :, a:b], 2) for a, b in zip(cuts, cuts[1:])]
    upstream = cotangent.reshape(count, width)
    up_both = jnp.concatenate([upstream, swap(upstream, "batch", 1, plan.batch)])

    source = tokens.reshape(count, width).astype(F32)
    inverse_in = inverse_rms(source)
    normed_in = (source * inverse_in * entry_gain).astype(BF)
    key_full, value_full = assemble(plan, 1, pair_kv)
    key_linear = dot(normed_in, key_full)
    value_linear = dot(normed_in, value_full)
    shaped = (rows_here, span, HEADS, HEAD)
    keys = jax.nn.softplus(key_linear).astype(BF).reshape(shaped)
    values = value_linear.astype(BF).reshape(shaped)
    place = jnp.arange(span)
    segment = dot(starts.astype(BF), (place[:, None] <= place[None, :]).astype(BF)).astype(jnp.int32)
    last = segment[:, span - 1 :]
    tail = (segment == last).astype(BF)
    keep = (last[:, 0] == 0).astype(F32)
    inherit = (segment == 0).astype(BF)[:, :, None, None]
    fresh = jnp.einsum(
        "rshd,rshe->rhde", keys, values * tail[:, :, None, None], preferred_element_type=F32
    )
    state_low = chain(fresh, keep, 1, seq).astype(BF)
    query_full, gate_full = assemble(plan, 1, pair_qg)
    query_linear = dot(normed_in, query_full)
    gate_linear = dot(normed_in, gate_full)
    query = jax.nn.softplus(query_linear).astype(BF).reshape(shaped)
    gate = jax.nn.sigmoid(gate_linear)
    attended = lax.map(forward_row, (query, keys, values, segment, state_low))
    inverse_head = inverse_rms(attended)
    head_shaped = head_gain.reshape(HEADS, HEAD)
    headed = (attended * inverse_head * head_shaped).reshape(count, width)
    gated = (headed * gate).astype(BF)
    (output_full,) = assemble(plan, 1, one_o)
    middle = source + dot(gated, output_full)
    inverse_mid = inverse_rms(middle)
    normed_mid = (middle * inverse_mid * middle_gain).astype(BF)

    nm_both = jnp.concatenate([normed_mid, swap(normed_mid, "batch", 1, plan.batch)])
    carry, terms = None, []
    for i, pieces in enumerate(ff_pieces):
        term, carry = feed_forward(plan, 2, pieces, nm_both, up_both, carry, i == len(ff_pieces) - 1)
        terms.append(term)
    mixed_own, mixed_send, back_own, back_send = carry
    normed_mid_back = back_own + swap(back_send, "batch", 1, plan.batch).astype(F32)
    mixed = (
        (middle + (mixed_own + swap(mixed_send, "batch", 1, plan.batch).astype(F32)))
        .astype(BF)
        .reshape(tokens.shape)
    )

    middle_back, middle_term = norm_back(normed_mid_back, middle, inverse_mid, middle_gain)
    middle_back = middle_back + upstream.astype(F32)
    branch_back = middle_back.astype(BF)
    output_term = dot_tn(gated, branch_back)
    gated_back = dot_nt(branch_back, output_full)
    gate_linear_back = (gated_back * headed * gate * (1.0 - gate)).astype(BF)
    attended_grad, head_part = norm_back(
        (gated_back * gate).reshape(count, HEADS, HEAD),
        attended.reshape(count, HEADS, HEAD),
        inverse_head.reshape(count, HEADS, 1),
        head_shaped,
    )
    head_term = head_part.reshape(width)
    attended_back = attended_grad.astype(BF).reshape(shaped)
    direct = jnp.einsum("rthd,rthe->rhde", query * inherit, attended_back, preferred_element_type=F32)
    after_low = chain(direct, keep, -1, seq).astype(BF)
    query_back, keys_back, values_back = lax.map(
        backward_row, (query, keys, values, segment, state_low, after_low, attended_back)
    )
    query_linear_back = (query_back.reshape(count, width) * jax.nn.sigmoid(query_linear)).astype(BF)
    key_linear_back = (keys_back.reshape(count, width) * jax.nn.sigmoid(key_linear)).astype(BF)
    value_linear_back = values_back.reshape(count, width).astype(BF)
    query_term = dot_tn(normed_in, query_linear_back)
    key_term = dot_tn(normed_in, key_linear_back)
    value_term = dot_tn(normed_in, value_linear_back)
    gate_term = dot_tn(normed_in, gate_linear_back)
    normed_in_back = dot_nt(query_linear_back, query_full) + dot_nt(key_linear_back, key_full)
    normed_in_back = (
        normed_in_back + dot_nt(value_linear_back, value_full) + dot_nt(gate_linear_back, gate_full)
    )
    input_back, entry_term = norm_back(normed_in_back, source, inverse_in, entry_gain)
    input_gradient = (input_back + middle_back).reshape(tokens.shape)

    def square_sum(term_list):
        m = len(term_list)
        whole = jnp.stack([t.astype(BF) for t in term_list])
        if not plan.fast:
            whole = whole.reshape(m, plan.nz, plan.span, width).swapaxes(0, 1)
            part = plan.reduce(whole, None, 1)
            return lax.psum(part, "batch").astype(F32)
        whole = whole.reshape(m, 4, 2, 2, plan.part, width).transpose(3, 2, 1, 0, 4, 5)
        x = plan.place % 2

        def side(db):
            half = lax.dynamic_index_in_dim(whole, core ^ db, 0, keepdims=False)
            return jnp.stack(
                [lax.dynamic_index_in_dim(half, x ^ dx, 0, keepdims=False) for dx in range(2)]
            )

        part = plan.reduce(side(0), side(1), 1)
        part = (part.astype(F32) + swap(part, "batch", 2, 4).astype(F32)).astype(BF)
        return plan.join(part, 1).astype(F32)

    wide = []
    for term in terms:
        if plan.fast:
            wide.append(plan.join(plan.reduce(term[0], term[1], 2), 2))
        else:
            part = plan.reduce(term[0][0], None, 2)
            groups = [[i for i in range(plan.batch) if i % 2 == c] for c in range(2)]
            wide.append(lax.psum(part, "batch", axis_index_groups=groups))
    wide = jnp.concatenate(wide, axis=2)
    other = swap(wide, "batch", 1, plan.batch)
    wide = jnp.concatenate(
        [jnp.where(core == 0, wide, other), jnp.where(core == 0, other, wide)], axis=2
    ).astype(F32)
    left_total, right_total, down_total = wide[0], wide[1], wide[2].T
    (output_total, gate_total) = square_sum([output_term, gate_term])
    (query_total, key_total, value_total) = square_sum([query_term, key_term, value_term])
    gains = lax.psum(jnp.stack([entry_term, head_term, middle_term]), ("seq", "batch"))
    gains = lax.dynamic_slice(gains, (0, plan.place * plan.rows), (3, plan.rows))
    return (
        mixed,
        input_gradient,
        gains[0],
        query_total,
        key_total,
        value_total,
        gate_total,
        gains[1],
        output_total,
        gains[2],
        left_total,
        right_total,
        down_total,
    )


def solution(mesh):
    row, cut, wide = P("batch", "seq", None), P("seq", None), P(None, "seq")
    in_specs = (row, P("batch", "seq"), P(), cut, cut, cut, cut, P(), cut, P(), cut, cut, wide, row)
    out_specs = (row, row, P("seq"), cut, cut, cut, cut, P("seq"), cut, P("seq"), cut, cut, wide)
    return jax.shard_map(
        functools.partial(shards, dict(mesh.shape)),
        mesh=mesh,
        in_specs=in_specs,
        out_specs=out_specs,
        check_vma=False,
    )
```

time: 1990 us -> 1110 us (0.56)
  waiting for transfers between devices: 1600 us -> 285 us
  Pallas kernels: 0 us -> 381 us
  matrix products: 161 us -> 75.7 us
  starting transfers between devices: 1.3 us -> 60 us
  blocking collectives: 60.4 us -> 99.6 us
  other arithmetic: 68 us -> 93.9 us
    reduce_scatter x8 -> x4, waiting for transfers between devices: 914 us -> 0.03 us  [reduce(): lax.psum_scatter(near, 'seq', scatter_dimension=0, axis_index_groups=self...]
    all_gather x10 -> x3, waiting for transfers between devices: 658 us -> 58 us  [gather(): near = lax.all_gather(mine, 'seq', axis=0, axis_index_groups=self.groups)]
    pallas_call x0 -> x5, Pallas kernels: none -> 381 us  [the longest x3 323 us: assemble(): pl.pallas_call(body, out_shape=[jax.ShapeDtypeStruct((nz, plan.span, w),...]
    ppermute x0 -> x44, waiting for transfers between devices: none -> 227 us  [the longest x34 171 us: swap(): return lax.ppermute(value, axis, [(i, i ^ bit) for i in range(size)])]
    dot_general x28 -> x20, matrix products: 128 us -> 44.6 us  [the longest x6 20.3 us: dot(): return jnp.dot(left, right, preferred_element_type=F32)]
    all_gather x0 -> x2, blocking collectives: none -> 59.8 us  [gather(): near = lax.all_gather(mine, 'seq', axis=0, axis_index_groups=self.groups)]
    ppermute x0 -> x44, starting transfers between devices: none -> 59.7 us  [the longest x34 34.5 us: swap(): return lax.ppermute(value, axis, [(i, i ^ bit) for i in range(size)])]
    unnamed x2 -> x0, blocking collectives: 54.3 us -> none
  transfers between devices with their start and end apart: 19 -> 51, of which waited for: 18 -> 19; matrix products, arithmetic and copies ran while one was open for 11% -> 19% of each run, Pallas kernels for 0% -> 32%
where the time goes in v1:
time: 1110 us; the launch traced here: 1100 us
  Pallas kernels  381 us (34%)
  waiting for transfers between devices  285 us (26%)
  blocking collectives  99.6 us (9%)
  other arithmetic  93.9 us (8%)
  local copies, waits for them, and re-layouts  89 us (8%)
  matrix products  75.7 us (7%)
  starting transfers between devices  60 us (5%)
  between operations  15.8 us (1%)
    pallas_call x3, Pallas kernels, assemble(): pl.pallas_call(body, out_shape=[jax.ShapeDtypeStruct((nz, plan.span, w),...  323 us
    ppermute x34, waiting for transfers between devices, swap(): return lax.ppermute(value, axis, [(i, i ^ bit) for i in range(size)])  171 us
    all_gather x2, blocking collectives, gather(): near = lax.all_gather(mine, 'seq', axis=0, axis_index_groups=self.groups)  59.8 us
    all_gather x3, waiting for transfers between devices, gather(): near = lax.all_gather(mine, 'seq', axis=0, axis_index_groups=self.groups)  58 us
    pallas_call x2, Pallas kernels, feed_forward(): pl.pallas_call(functools.partial(ff_body, plan, nb, width, first, last),...  57.4 us
    ppermute x6, waiting for transfers between devices, chain(): got = lax.ppermute(total.astype(BF), 'seq', pairs).astype(F32)  43 us
    psum x1, blocking collectives, shards(): lax.psum(jnp.stack([entry_term, head_term, middle_term]), ('seq', 'batch'))  39.8 us
    ppermute x34, starting transfers between devices, swap(): return lax.ppermute(value, axis, [(i, i ^ bit) for i in range(size)])  34.5 us
  transfers between devices with their start and end apart: 51, of which 19 were waited for; matrix products, arithmetic and copies ran while one was open for 19% of the time, Pallas kernels for 32%

profile of v1, /device:TPU:0, one launch (start us, length us, event | category | flops | bytes accessed | tf_op | source)
XLA Modules:
  0.0 1100.3 jit_solution(13515014026715891141)
XLA Ops:
  10.9 30.0 %all-gather.11.cloned.1.call-done = bf16[8,64,1024]{2,1,0:T(8,128)(2,1)} async-done(((bf16[2,64,1024]{2,1,0:T(8,128)(2,1)}), bf16[8,64,1024]{2,1,0:T(8,128)(2,1)}) %all-gather.11.cloned.1.call-update) | async-done | bytes 1048592 | tf_op jit(solution)/shard_map/all_gather | solution.py:80
  42.5 28.0 %all-gather.9.cloned.1.call-done = bf16[8,64,1024]{2,1,0:T(8,128)(2,1)} async-done(((bf16[2,64,1024]{2,1,0:T(8,128)(2,1)}), bf16[8,64,1024]{2,1,0:T(8,128)(2,1)}) %all-gather.9.cloned.1.call-update) | async-done | bytes 1048592 | tf_op jit(solution)/shard_map/all_gather | solution.py:80
  78.0 17.5 %collective-permute-done.refs_1_ = bf16[4,2,64,1024]{3,2,1,0:T(8,128)(2,1)} collective-permute-done((bf16[4,2,64,1024]{3,2,1,0:T(8,128)(2,1)}, bf16[4,2,64,1024]{3,2,1,0:T(8,128)(2,1)}, u32[]{:S(2)}, u32[]{:S(2)}) %collective-permute-start) | collective-permute-done | bytes 1048608 | tf_op jit(solution)/shard_map/ppermute | solution.py:48
  97.5 3.5 collective-permute-start.7
  101.0 128.9 %assemble.4 = (bf16[4,256,1024]{2,1,0:T(8,128)(2,1)}, bf16[4,256,1024]{2,1,0:T(8,128)(2,1)}) custom-call(s32[4]{0:T(128)} %pad_add_fusion.base_ref, bf16[4,2,64,1024]{3,2,1,0:T(8,128)(2,1)} %bitcast.421, bf16[4,2,64,1024]{3,2,1,0:T(8,128)(2,1)} %collective-permute-done.3.refs_1_, bf16[4,2,64,1024]{3,2,1,0:T(8,128)(2,1)} %collective-permute-done.4.refs_2_, ...), custom_call_target="tpu_custom_call" | custom-call | tf_op jit(solution)/shard_map/assemble/pallas_call | solution.py:125
  229.9 5.0 fusion.81
  235.8 129.0 %assemble.3 = (bf16[4,256,1024]{2,1,0:T(8,128)(2,1)}, bf16[4,256,1024]{2,1,0:T(8,128)(2,1)}) custom-call(s32[4]{0:T(128)} %pad_add_fusion.base_ref, bf16[4,2,64,1024]{3,2,1,0:T(8,128)(2,1)} %bitcast.31.refs_0_, bf16[4,2,64,1024]{3,2,1,0:T(8,128)(2,1)} %collective-permute-done.refs_1_, bf16[4,2,64,1024]{3,2,1,0:T(8,128)(2,1)} %collective-permute-done.1.refs_2_, ...), custom_call_target="tpu_custom_call" | custom-call | tf_op jit(solution)/shard_map/assemble/pallas_call | solution.py:125
  368.6 5.7 fusion.82
  381.0 3.4 collective-permute-start.6
  384.5 16.7 %all-gather.2 = bf16[256,1024]{1,0:T(8,128)(2,1)} all-gather(bf16[64,1024]{1,0:T(8,128)(2,1)S(1)} %constant_dynamic-slice_fusion.9), channel_id=4, replica_groups={{0,8,16,24},{4,12,20,28},{1,9,17,25},{5,13,21,29},{2,10,18,26},{6,14,22..., dimensions={0}, use_global_device_ids=true | all-gather | bytes 655360 | tf_op jit(solution)/shard_map/all_gather | solution.py:80
  401.1 8.7 collective-permute-start.11
  411.6 4.5 collective-permute-start.8
  416.5 4.3 collective-permute-done.11.refs_1_
  420.8 6.7 collective-permute-done.8
  429.8 5.2 collective-permute-start.10
  435.0 43.1 %all-gather.3 = bf16[12,64,640]{2,1,0:T(8,128)(2,1)} all-gather(bf16[3,64,640]{2,1,0:T(8,128)(2,1)S(1)} %constant_dynamic-slice_fusion.8), channel_id=5, replica_groups={{0,8,16,24},{4,12,20,28},{1,9,17,25},{5,13,21,29},{2,10,18,26},{6,14,22..., dimensions={0}, use_global_device_ids=true | all-gather | bytes 1228800 | tf_op jit(solution)/shard_map/all_gather | solution.py:80
  482.4 65.3 %assemble.5 = bf16[4,256,1024]{2,1,0:T(8,128)(2,1)} custom-call(s32[4]{0:T(128)} %pad_add_fusion.base_ref, bf16[4,1,64,1024]{3,2,1,0:T(8,128)(2,1)} %bitcast.40.refs_0_, bf16[4,1,64,1024]{3,2,1,0:T(8,128)(2,1)} %collective-permute-done.11.refs_1_, bf16[4,1,64,1024]{3,2,1,0:T(8,128)(2,1)} %collective-permute-done.12.refs_2_, bf16[4,1,64,1024]{3,2,1,0:T(8,128)(2,1)} %copy-done.58), custom_call_target="tpu_custom_call" | custom-call | tf_op jit(solution)/shard_map/assemble/pallas_call | solution.py:125
  555.2 9.7 while.24
  573.8 5.2 multiply_convert_fusion.7
  593.2 18.7 %collective-permute-done.20.refs_2_ = bf16[4,3,64,768]{3,2,1,0:T(8,128)(2,1)} collective-permute-done((bf16[4,3,64,768]{3,2,1,0:T(8,128)(2,1)}, bf16[4,3,64,768]{3,2,1,0:T(8,128)(2,1)}, u32[]{:S(2)}, u32[]{:S(2)}) %collective-permute-start.20) | collective-permute-done | bytes 1179680 | tf_op jit(solution)/shard_map/ppermute | solution.py:48
  611.9 25.3 %collective-permute-done.21.refs_3_ = bf16[4,3,64,768]{3,2,1,0:T(8,128)(2,1)} collective-permute-done((bf16[4,3,64,768]{3,2,1,0:T(8,128)(2,1)}, bf16[4,3,64,768]{3,2,1,0:T(8,128)(2,1)}, u32[]{:S(2)}, u32[]{:S(2)}) %collective-permute-start.21) | collective-permute-done | bytes 1179680 | tf_op jit(solution)/shard_map/ppermute | solution.py:48
  637.2 28.0 %feed_forward.2 = (bf16[2,4,3,64,768]{4,3,2,1,0:T(8,128)(2,1)}, bf16[2,4,3,64,768]{4,3,2,1,0:T(8,128)(2,1)}, f32[1024,1024]{1,0:T(8,128)}, f32[1024,1024]{1,0:T(8,128)}) custom-call(s32[4]{0:T(128)} %pad_add_fusion.1.base_ref, bf16[1024,1024]{1,0:T(8,128)(2,1)} %pad_maximum_fusion.2.nm_ref, bf16[1024,1024]{1,0:T(8,128)(2,1)} %pad_maximum_fusion.3.up_ref, ...), custom_call_target="tpu_custom_call" | custom-call | flops 14495514624 | bytes 26214400 | tf_op jit(solution)/shard_map/feed_forward/pallas_call | solution.py:274
  665.2 13.7 %collective-permute-done.18.refs_3_ = bf16[4,3,64,640]{3,2,1,0:T(8,128)(2,1)} collective-permute-done((bf16[4,3,64,640]{3,2,1,0:T(8,128)(2,1)}, bf16[4,3,64,640]{3,2,1,0:T(8,128)(2,1)}, u32[]{:S(2)}, u32[]{:S(2)}) %collective-permute-start.18) | collective-permute-done | bytes 983072 | tf_op jit(solution)/shard_map/ppermute | solution.py:48
  679.0 29.4 %feed_forward.3 = (bf16[2,4,3,64,640]{4,3,2,1,0:T(8,128)(2,1)}, bf16[2,4,3,64,640]{4,3,2,1,0:T(8,128)(2,1)}, f32[512,1024]{1,0:T(8,128)}, bf16[512,1024]{1,0:T(8...) custom-call(s32[4]{0:T(128)} %pad_add_fusion.1.base_ref, bf16[1024,1024]{1,0:T(8,128)(2,1)} %pad_maximum_fusion.2.nm_ref, ...), custom_call_target="tpu_custom_call" | custom-call | flops 12079595520 | bytes 24641536 | tf_op jit(solution)/shard_map/feed_forward/pallas_call | solution.py:274
  709.0 4.9 copy.178
  713.9 4.9 reshape.466
  727.1 4.3 convert_add_fusion.5
  733.5 3.4 multiply_reduce_fusion.1
  739.9 3.5 reshape.443
  743.4 5.1 multiply_reduce_fusion.2
  753.3 14.5 %collective-permute-done.24 = bf16[2,16,64,64]{3,2,1,0:T(8,128)(2,1)S(1)} collective-permute-done((bf16[2,16,64,64]{3,2,1,0:T(8,128)(2,1)S(1)}, bf16[2,16,64,64]{3,2,1,0:T(8,128)(2,1)S(1)}, u32[]{:S(2)}, u32[]{:S(2)}) %collective-permute-start.24) | collective-permute-done | bytes 262176 | tf_op jit(solution)/shard_map/ppermute | solution.py:346
  773.3 12.0 %collective-permute-done.27 = f32[2]{0:T(128)S(1)} collective-permute-done((f32[2]{0:T(128)S(1)}, f32[2]{0:T(128)S(1)}, u32[]{:S(2)}, u32[]{:S(2)}) %collective-permute-start.27) | collective-permute-done | bytes 40 | tf_op jit(solution)/shard_map/ppermute | solution.py:347
  795.4 21.8 %collective-permute-done.28 = bf16[2,16,64,64]{3,2,1,0:T(8,128)(2,1)S(1)} collective-permute-done((bf16[2,16,64,64]{3,2,1,0:T(8,128)(2,1)S(1)}, bf16[2,16,64,64]{3,2,1,0:T(8,128)(2,1)S(1)}, u32[]{:S(2)}, u32[]{:S(2)}) %collective-permute-start.28) | collective-permute-done | bytes 262176 | tf_op jit(solution)/shard_map/ppermute | solution.py:346
  822.5 32.3 %while.25 = (s32[]{:T(128)}, f32[2,256,16,64]{1,3,2,0:T(8,128)}, f32[2,256,16,64]{1,3,2,0:T(8,128)}, bf16[2,256,16,64]{1,3,2,0:T(8,128)(2,1)}, bf16[2,256,16,64]...) while((s32[]{:T(128)}, f32[2,256,16,64]{1,3,2,0:T(8,128)}, ...), condition=%wide.region_8.9_spmd, body=%wide.region_7.8_spmd.sunk | while | flops 778568960 | bytes 54017900 | solution.py:458
  854.9 4.8 copy.177
  859.7 3.5 reshape.465
  868.1 3.9 copy.176
  872.0 3.7 reshape.464
  902.7 15.1 %collective-permute-done.41 = bf16[4,3,64,640]{3,2,1,0:T(8,128)(2,1)S(1)} collective-permute-done((bf16[4,3,64,640]{3,2,1,0:T(8,128)(2,1)S(1)}, bf16[4,3,64,640]{3,2,1,0:T(8,128)(2,1)S(1)}, u32[]{:S(2)}, u32[]{:S(2)}) %collective-permute-start.41) | collective-permute-done | bytes 983072 | tf_op jit(solution)/shard_map/ppermute | solution.py:48
  931.1 18.6 %collective-permute-done.38 = bf16[4,3,64,768]{3,2,1,0:T(8,128)(2,1)S(1)} collective-permute-done((bf16[4,3,64,768]{3,2,1,0:T(8,128)(2,1)S(1)}, bf16[4,3,64,768]{3,2,1,0:T(8,128)(2,1)S(1)}, u32[]{:S(2)}, u32[]{:S(2)}) %collective-permute-start.38) | collective-permute-done | bytes 1179680 | tf_op jit(solution)/shard_map/ppermute | solution.py:48
  956.3 21.5 %collective-permute-done.34 = bf16[4,2,64,1024]{3,2,1,0:T(8,128)(2,1)S(1)} collective-permute-done((bf16[4,2,64,1024]{3,2,1,0:T(8,128)(2,1)S(1)}, bf16[4,2,64,1024]{3,2,1,0:T(8,128)(2,1)S(1)}, u32[]{:S(2)}, u32[]{:S(2)}) %collective-permute-start.34) | collective-permute-done | bytes 1048608 | tf_op jit(solution)/shard_map/ppermute | solution.py:48
  980.7 3.8 fusion.78
  988.0 30.3 %collective-permute-done.30 = bf16[4,3,64,1024]{3,2,1,0:T(8,128)(2,1)} collective-permute-done((bf16[4,3,64,1024]{3,2,1,0:T(8,128)(2,1)}, bf16[4,3,64,1024]{3,2,1,0:T(8,128)(2,1)}, u32[]{:S(2)}, u32[]{:S(2)}) %collective-permute-start.30) | collective-permute-done | bytes 1572896 | tf_op jit(solution)/shard_map/ppermute | solution.py:48
  1018.3 4.1 add_convert_fusion
  1026.7 39.8 %psum.7 = f32[3,1024]{1,0:T(4,128)S(1)} all-reduce(f32[3,1024]{1,0:T(4,128)S(1)} %pad_maximum_fusion.5), channel_id=1, replica_groups=mesh['seq'=8,'batch'=4] {'seq','batch'}, use_global_device_ids=true, to_apply=%region_13.14 | all-reduce | flops 3072 | bytes 24576 | tf_op jit(solution)/shard_map/psum | solution.py:511
  1067.1 3.5 fusion.90
  1079.9 4.1 slice_bitcast_fusion.2
  1085.6 4.3 collective-permute-done.31
  (393 shorter events, 223.1 us)
Async XLA Ops:
  7.2 33.6 %all-gather.11.cloned.1.call-start = ((), (), s32[]{:S(2)}) async-start(), calls=%async_computation.9 | async-start | bytes 1310720 | tf_op jit(solution)/shard_map/all_gather | solution.py:80
  9.1 61.4 %all-gather.9.cloned.1.call-start = ((), (), s32[]{:S(2)}) async-start(), calls=%async_computation.8 | async-start | bytes 1310720 | tf_op jit(solution)/shard_map/all_gather | solution.py:80
  10.9 536.9 %all-gather.13.cloned.1.call-start = ((), (), s32[]{:S(2)}) async-start(), calls=%async_computation.10 | async-start | bytes 1474560 | tf_op jit(solution)/shard_map/all_gather | solution.py:80
  40.9 35.4 %collective-permute-start.3 = (bf16[4,2,64,1024]{3,2,1,0:T(8,128)(2,1)}, bf16[4,2,64,1024]{3,2,1,0:T(8,128)(2,1)}, u32[]{:S(2)}, u32[]{:S(2)}) collective-permute-start(bf16[4,2,64,1024]{3,2,1,0:T(8,128)(2,1)} %bitcast.420), channel_id=1, source_target_pairs={{0,4},{4,0},{8,12},{12,8},{16,20},{20,16},{24,28},{28,24},{1,5},{5... | collective-permute-start | bytes 3145736 | tf_op jit(solution)/shard_map/ppermute | solution.py:48
  70.5 25.1 %collective-permute-start = (bf16[4,2,64,1024]{3,2,1,0:T(8,128)(2,1)}, bf16[4,2,64,1024]{3,2,1,0:T(8,128)(2,1)}, u32[]{:S(2)}, u32[]{:S(2)}) collective-permute-start(bf16[4,2,64,1024]{3,2,1,0:T(8,128)(2,1)} %bitcast.31.refs_0_), channel_id=1, source_target_pairs={{0,4},{4,0},{8,12},{12,8},{16,20},{20,16},{24,28},{28,24},{1,5},{5... | collective-permute-start | bytes 3145736 | tf_op jit(solution)/shard_map/ppermute | solution.py:48
  72.1 344.1 %collective-permute-start.25 = (f32[2]{0:T(128)S(1)}, f32[2]{0:T(128)S(1)}, u32[]{:S(2)}, u32[]{:S(2)}) collective-permute-start(f32[2]{0:T(128)S(1)} %fusion.130), channel_id=1, source_target_pairs={{4,0},{8,4},{12,8},{16,12},{20,16},{24,20},{28,24},{5,1},{9,5},{13... | collective-permute-start | bytes 32 | tf_op jit(solution)/shard_map/ppermute | solution.py:347
  76.2 21.3 %collective-permute-start.4 = (bf16[4,2,64,1024]{3,2,1,0:T(8,128)(2,1)S(1)}, bf16[4,2,64,1024]{3,2,1,0:T(8,128)(2,1)}, u32[]{:S(2)}, u32[]{:S(2)}) collective-permute-start(bf16[4,2,64,1024]{3,2,1,0:T(8,128)(2,1)S(1)} %bitcast.422), channel_id=1, source_target_pairs={{0,1},{1,0},{2,3},{3,2},{4,5},{5,4},{6,7},{7,6},{8,9},{9,8},{10,11... | collective-permute-start | bytes 3145736 | tf_op jit(solution)/shard_map/ppermute | solution.py:48
  76.2 24.8 %collective-permute-start.5 = (bf16[4,2,64,1024]{3,2,1,0:T(8,128)(2,1)}, bf16[4,2,64,1024]{3,2,1,0:T(8,128)(2,1)}, u32[]{:S(2)}, u32[]{:S(2)}) collective-permute-start(bf16[4,2,64,1024]{3,2,1,0:T(8,128)(2,1)} %collective-permute-done.3.refs_1_), channel_id=1, source_target_pairs={{0,1},{1,0},{2,3},{3,2},{4,5},{5,4},{6,7},{7,6},{8,9},{9,8},{10,11... | collective-permute-start | bytes 3145736 | tf_op jit(solution)/shard_map/ppermute | solution.py:48
  77.5 908.5 %reduce-scatter.11.cloned.1.call-start = ((), (), s32[]{:S(2)}) async-start(), calls=%async_computation.7 | async-start | bytes 1228800 | tf_op jit(solution)/shard_map/reduce_scatter | solution.py:93
  77.9 157.9 %collective-permute-start.1 = (bf16[4,2,64,1024]{3,2,1,0:T(8,128)(2,1)}, bf16[4,2,64,1024]{3,2,1,0:T(8,128)(2,1)}, u32[]{:S(2)}, u32[]{:S(2)}) collective-permute-start(bf16[4,2,64,1024]{3,2,1,0:T(8,128)(2,1)} %bitcast.31.refs_0_), channel_id=1, source_target_pairs={{0,1},{1,0},{2,3},{3,2},{4,5},{5,4},{6,7},{7,6},{8,9},{9,8},{10,11... | collective-permute-start | bytes 3145736 | tf_op jit(solution)/shard_map/ppermute | solution.py:48
  95.5 140.3 %collective-permute-start.2 = (bf16[4,2,64,1024]{3,2,1,0:T(8,128)(2,1)}, bf16[4,2,64,1024]{3,2,1,0:T(8,128)(2,1)}, u32[]{:S(2)}, u32[]{:S(2)}) collective-permute-start(bf16[4,2,64,1024]{3,2,1,0:T(8,128)(2,1)} %collective-permute-done.refs_1_), channel_id=1, source_target_pairs={{0,1},{1,0},{2,3},{3,2},{4,5},{5,4},{6,7},{7,6},{8,9},{9,8},{10,11... | collective-permute-start | bytes 3145736 | tf_op jit(solution)/shard_map/ppermute | solution.py:48
  97.5 319.0 %collective-permute-start.7 = (f32[2]{0:T(128)S(1)}, f32[2]{0:T(128)S(1)}, u32[]{:S(2)}, u32[]{:S(2)}) collective-permute-start(f32[2]{0:T(128)S(1)} %fusion.130), channel_id=1, source_target_pairs={{0,4},{4,8},{8,12},{12,16},{16,20},{20,24},{24,28},{1,5},{5,9},{9,... | collective-permute-start | bytes 32 | tf_op jit(solution)/shard_map/ppermute | solution.py:347
  381.0 28.8 %collective-permute-start.6 = (bf16[2,16,64,64]{3,2,1,0:T(8,128)(2,1)S(1)}, bf16[2,16,64,64]{3,2,1,0:T(8,128)(2,1)S(1)}, u32[]{:S(2)}, u32[]{:S(2)}) collective-permute-start(bf16[2,16,64,64]{3,2,1,0:T(8,128)(2,1)S(1)} %get-tuple-element.359), channel_id=1, source_target_pairs={{0,4},{4,8},{8,12},{12,16},{16,20},{20,24},{24,28},{1,5},{5,9},{9,... | collective-permute-start | bytes 786440 | tf_op jit(solution)/shard_map/ppermute | solution.py:346
  401.1 19.6 %collective-permute-start.11 = (bf16[4,1,64,1024]{3,2,1,0:T(8,128)(2,1)}, bf16[4,1,64,1024]{3,2,1,0:T(8,128)(2,1)}, u32[]{:S(2)}, u32[]{:S(2)}) collective-permute-start(bf16[4,1,64,1024]{3,2,1,0:T(8,128)(2,1)} %bitcast.40.refs_0_), channel_id=1, source_target_pairs={{0,4},{4,0},{8,12},{12,8},{16,20},{20,16},{24,28},{28,24},{1,5},{5... | collective-permute-start | bytes 1572872 | tf_op jit(solution)/shard_map/ppermute | solution.py:48
  409.8 71.8 %collective-permute-start.12 = (bf16[4,1,64,1024]{3,2,1,0:T(8,128)(2,1)}, bf16[4,1,64,1024]{3,2,1,0:T(8,128)(2,1)}, u32[]{:S(2)}, u32[]{:S(2)}) collective-permute-start(bf16[4,1,64,1024]{3,2,1,0:T(8,128)(2,1)} %bitcast.40.refs_0_), channel_id=1, source_target_pairs={{0,1},{1,0},{2,3},{3,2},{4,5},{5,4},{6,7},{7,6},{8,9},{9,8},{10,11... | collective-permute-start | bytes 1572872 | tf_op jit(solution)/shard_map/ppermute | solution.py:48
  411.6 15.9 %collective-permute-start.8 = (bf16[2,16,64,64]{3,2,1,0:T(8,128)(2,1)}, bf16[2,16,64,64]{3,2,1,0:T(8,128)(2,1)}, u32[]{:S(2)}, u32[]{:S(2)}) collective-permute-start(bf16[2,16,64,64]{3,2,1,0:T(8,128)(2,1)} %fusion.123), channel_id=1, source_target_pairs={{0,8},{4,12},{8,16},{12,20},{16,24},{20,28},{1,9},{5,13},{9,17},{1... | collective-permute-start | bytes 786440 | tf_op jit(solution)/shard_map/ppermute | solution.py:346
  416.3 170.7 %collective-permute-start.15 = (bf16[512,1024]{1,0:T(8,128)(2,1)}, bf16[512,1024]{1,0:T(8,128)(2,1)}, u32[]{:S(2)}, u32[]{:S(2)}) collective-permute-start(bf16[512,1024]{1,0:T(8,128)(2,1)} %bitcast.403), channel_id=1, source_target_pairs={{0,1},{1,0},{2,3},{3,2},{4,5},{5,4},{6,7},{7,6},{8,9},{9,8},{10,11... | collective-permute-start | bytes 3145736 | tf_op jit(solution)/shard_map/ppermute | solution.py:48
  420.8 60.8 %collective-permute-start.13 = (bf16[4,1,64,1024]{3,2,1,0:T(8,128)(2,1)}, bf16[4,1,64,1024]{3,2,1,0:T(8,128)(2,1)S(1)}, u32[]{:S(2)}, u32[]{:S(2)}) collective-permute-start(bf16[4,1,64,1024]{3,2,1,0:T(8,128)(2,1)} %collective-permute-done.11.refs_1_), channel_id=1, source_target_pairs={{0,1},{1,0},{2,3},{3,2},{4,5},{5,4},{6,7},{7,6},{8,9},{9,8},{10,11... | collective-permute-start | bytes 1572872 | tf_op jit(solution)/shard_map/ppermute | solution.py:48
  429.8 121.5 %collective-permute-start.10 = (bf16[2,16,64,64]{3,2,1,0:T(8,128)(2,1)}, bf16[2,16,64,64]{3,2,1,0:T(8,128)(2,1)}, u32[]{:S(2)}, u32[]{:S(2)}) collective-permute-start(bf16[2,16,64,64]{3,2,1,0:T(8,128)(2,1)} %fusion.106), channel_id=1, source_target_pairs={{0,16},{4,20},{8,24},{12,28},{1,17},{5,21},{9,25},{13,29},{2,18},{... | collective-permute-start | bytes 786440 | tf_op jit(solution)/shard_map/ppermute | solution.py:346
  481.6 103.9 %collective-permute-start.16 = (bf16[4,3,64,640]{3,2,1,0:T(8,128)(2,1)}, bf16[4,3,64,640]{3,2,1,0:T(8,128)(2,1)}, u32[]{:S(2)}, u32[]{:S(2)}) collective-permute-start(bf16[4,3,64,640]{3,2,1,0:T(8,128)(2,1)} %bitcast.51.refs_0_), channel_id=1, source_target_pairs={{0,4},{4,0},{8,12},{12,8},{16,20},{20,16},{24,28},{28,24},{1,5},{5... | collective-permute-start | bytes 2949128 | tf_op jit(solution)/shard_map/ppermute | solution.py:48
  547.8 36.5 %collective-permute-start.19 = (bf16[4,3,64,768]{3,2,1,0:T(8,128)(2,1)}, bf16[4,3,64,768]{3,2,1,0:T(8,128)(2,1)}, u32[]{:S(2)}, u32[]{:S(2)}) collective-permute-start(bf16[4,3,64,768]{3,2,1,0:T(8,128)(2,1)} %bitcast.52.refs_0_), channel_id=1, source_target_pairs={{0,4},{4,0},{8,12},{12,8},{16,20},{20,16},{24,28},{28,24},{1,5},{5... | collective-permute-start | bytes 3538952 | tf_op jit(solution)/shard_map/ppermute | solution.py:48
  582.9 29.1 %collective-permute-start.20 = (bf16[4,3,64,768]{3,2,1,0:T(8,128)(2,1)}, bf16[4,3,64,768]{3,2,1,0:T(8,128)(2,1)}, u32[]{:S(2)}, u32[]{:S(2)}) collective-permute-start(bf16[4,3,64,768]{3,2,1,0:T(8,128)(2,1)} %bitcast.52.refs_0_), channel_id=1, source_target_pairs={{0,2},{1,3},{2,0},{3,1},{4,6},{5,7},{6,4},{7,5},{8,10},{9,11},{10,... | collective-permute-start | bytes 3538952 | tf_op jit(solution)/shard_map/ppermute | solution.py:48
  584.3 52.9 %collective-permute-start.21 = (bf16[4,3,64,768]{3,2,1,0:T(8,128)(2,1)}, bf16[4,3,64,768]{3,2,1,0:T(8,128)(2,1)}, u32[]{:S(2)}, u32[]{:S(2)}) collective-permute-start(bf16[4,3,64,768]{3,2,1,0:T(8,128)(2,1)} %collective-permute-done.19.refs_1_), channel_id=1, source_target_pairs={{0,2},{1,3},{2,0},{3,1},{4,6},{5,7},{6,4},{7,5},{8,10},{9,11},{10,... | collective-permute-start | bytes 3538952 | tf_op jit(solution)/shard_map/ppermute | solution.py:48
  585.5 79.7 %collective-permute-start.17 = (bf16[4,3,64,640]{3,2,1,0:T(8,128)(2,1)}, bf16[4,3,64,640]{3,2,1,0:T(8,128)(2,1)}, u32[]{:S(2)}, u32[]{:S(2)}) collective-permute-start(bf16[4,3,64,640]{3,2,1,0:T(8,128)(2,1)} %bitcast.51.refs_0_), channel_id=1, source_target_pairs={{0,2},{1,3},{2,0},{3,1},{4,6},{5,7},{6,4},{7,5},{8,10},{9,11},{10,... | collective-permute-start | bytes 2949128 | tf_op jit(solution)/shard_map/ppermute | solution.py:48
  586.9 92.0 %collective-permute-start.18 = (bf16[4,3,64,640]{3,2,1,0:T(8,128)(2,1)}, bf16[4,3,64,640]{3,2,1,0:T(8,128)(2,1)}, u32[]{:S(2)}, u32[]{:S(2)}) collective-permute-start(bf16[4,3,64,640]{3,2,1,0:T(8,128)(2,1)} %collective-permute-done.16.refs_1_), channel_id=1, source_target_pairs={{0,2},{1,3},{2,0},{3,1},{4,6},{5,7},{6,4},{7,5},{8,10},{9,11},{10,... | collective-permute-start | bytes 2949128 | tf_op jit(solution)/shard_map/ppermute | solution.py:48
  708.4 14.8 %collective-permute-start.23 = (bf16[512,1024]{1,0:T(8,128)(2,1)}, bf16[512,1024]{1,0:T(8,128)(2,1)}, u32[]{:S(2)}, u32[]{:S(2)}) collective-permute-start(bf16[512,1024]{1,0:T(8,128)(2,1)} %get-tuple-element.133), channel_id=1, source_target_pairs={{0,1},{1,0},{2,3},{3,2},{4,5},{5,4},{6,7},{7,6},{8,9},{9,8},{10,11... | collective-permute-start | bytes 3145736 | tf_op jit(solution)/shard_map/ppermute | solution.py:48
  708.5 18.1 %collective-permute-start.22 = (bf16[512,1024]{1,0:T(8,128)(2,1)}, bf16[512,1024]{1,0:T(8,128)(2,1)}, u32[]{:S(2)}, u32[]{:S(2)}) collective-permute-start(bf16[512,1024]{1,0:T(8,128)(2,1)} %get-tuple-element.131), channel_id=1, source_target_pairs={{0,1},{1,0},{2,3},{3,2},{4,5},{5,4},{6,7},{7,6},{8,9},{9,8},{10,11... | collective-permute-start | bytes 3145736 | tf_op jit(solution)/shard_map/ppermute | solution.py:48
  752.0 15.8 %collective-permute-start.24 = (bf16[2,16,64,64]{3,2,1,0:T(8,128)(2,1)S(1)}, bf16[2,16,64,64]{3,2,1,0:T(8,128)(2,1)S(1)}, u32[]{:S(2)}, u32[]{:S(2)}) collective-permute-start(bf16[2,16,64,64]{3,2,1,0:T(8,128)(2,1)S(1)} %get-tuple-element.365), channel_id=1, source_target_pairs={{4,0},{8,4},{12,8},{16,12},{20,16},{24,20},{28,24},{5,1},{9,5},{13... | collective-permute-start | bytes 786440 | tf_op jit(solution)/shard_map/ppermute | solution.py:346
  769.6 20.5 %collective-permute-start.26 = (bf16[2,16,64,64]{3,2,1,0:T(8,128)(2,1)}, bf16[2,16,64,64]{3,2,1,0:T(8,128)(2,1)}, u32[]{:S(2)}, u32[]{:S(2)}) collective-permute-start(bf16[2,16,64,64]{3,2,1,0:T(8,128)(2,1)} %fusion.122), channel_id=1, source_target_pairs={{8,0},{12,4},{16,8},{20,12},{24,16},{28,20},{9,1},{13,5},{17,9},{2... | collective-permute-start | bytes 786440 | tf_op jit(solution)/shard_map/ppermute | solution.py:346
  772.0 13.3 %collective-permute-start.27 = (f32[2]{0:T(128)S(1)}, f32[2]{0:T(128)S(1)}, u32[]{:S(2)}, u32[]{:S(2)}) collective-permute-start(f32[2]{0:T(128)S(1)} %get-tuple-element.353), channel_id=1, source_target_pairs={{8,0},{12,4},{16,8},{20,12},{24,16},{28,20},{9,1},{13,5},{17,9},{2... | collective-permute-start | bytes 32 | tf_op jit(solution)/shard_map/ppermute | solution.py:347
  785.4 135.3 %collective-permute-start.37 = (bf16[2,4,3,64,768]{4,3,2,1,0:T(8,128)(2,1)}, bf16[2,4,3,64,768]{4,3,2,1,0:T(8,128)(2,1)}, u32[]{:S(2)}, u32[]{:S(2)}) collective-permute-start(bf16[2,4,3,64,768]{4,3,2,1,0:T(8,128)(2,1)} %get-tuple-element.138), channel_id=1, source_target_pairs={{0,2},{1,3},{2,0},{3,1},{4,6},{5,7},{6,4},{7,5},{8,10},{9,11},{10,... | collective-permute-start | bytes 7077896 | tf_op jit(solution)/shard_map/ppermute | solution.py:48
  786.8 105.2 %collective-permute-start.40 = (bf16[2,4,3,64,640]{4,3,2,1,0:T(8,128)(2,1)}, bf16[2,4,3,64,640]{4,3,2,1,0:T(8,128)(2,1)}, u32[]{:S(2)}, u32[]{:S(2)}) collective-permute-start(bf16[2,4,3,64,640]{4,3,2,1,0:T(8,128)(2,1)} %get-tuple-element.140), channel_id=1, source_target_pairs={{0,2},{1,3},{2,0},{3,1},{4,6},{5,7},{6,4},{7,5},{8,10},{9,11},{10,... | collective-permute-start | bytes 5898248 | tf_op jit(solution)/shard_map/ppermute | solution.py:48
  791.5 25.8 %collective-permute-start.28 = (bf16[2,16,64,64]{3,2,1,0:T(8,128)(2,1)S(1)}, bf16[2,16,64,64]{3,2,1,0:T(8,128)(2,1)S(1)}, u32[]{:S(2)}, u32[]{:S(2)}) collective-permute-start(bf16[2,16,64,64]{3,2,1,0:T(8,128)(2,1)S(1)} %fusion.111), channel_id=1, source_target_pairs={{16,0},{20,4},{24,8},{28,12},{17,1},{21,5},{25,9},{29,13},{18,2},{... | collective-permute-start | bytes 786440 | tf_op jit(solution)/shard_map/ppermute | solution.py:346
  892.0 60.6 %collective-permute-start.33 = (bf16[2,4,2,64,1024]{4,3,2,1,0:T(8,128)(2,1)}, bf16[2,4,2,64,1024]{4,3,2,1,0:T(8,128)(2,1)}, u32[]{:S(2)}, u32[]{:S(2)}) collective-permute-start(bf16[2,4,2,64,1024]{4,3,2,1,0:T(8,128)(2,1)} %pad_maximum_fusion.4), channel_id=1, source_target_pairs={{0,1},{1,0},{2,3},{3,2},{4,5},{5,4},{6,7},{7,6},{8,9},{9,8},{10,11... | collective-permute-start | bytes 6291464 | tf_op jit(solution)/shard_map/ppermute | solution.py:48
  894.2 23.6 %collective-permute-start.41 = (bf16[4,3,64,640]{3,2,1,0:T(8,128)(2,1)S(1)}, bf16[4,3,64,640]{3,2,1,0:T(8,128)(2,1)S(1)}, u32[]{:S(2)}, u32[]{:S(2)}) collective-permute-start(bf16[4,3,64,640]{3,2,1,0:T(8,128)(2,1)S(1)} %fusion.121), channel_id=1, source_target_pairs={{0,4},{4,0},{8,12},{12,8},{16,20},{20,16},{24,28},{28,24},{1,5},{5... | collective-permute-start | bytes 2949128 | tf_op jit(solution)/shard_map/ppermute | solution.py:48
  920.6 66.7 %reduce-scatter.9.cloned.1.call-start = ((), (), s32[]{:S(2)}) async-start(), calls=%async_computation.6 | async-start | bytes 1474560 | tf_op jit(solution)/shard_map/reduce_scatter | solution.py:93
  922.8 26.9 %collective-permute-start.38 = (bf16[4,3,64,768]{3,2,1,0:T(8,128)(2,1)S(1)}, bf16[4,3,64,768]{3,2,1,0:T(8,128)(2,1)S(1)}, u32[]{:S(2)}, u32[]{:S(2)}) collective-permute-start(bf16[4,3,64,768]{3,2,1,0:T(8,128)(2,1)S(1)} %fusion.98), channel_id=1, source_target_pairs={{0,4},{4,0},{8,12},{12,8},{16,20},{20,16},{24,28},{28,24},{1,5},{5... | collective-permute-start | bytes 3538952 | tf_op jit(solution)/shard_map/ppermute | solution.py:48
  931.1 49.6 %collective-permute-start.29 = (bf16[2,4,3,64,1024]{4,3,2,1,0:T(8,128)(2,1)}, bf16[2,4,3,64,1024]{4,3,2,1,0:T(8,128)(2,1)}, u32[]{:S(2)}, u32[]{:S(2)}) collective-permute-start(bf16[2,4,3,64,1024]{4,3,2,1,0:T(8,128)(2,1)} %pad_maximum_fusion.1), channel_id=1, source_target_pairs={{0,1},{1,0},{2,3},{3,2},{4,5},{5,4},{6,7},{7,6},{8,9},{9,8},{10,11... | collective-permute-start | bytes 9437192 | tf_op jit(solution)/shard_map/ppermute | solution.py:48
  952.5 118.0 %reduce-scatter.7.cloned.1.call-start = ((), (), s32[]{:S(2)}) async-start(), calls=%async_computation.5 | async-start | bytes 1310720 | tf_op jit(solution)/shard_map/reduce_scatter | solution.py:93
  954.6 23.2 %collective-permute-start.34 = (bf16[4,2,64,1024]{3,2,1,0:T(8,128)(2,1)S(1)}, bf16[4,2,64,1024]{3,2,1,0:T(8,128)(2,1)S(1)}, u32[]{:S(2)}, u32[]{:S(2)}) collective-permute-start(bf16[4,2,64,1024]{3,2,1,0:T(8,128)(2,1)S(1)} %fusion.83), channel_id=1, source_target_pairs={{0,4},{4,0},{8,12},{12,8},{16,20},{20,16},{24,28},{28,24},{1,5},{5... | collective-permute-start | bytes 3145736 | tf_op jit(solution)/shard_map/ppermute | solution.py:48
  980.6 97.5 %reduce-scatter.5.cloned.1.call-start = ((), (), s32[]{:S(2)}) async-start(), calls=%async_computation.4 | async-start | bytes 1966080 | tf_op jit(solution)/shard_map/reduce_scatter | solution.py:93
  984.5 33.8 %collective-permute-start.30 = (bf16[4,3,64,1024]{3,2,1,0:T(8,128)(2,1)}, bf16[4,3,64,1024]{3,2,1,0:T(8,128)(2,1)}, u32[]{:S(2)}, u32[]{:S(2)}) collective-permute-start(bf16[4,3,64,1024]{3,2,1,0:T(8,128)(2,1)} %fusion.78), channel_id=1, source_target_pairs={{0,4},{4,0},{8,12},{12,8},{16,20},{20,16},{24,28},{28,24},{1,5},{5... | collective-permute-start | bytes 4718600 | tf_op jit(solution)/shard_map/ppermute | solution.py:48
  986.0 36.4 %collective-permute-start.42 = (bf16[3,64,640]{2,1,0:T(8,128)(2,1)}, bf16[3,64,640]{2,1,0:T(8,128)(2,1)}, u32[]{:S(2)}, u32[]{:S(2)}) collective-permute-start(bf16[3,64,640]{2,1,0:T(8,128)(2,1)} %bitcast.441), channel_id=1, source_target_pairs={{0,2},{1,3},{2,0},{3,1},{4,6},{5,7},{6,4},{7,5},{8,10},{9,11},{10,... | collective-permute-start | bytes 737288 | tf_op jit(solution)/shard_map/ppermute | solution.py:48
  987.3 36.4 %collective-permute-start.39 = (bf16[3,64,768]{2,1,0:T(8,128)(2,1)}, bf16[3,64,768]{2,1,0:T(8,128)(2,1)}, u32[]{:S(2)}, u32[]{:S(2)}) collective-permute-start(bf16[3,64,768]{2,1,0:T(8,128)(2,1)} %bitcast.435), channel_id=1, source_target_pairs={{0,2},{1,3},{2,0},{3,1},{4,6},{5,7},{6,4},{7,5},{8,10},{9,11},{10,... | collective-permute-start | bytes 884744 | tf_op jit(solution)/shard_map/ppermute | solution.py:48
  1026.7 46.2 %collective-permute-start.43 = (bf16[3,128,1408]{2,1,0:T(8,128)(2,1)}, bf16[3,128,1408]{2,1,0:T(8,128)(2,1)}, u32[]{:S(2)}, u32[]{:S(2)}) collective-permute-start(bf16[3,128,1408]{2,1,0:T(8,128)(2,1)} %maximum_maximum_fusion), channel_id=1, source_target_pairs={{0,1},{1,0},{2,3},{3,2},{4,5},{5,4},{6,7},{7,6},{8,9},{9,8},{10,11... | collective-permute-start | bytes 3244040 | tf_op jit(solution)/shard_map/ppermute | solution.py:48
  1070.5 7.5 collective-permute-start.35
  1078.1 7.5 collective-permute-start.36
  1078.2 11.7 %collective-permute-start.31 = (bf16[3,64,1024]{2,1,0:T(8,128)(2,1)}, bf16[3,64,1024]{2,1,0:T(8,128)(2,1)S(1)}, u32[]{:S(2)}, u32[]{:S(2)}) collective-permute-start(bf16[3,64,1024]{2,1,0:T(8,128)(2,1)} %bitcast.434), channel_id=1, source_target_pairs={{0,2},{1,3},{2,0},{3,1},{4,6},{5,7},{6,4},{7,5},{8,10},{9,11},{10,... | collective-permute-start | bytes 1179656 | tf_op jit(solution)/shard_map/ppermute | solution.py:48
  (82 other events, 1158.0 us)
Sparse Core Ops, SparseCore 0:
  10.2 30.6 all-gather.10
  43.0 27.4 all-gather.8
  77.6 31.1 all-gather.12
  920.8 24.3 reduce-scatter.10
  952.6 27.3 reduce-scatter.8
  982.8 25.8 reduce-scatter.6
  1022.5 34.1 reduce-scatter.4

commit v2 on v0

v2 whole, which is shorter than its diff:
```python
import functools

import jax
import jax.numpy as jnp
from jax import lax
from jax.experimental import pallas as pl
from jax.experimental.pallas import tpu as pltpu
from jax.sharding import PartitionSpec as P

HEADS = 16
HEAD = 64
EPSILON = 1e-06
BF = jnp.bfloat16
F32 = jnp.float32
VMEM = pl.BlockSpec(memory_space=pltpu.VMEM)
SMEM = pl.BlockSpec(memory_space=pltpu.SMEM)
ANY = pl.BlockSpec(memory_space=pl.ANY)
LIMIT = 60 * 1024 * 1024
LIGHT = pl.CostEstimate(flops=1, bytes_accessed=1, transcendentals=0)


def inverse_rms(values):
    return lax.rsqrt(jnp.mean(values * values, axis=-1, keepdims=True) + EPSILON)


def dot(left, right):
    return jnp.dot(left, right, preferred_element_type=F32)


def dot_nt(left, right):
    return lax.dot_general(left, right, (((1,), (1,)), ((), ())), preferred_element_type=F32)


def dot_tn(left, right):
    return lax.dot_general(left, right, (((0,), (0,)), ((), ())), preferred_element_type=F32)


def swap(value, axis, bit, size):
    return lax.ppermute(value, axis, [(i, i ^ bit) for i in range(size)])


def tie(value, *others):
    return lax.optimization_barrier((value,) + others)[0]


class Plan:
    def __init__(self, mesh_shape, width):
        self.seq = mesh_shape["seq"]
        self.batch = mesh_shape["batch"]
        self.rows = width // self.seq
        self.fast = self.seq == 8 and self.batch == 4
        self.place = lax.axis_index("seq")
        self.lane = lax.axis_index("batch")
        self.nz = 4 if self.fast else self.seq
        self.span = width // self.nz
        self.groups = [[z * 2 + x for z in range(self.nz)] for x in range(2)]

    def half(self, bit):
        return (self.lane // bit) % 2

    def bases(self, bits):
        first = jnp.zeros((1,), jnp.int32)
        if self.fast:
            size = self.rows
            x = self.place % 2
            first = jnp.stack([x * size, (1 - x) * size])
            for bit in bits:
                size //= 2
                mine = self.half(bit)
                first = jnp.concatenate([first + mine * size, first + (1 - mine) * size])
        return first.astype(jnp.int32)

    def mine(self, shard, bits):
        if self.fast:
            for bit in bits:
                m, rows, w = shard.shape
                shard = lax.dynamic_slice(shard, (0, self.half(bit) * (rows // 2), 0), (m, rows // 2, w))
        return shard

    def along(self, mine, direct):
        if not self.fast:
            return lax.all_gather(mine, "seq", axis=0)
        if direct:
            copies = jnp.broadcast_to(mine[None], (self.nz,) + mine.shape)
            return lax.all_to_all(copies, "seq", 0, 0, axis_index_groups=self.groups)
        return lax.all_gather(mine, "seq", axis=0, axis_index_groups=self.groups)

    def across(self, near):
        return [near, swap(near, "seq", 1, self.seq)] if self.fast else [near]

    def pair(self, pieces, bit):
        return pieces + [swap(p, "batch", bit, 4) for p in pieces] if self.fast else pieces

    def sum_along(self, near):
        return lax.psum_scatter(near, "seq", scatter_dimension=0, axis_index_groups=self.groups)

    def join(self, mine, bit, axis):
        other = swap(mine, "batch", bit, self.batch)
        lower = self.half(bit) == 0
        return jnp.concatenate([jnp.where(lower, mine, other), jnp.where(lower, other, mine)], axis=axis)


def add(left, right):
    return (left.astype(F32) + right.astype(F32)).astype(BF)


def params(mib):
    return pltpu.CompilerParams(vmem_limit_bytes=mib * 1024 * 1024)


def low_lanes():
    return lax.broadcasted_iota(jnp.int32, (1, 128), 1) < HEAD


def spread(state):
    low = low_lanes()
    zero = jnp.zeros_like(state)
    return jnp.concatenate([jnp.where(low, state, zero), jnp.where(low, zero, state)], axis=0)


def squeeze(full):
    return jnp.where(low_lanes(), full[:HEAD], full[HEAD:])


def head_sums(values):
    row = lax.broadcasted_iota(jnp.int32, (128, 128), 0) < HEAD
    col = lax.broadcasted_iota(jnp.int32, (128, 128), 1) < HEAD
    ones = (row == col).astype(BF)
    high = values.astype(BF)
    rest = values - high.astype(F32)
    mid = rest.astype(BF)
    return dot(high, ones) + dot(mid, ones)


def block(i, size=256):
    return pl.ds(pl.multiple_of(i * size, size), size)


def fetch(base_ref, pieces, weight, sem, picks):
    return [
        [
            pltpu.make_async_copy(
                piece.at[:, pick],
                weight.at[:, k, pl.ds(pl.multiple_of(base_ref[b], 16), piece.shape[2]), :],
                sem.at[k, b],
            )
            for b, piece in enumerate(pieces)
        ]
        for k, pick in enumerate(picks)
    ]


def hand_out(base_ref, grads, outs, sem):
    m = grads.shape[1]
    return [
        [
            pltpu.make_async_copy(
                grads.at[:, k, pl.ds(pl.multiple_of(base_ref[b], 16), out.shape[-2]), :],
                out.at[:, k],
                sem.at[k, b],
            )
            for b, out in enumerate(outs)
        ]
        for k in range(m)
    ]


def piece_shapes(plan, m, part, w, count):
    return [jax.ShapeDtypeStruct((plan.nz, m, part, w), BF)] * (count if plan.fast else 1)


def start_all(copies):
    for c in copies:
        c.start()


def wait_all(copies):
    for c in copies:
        c.wait()


def soft(x):
    e = jnp.exp(-jnp.abs(x))
    return jnp.maximum(x, 0.0) + jnp.log1p(e), jnp.where(x >= 0.0, 1.0, e) / (1.0 + e)


def kv_body(plan, nb, base_ref, tokens_ref, gain_ref, tail_ref, *refs):
    pieces = refs[:nb]
    normed_ref, keys_ref, sig_ref, values_ref, fresh_ref, weight, sem = refs[nb:]
    d = tokens_ref.shape[1]
    copies = fetch(base_ref, pieces, weight, sem, (0, 1))
    for c in copies:
        start_all(c)

    def norm(i, _):
        source = tokens_ref[block(i), :].astype(F32)
        normed_ref[block(i), :] = (source * inverse_rms(source) * gain_ref[...]).astype(BF)
        return 0

    lax.fori_loop(0, 2, norm, 0)
    wait_all(copies[0])

    def key_part(j, _):
        linear = dot(normed_ref[...], weight[:, 0, :, block(j)].reshape(d, 256))
        plus, sig = soft(linear)
        keys_ref[:, block(j)] = plus.astype(BF)
        sig_ref[:, block(j)] = sig.astype(BF)
        return 0

    lax.fori_loop(0, d // 256, key_part, 0)
    wait_all(copies[1])

    def value_part(j, _):
        linear = dot(normed_ref[...], weight[:, 1, :, block(j)].reshape(d, 256))
        values_ref[:, block(j)] = linear.astype(BF)
        return 0

    lax.fori_loop(0, d // 256, value_part, 0)

    def states(i, _):
        rows, lanes = block(i // 8), block(i % 8, 128)
        tail = tail_ref[rows, :].astype(BF)
        fresh_ref[i] = squeeze(dot_tn(keys_ref[rows, lanes], values_ref[rows, lanes] * tail))
        return 0

    lax.fori_loop(0, 16, states, 0, unroll=2)


def kv_call(plan, bases, tokens, gain, tail, pieces):
    nb = len(pieces)
    count, d = tokens.shape
    shape = jax.ShapeDtypeStruct((count, d), BF)
    return pl.pallas_call(
        functools.partial(kv_body, plan, nb),
        out_shape=[shape] * 4 + [jax.ShapeDtypeStruct((16, HEAD, 128), F32)],
        in_specs=[SMEM] + [VMEM] * 3 + [ANY] * nb,
        out_specs=[VMEM] * 5,
        scratch_shapes=[
            pltpu.VMEM((plan.nz, 2, plan.span, d), BF),
            pltpu.SemaphoreType.DMA((2, nb)),
        ],
        compiler_params=params(24),
        cost_estimate=LIGHT,
        name="keys_values",
    )(bases, tokens, gain, tail, *pieces)


def qg_body(plan, nb, base_ref, normed_ref, *refs):
    pieces = refs[:nb]
    query_ref, sig_ref, gate_ref, weight, sem = refs[nb:]
    d = normed_ref.shape[1]
    copies = fetch(base_ref, pieces, weight, sem, (0, 1))
    for c in copies:
        start_all(c)
    wait_all(copies[0])

    def query_part(j, _):
        linear = dot(normed_ref[...], weight[:, 0, :, block(j)].reshape(d, 256))
        plus, sig = soft(linear)
        query_ref[:, block(j)] = plus.astype(BF)
        sig_ref[:, block(j)] = sig.astype(BF)
        return 0

    lax.fori_loop(0, d // 256, query_part, 0)
    wait_all(copies[1])

    def gate_part(j, _):
        linear = dot(normed_ref[...], weight[:, 1, :, block(j)].reshape(d, 256))
        gate_ref[:, block(j)] = jax.nn.sigmoid(linear)
        return 0

    lax.fori_loop(0, d // 256, gate_part, 0)


def qg_call(plan, bases, normed, pieces):
    nb = len(pieces)
    count, d = normed.shape
    shape = jax.ShapeDtypeStruct((count, d), BF)
    return pl.pallas_call(
        functools.partial(qg_body, plan, nb),
        out_shape=[shape, shape, jax.ShapeDtypeStruct((count, d), F32)],
        in_specs=[SMEM, VMEM] + [ANY] * nb,
        out_specs=[VMEM] * 3,
        scratch_shapes=[
            pltpu.VMEM((plan.nz, 2, plan.span, d), BF),
            pltpu.SemaphoreType.DMA((2, nb)),
        ],
        compiler_params=params(24),
        cost_estimate=LIGHT,
        name="query_gate",
    )(bases, normed, *pieces)


def pair_mask(segcol_ref, segrow_ref, r):
    t = lax.broadcasted_iota(jnp.int32, (256, 256), 0)
    s = lax.broadcasted_iota(jnp.int32, (256, 256), 1)
    return (segcol_ref[block(r), :] == segrow_ref[r]) & (t >= s)


def attend_body(
    plan, nb, base_ref, query_ref, keys_ref, values_ref, gate_ref, state_ref, segcol_ref, segrow_ref,
    gain_ref, tokens_ref, midgain_ref, *refs
):
    pieces = refs[:nb]
    attended_ref, gated_ref, middle_ref, normed_ref, mask_ref, weight, sem = refs[nb:]
    d = query_ref.shape[1]
    (copies,) = fetch(base_ref, pieces, weight, sem, (2,))
    start_all(copies)
    for r in range(2):
        mask_ref[r] = pair_mask(segcol_ref, segrow_ref, r).astype(F32)

    def pair(i, _):
        r = i // 8
        rows, lanes = block(r), block(i % 8, 128)
        low = low_lanes()
        mask = mask_ref[r]
        q, k, v = query_ref[rows, lanes], keys_ref[rows, lanes], values_ref[rows, lanes]
        zero = jnp.zeros_like(q)
        inherit = (segcol_ref[rows, :] == 0.0).astype(BF)
        q0, q1 = jnp.where(low, q, zero), jnp.where(low, zero, q)
        w0 = (dot_nt(q0, k) * mask).astype(BF)
        w1 = (dot_nt(q1, k) * mask).astype(BF)
        carried = dot(q * inherit, spread(state_ref[i]))
        attended = jnp.where(low, dot(w0, v), dot(w1, v)) + carried
        inverse = lax.rsqrt(head_sums(attended * attended) * (1.0 / HEAD) + EPSILON)
        headed = attended * inverse * gain_ref[:, lanes]
        attended_ref[rows, lanes] = attended
        gated_ref[rows, lanes] = (headed * gate_ref[rows, lanes]).astype(BF)
        return 0

    lax.fori_loop(0, 16, pair, 0, unroll=2)
    wait_all(copies)

    def project(j, _):
        out = dot(gated_ref[...], weight[:, 0, :, block(j)].reshape(d, 256))
        middle_ref[:, block(j)] = tokens_ref[:, block(j)].astype(F32) + out
        return 0

    lax.fori_loop(0, d // 256, project, 0)

    def norm(i, _):
        middle = middle_ref[block(i), :]
        normed_ref[block(i), :] = (middle * inverse_rms(middle) * midgain_ref[...]).astype(BF)
        return 0

    lax.fori_loop(0, 2, norm, 0)


def attend_call(plan, bases, query, keys, values, gate, state, segcol, segrow, gain, tokens, midgain, pieces):
    nb = len(pieces)
    count, d = query.shape
    low, high = jax.ShapeDtypeStruct((count, d), BF), jax.ShapeDtypeStruct((count, d), F32)
    return pl.pallas_call(
        functools.partial(attend_body, plan, nb),
        out_shape=[high, low, high, low],
        in_specs=[SMEM] + [VMEM] * 10 + [ANY] * nb,
        out_specs=[VMEM] * 4,
        scratch_shapes=[
            pltpu.VMEM((2, 256, 256), F32),
            pltpu.VMEM((plan.nz, 1, plan.span, d), BF),
            pltpu.SemaphoreType.DMA((1, nb)),
        ],
        compiler_params=params(28),
        cost_estimate=LIGHT,
        name="attend",
    )(bases, query, keys, values, gate, state, segcol, segrow, gain, tokens, midgain, *pieces)


def mid_body(
    plan, nb, base_ref, back_ref, got_ref, middle_ref, midgain_ref, upstream_ref, gate_ref, attended_ref,
    gain_ref, query_ref, segcol_ref, *refs
):
    pieces = refs[:nb]
    midback_ref, branch_ref, gateback_ref, attback_ref, direct_ref, gains_ref, gated_back, weight, sem = refs[nb:]
    d = query_ref.shape[1]
    (copies,) = fetch(base_ref, pieces, weight, sem, (2,))
    start_all(copies)

    def norm(i, total):
        rows = block(i, 128)
        dy = back_ref[rows, :].astype(F32) + got_ref[rows, :].astype(F32)
        v = middle_ref[rows, :]
        r = inverse_rms(v)
        scaled = dy * midgain_ref[...]
        mean = jnp.mean(scaled * v, axis=-1, keepdims=True)
        back = upstream_ref[rows, :].astype(F32) + r * scaled - v * (r * r * r * mean)
        midback_ref[rows, :] = back
        branch_ref[rows, :] = back.astype(BF)
        return total + jnp.sum(dy * v * r, axis=0, keepdims=True)

    gains_ref[0:1, :] = lax.fori_loop(0, 4, norm, jnp.zeros((1, d), F32))
    wait_all(copies)

    slabs = 256 // plan.span

    def through(j, _):
        out_w = weight[pl.ds(j * slabs, slabs), 0].reshape(256, d)
        gated_back[:, block(j)] = dot_nt(branch_ref[...], out_w)
        return 0

    lax.fori_loop(0, d // 256, through, 0)

    def pair(p, _):
        lanes = block(p, 128)
        gain = gain_ref[:, lanes]
        total = jnp.zeros((1, 128), F32)
        for r in range(2):
            rows = pl.ds(r * 256, 256)
            att = attended_ref[rows, lanes]
            inverse = lax.rsqrt(head_sums(att * att) * (1.0 / HEAD) + EPSILON)
            gate = gate_ref[rows, lanes]
            back = gated_back[rows, lanes]
            unit = att * inverse
            gateback_ref[rows, lanes] = (back * (unit * gain) * gate * (1.0 - gate)).astype(BF)
            dy = back * gate
            total = total + jnp.sum(dy * unit, axis=0, keepdims=True)
            scaled = dy * gain
            mean = head_sums(scaled * unit) * (1.0 / HEAD)
            attback = (inverse * (scaled - unit * mean)).astype(BF)
            attback_ref[rows, lanes] = attback
            inherit = (segcol_ref[rows, :] == 0.0).astype(BF)
            direct_ref[r * 8 + p] = squeeze(dot_tn(query_ref[rows, lanes] * inherit, attback))
        gains_ref[1:2, lanes] = total
        return 0

    lax.fori_loop(0, 8, pair, 0)


def mid_call(plan, bases, back, got, middle, midgain, upstream, gate, attended, gain, query, segcol, pieces):
    nb = len(pieces)
    count, d = query.shape
    low, high = jax.ShapeDtypeStruct((count, d), BF), jax.ShapeDtypeStruct((count, d), F32)
    return pl.pallas_call(
        functools.partial(mid_body, plan, nb),
        out_shape=[
            high, low, low, low,
            jax.ShapeDtypeStruct((16, HEAD, 128), F32),
            jax.ShapeDtypeStruct((2, d), F32),
        ],
        in_specs=[SMEM] + [VMEM] * 10 + [ANY] * nb,
        out_specs=[VMEM] * 6,
        scratch_shapes=[
            pltpu.VMEM((count, d), F32),
            pltpu.VMEM((plan.nz, 1, plan.span, d), BF),
            pltpu.SemaphoreType.DMA((1, nb)),
        ],
        compiler_params=params(32),
        cost_estimate=LIGHT,
        name="middle_back",
    )(bases, back, got, middle, midgain, upstream, gate, attended, gain, query, segcol, *pieces)


def turn_rows(source_ref, turned):
    def turn(i, _):
        turned[block(i), :] = source_ref[:, block(i)].T
        return 0

    lax.fori_loop(0, source_ref.shape[1] // 256, turn, 0)


def gradient_rows(plan, turned, right_ref, grads, k):
    d = turned.shape[0]
    slabs = 256 // plan.span

    def features(i, _):
        value = dot(turned[block(i), :], right_ref[...]).astype(BF)
        grads[pl.ds(i * slabs, slabs), k] = value.reshape(slabs, plan.span, d)
        return 0

    lax.fori_loop(0, d // 256, features, 0)


def grads_body(plan, which, base_ref, *refs):
    m, n = len(which), max(which) + 1
    lefts, rights = refs[:n], refs[n : n + m]
    outs = refs[n + m : -3]
    turned, grads, sem = refs[-3:]
    copies = hand_out(base_ref, grads, outs, sem)
    for k in range(m):
        if k == 0 or which[k] != which[k - 1]:
            turn_rows(lefts[which[k]], turned)
        gradient_rows(plan, turned, rights[k], grads, k)
        start_all(copies[k])
    for k in range(m):
        wait_all(copies[k])


def grads_call(plan, bases, lefts, which, rights):
    m = len(rights)
    count, d = lefts[0].shape
    outs = piece_shapes(plan, m, plan.rows // 2 if plan.fast else plan.rows, d, 4)
    return pl.pallas_call(
        functools.partial(grads_body, plan, which),
        out_shape=outs,
        in_specs=[SMEM] + [VMEM] * (len(lefts) + m),
        out_specs=[ANY] * len(outs),
        scratch_shapes=[
            pltpu.VMEM((d, count), BF),
            pltpu.VMEM((plan.nz, m, plan.span, d), BF),
            pltpu.SemaphoreType.DMA((m, len(outs))),
        ],
        compiler_params=params(24),
        cost_estimate=LIGHT,
        name="square_gradients",
    )(bases, *lefts, *rights)


def inner_body(
    plan, query_ref, keys_ref, values_ref, qsig_ref, attback_ref, state_ref, segcol_ref, segrow_ref,
    qback_ref, kin_ref, vin_ref, mask_ref, turn_ref
):
    for r in range(2):
        mask = pair_mask(segcol_ref, segrow_ref, r).astype(F32)
        mask_ref[r] = mask
        turn_ref[r] = mask.T

    def pair(i, _):
        r = i // 8
        rows, lanes = block(r), block(i % 8, 128)
        low = low_lanes()
        mask, mask_t = mask_ref[r], turn_ref[r]
        q, k, v, ab = (x[rows, lanes] for x in (query_ref, keys_ref, values_ref, attback_ref))
        zero = jnp.zeros_like(q)
        inherit = (segcol_ref[rows, :] == 0.0).astype(BF)
        halves = []
        for h in range(2):
            pick = (lambda x: jnp.where(low, x, zero)) if h == 0 else (lambda x: jnp.where(low, zero, x))
            k_h, v_h, ab_h = pick(k), pick(v), pick(ab)
            w_t = (dot_nt(k_h, q) * mask_t).astype(BF)
            sb = (dot_nt(ab_h, v) * mask).astype(BF)
            sb_t = (dot_nt(v_h, ab) * mask_t).astype(BF)
            halves.append((dot(sb, k), dot(sb_t, q), dot(w_t, ab)))
        qb, kb, vb = (jnp.where(low, a, b) for a, b in zip(*halves))
        qb = qb + dot_nt(ab * inherit, spread(state_ref[i]))
        qback_ref[rows, lanes] = (qb * qsig_ref[rows, lanes].astype(F32)).astype(BF)
        kin_ref[rows, lanes] = kb
        vin_ref[rows, lanes] = vb
        return 0

    lax.fori_loop(0, 16, pair, 0)


def inner_call(plan, query, keys, values, qsig, attback, state, segcol, segrow):
    count, d = query.shape
    low, high = jax.ShapeDtypeStruct((count, d), BF), jax.ShapeDtypeStruct((count, d), F32)
    return pl.pallas_call(
        functools.partial(inner_body, plan),
        out_shape=[low, high, high],
        in_specs=[VMEM] * 8,
        out_specs=[VMEM] * 3,
        scratch_shapes=[pltpu.VMEM((2, 256, 256), F32), pltpu.VMEM((2, 256, 256), F32)],
        compiler_params=params(20),
        cost_estimate=LIGHT,
        name="attend_back",
    )(query, keys, values, qsig, attback, state, segcol, segrow)


def outer_body(
    plan, sides, base_ref, keys_ref, values_ref, ksig_ref, kin_ref, vin_ref, after_ref, segcol_ref, segrow_ref,
    normed_ref, *refs
):
    outs = refs[:sides]
    kback_ref, vback_ref, turned, grads, sem = refs[sides:]
    copies = hand_out(base_ref, grads, outs, sem)

    def pair(i, _):
        r = i // 8
        rows, lanes = block(r), block(i % 8, 128)
        tail = (segcol_ref[rows, :] == segrow_ref[r][:, 255:256]).astype(F32)
        after = spread(after_ref[i])
        kb = kin_ref[rows, lanes] + dot_nt(values_ref[rows, lanes], after) * tail
        vb = vin_ref[rows, lanes] + dot(keys_ref[rows, lanes], after) * tail
        kback_ref[rows, lanes] = (kb * ksig_ref[rows, lanes].astype(F32)).astype(BF)
        vback_ref[rows, lanes] = vb.astype(BF)
        return 0

    lax.fori_loop(0, 16, pair, 0, unroll=2)
    turn_rows(normed_ref, turned)
    for k, right in enumerate((kback_ref, vback_ref)):
        gradient_rows(plan, turned, right, grads, k)
        start_all(copies[k])
    for k in range(2):
        wait_all(copies[k])


def outer_call(plan, bases, keys, values, ksig, kin, vin, after, segcol, segrow, normed):
    count, d = keys.shape
    outs = piece_shapes(plan, 2, plan.rows // 2 if plan.fast else plan.rows, d, 4)
    low = jax.ShapeDtypeStruct((count, d), BF)
    got = pl.pallas_call(
        functools.partial(outer_body, plan, len(outs)),
        out_shape=outs + [low] * 2,
        in_specs=[SMEM] + [VMEM] * 9,
        out_specs=[ANY] * len(outs) + [VMEM] * 2,
        scratch_shapes=[
            pltpu.VMEM((d, count), BF),
            pltpu.VMEM((plan.nz, 2, plan.span, d), BF),
            pltpu.SemaphoreType.DMA((2, len(outs))),
        ],
        compiler_params=params(24),
        cost_estimate=LIGHT,
        name="key_value_gradients",
    )(bases, keys, values, ksig, kin, vin, after, segcol, segrow, normed)
    return got[: len(outs)], got[len(outs) :]


def entry_body(plan, nb, base_ref, tokens_ref, gain_ref, midback_ref, qb_ref, kb_ref, vb_ref, gb_ref, *refs):
    kv, qg = refs[:nb], refs[nb : 2 * nb]
    out_ref, gains_ref, total, weight, more, sem = refs[2 * nb :]
    d = tokens_ref.shape[1]
    copies = fetch(base_ref, qg, weight, sem.at[0], (0, 1)) + fetch(
        base_ref, kv, more, sem.at[1], (0, 1)
    )
    for c in copies:
        start_all(c)
    slabs = 256 // plan.span
    for c, (back, scr, k) in zip(
        copies, ((qb_ref, weight, 0), (gb_ref, weight, 1), (kb_ref, more, 0), (vb_ref, more, 1))
    ):
        wait_all(c)
        first = back is qb_ref

        def through(j, _, back=back, scr=scr, k=k, first=first):
            rows_w = scr[pl.ds(j * slabs, slabs), k].reshape(256, d)
            value = dot_nt(back[...], rows_w)
            if first:
                total[:, block(j)] = value
            else:
                total[:, block(j)] += value
            return 0

        lax.fori_loop(0, d // 256, through, 0)

    def norm(i, gains):
        rows = block(i, 128)
        dy = total[rows, :]
        v = tokens_ref[rows, :].astype(F32)
        r = inverse_rms(v)
        scaled = dy * gain_ref[...]
        mean = jnp.mean(scaled * v, axis=-1, keepdims=True)
        out_ref[rows, :] = midback_ref[rows, :] + r * scaled - v * (r * r * r * mean)
        return gains + jnp.sum(dy * v * r, axis=0, keepdims=True)

    gains_ref[...] = lax.fori_loop(0, 4, norm, jnp.zeros((1, d), F32))


def entry_call(plan, bases, tokens, gain, midback, qb, kb, vb, gb, kv, qg):
    nb = len(kv)
    count, d = tokens.shape
    return pl.pallas_call(
        functools.partial(entry_body, plan, nb),
        out_shape=[jax.ShapeDtypeStruct((count, d), F32), jax.ShapeDtypeStruct((1, d), F32)],
        in_specs=[SMEM] + [VMEM] * 7 + [ANY] * (2 * nb),
        out_specs=[VMEM] * 2,
        scratch_shapes=[
            pltpu.VMEM((count, d), F32),
            pltpu.VMEM((plan.nz, 2, plan.span, d), BF),
            pltpu.VMEM((plan.nz, 2, plan.span, d), BF),
            pltpu.SemaphoreType.DMA((2, 2, nb)),
        ],
        compiler_params=params(32),
        cost_estimate=LIGHT,
        name="entry_back",
    )(bases, tokens, gain, midback, qb, kb, vb, gb, *kv, *qg)


def blocks(base_ref, pieces, whole, sem, inward):
    d = whole.shape[2]
    copies = []
    for k in range(3):
        copies.append([])
        for b, piece in enumerate(pieces):
            n = piece.shape[0]
            for z in range(n):
                lanes = pl.ds(pl.multiple_of(base_ref[b] + z * (d // n), 128), 128)
                ends = (piece.at[z, k], whole.at[k, :, lanes])
                copies[-1].append(pltpu.make_async_copy(*(ends if inward else ends[::-1]), sem.at[k, b, z]))
    return copies


def ff_body(nb, base_ref, nm0_ref, nm1_ref, up0_ref, up1_ref, *refs):
    pieces = refs[:nb]
    mixed_ref, back_ref, joined_t, left_t, right_t, weight, joined_s, left_s, right_s, sem = refs[nb:]
    count, d = nm0_ref.shape
    hidden = weight.shape[1]
    copies = blocks(base_ref, pieces, weight, sem, True)
    for c in copies:
        start_all(c)
    for c in copies:
        wait_all(c)
    for h, (nm_ref, up_ref) in enumerate(((nm0_ref, up0_ref), (nm1_ref, up1_ref))):
        rows = pl.ds(h * count, count)
        for start in range(0, hidden, 256):
            some = slice(start, min(start + 256, hidden))
            left = dot_nt(nm_ref[...], weight[0, some, :])
            right = dot_nt(nm_ref[...], weight[1, some, :])
            joined_back = dot_nt(up_ref[...], weight[2, some, :])
            for value, straight, turned in (
                (left * right, joined_s, joined_t),
                (joined_back * right, left_s, left_t),
                (joined_back * left, right_s, right_t),
            ):
                value = value.astype(BF)
                straight[rows, some] = value
                turned[some, rows] = value.T

    def through(j, _):
        for h in range(2):
            rows = pl.ds(h * count, count)
            mixed_ref[rows, block(j)] = dot(joined_s[rows, :], weight[2, :, block(j)]).astype(BF)
            back = dot(left_s[rows, :], weight[0, :, block(j)]) + dot(right_s[rows, :], weight[1, :, block(j)])
            back_ref[rows, block(j)] = back.astype(BF)
        return 0

    lax.fori_loop(0, d // 256, through, 0)


def ff_call(bases, nm, up, pieces):
    nb = len(pieces)
    n, three, hidden, _ = pieces[0].shape
    count, d = nm[0].shape
    whole, some = jax.ShapeDtypeStruct((2 * count, d), BF), jax.ShapeDtypeStruct((hidden, 2 * count), BF)
    return pl.pallas_call(
        functools.partial(ff_body, nb),
        out_shape=[whole, whole, some, some, some],
        in_specs=[SMEM] + [VMEM] * 4 + [ANY] * nb,
        out_specs=[VMEM] * 5,
        scratch_shapes=[pltpu.VMEM((three, hidden, d), BF)]
        + [pltpu.VMEM((2 * count, hidden), BF)] * 3
        + [pltpu.SemaphoreType.DMA((3, nb, n))],
        compiler_params=params(40),
        cost_estimate=LIGHT,
        name="feed_forward",
    )(bases, *nm, *up, *pieces)


def ffgrad_body(base_ref, *refs):
    nms, ups = refs[:4], refs[4:8]
    joined, left, right = [refs[8 + k : 14 : 3] for k in range(3)]
    outs, (grads, sem) = refs[14:-2], refs[-2:]
    count, d = nms[0].shape
    copies = blocks(base_ref, outs, grads, sem, False)
    for k, (turned, straight) in enumerate(((left, nms), (right, nms), (joined, ups))):

        def some(j, _, k=k, turned=turned, straight=straight):
            value = None
            for h in range(4):
                part = dot(turned[h // 2][:, pl.ds(h % 2 * count, count)], straight[h][:, block(j)])
                value = part if value is None else value + part
            grads[k, :, block(j)] = value.astype(BF)
            return 0

        lax.fori_loop(0, d // 256, some, 0)
        start_all(copies[k])
    for k in range(3):
        wait_all(copies[k])


def ffgrad_call(bases, nms, ups, first, second, shapes):
    hidden = first[0].shape[0]
    d = nms[0].shape[1]
    return pl.pallas_call(
        ffgrad_body,
        out_shape=[jax.ShapeDtypeStruct(shape, BF) for shape in shapes],
        in_specs=[SMEM] + [VMEM] * 14,
        out_specs=[ANY] * len(shapes),
        scratch_shapes=[
            pltpu.VMEM((3, hidden, d), BF),
            pltpu.SemaphoreType.DMA((3, len(shapes), shapes[0][0])),
        ],
        compiler_params=params(40),
        cost_estimate=LIGHT,
        name="feed_forward_gradients",
    )(bases, *nms, *ups, *first, *second)


def beyond(order, step, size):
    return [(i, i + order * step) for i in range(size) if 0 <= i + order * step < size]


def kept(keep, order, size):
    own, between, steps, step = keep, jnp.ones_like(keep), [], 1
    while step < size:
        steps.append((between, own))
        if step * 2 < size:
            got = lax.ppermute(own, "seq", beyond(order, step, size))
            between, own = between * got, own * got
        step *= 2
    return steps


def chain(own, steps, order, size, beside):
    total, before = own, jnp.zeros_like(own)
    for i, (between, whole) in enumerate(steps):
        sent = tie(total.astype(BF), *beside[i]) if i < len(beside) else total.astype(BF)
        got = lax.ppermute(sent, "seq", beyond(order, 2**i, size)).astype(F32)
        shape = between.shape + (1,) * (own.ndim - 1)
        before = before + between.reshape(shape) * got
        total = total + whole.reshape(shape) * got
    return before


def shards(
    mesh_shape,
    tokens,
    starts,
    entry_gain,
    query_weight,
    key_weight,
    value_weight,
    gate_weight,
    head_gain,
    output_weight,
    middle_gain,
    left_weight,
    right_weight,
    down_weight,
    cotangent,
):
    rows_here, span, width = tokens.shape
    count = rows_here * span
    hidden = left_weight.shape[1]
    plan = Plan(mesh_shape, width)
    seq = plan.seq
    by_x, by_half, by_quarter = plan.bases(()), plan.bases((1,)), plan.bases((2, 1))

    def square(shards, behind):
        near = plan.along(tie(plan.mine(jnp.stack(shards), (2, 1)), *behind), True)
        return near, plan.pair(plan.pair(plan.across(near), 2), 1)

    kv_z, kv = square([key_weight, value_weight], ())
    mine = hidden // 4
    stack = lax.dynamic_slice(
        jnp.stack([left_weight.T, right_weight.T, down_weight]),
        (0, plan.lane * mine, 0),
        (3, mine, plan.rows),
    )
    ff_z = plan.along(stack, False)
    qgo_z, qgo = square([query_weight, gate_weight, output_weight], (kv_z,))
    ff_pieces = plan.across(ff_z)
    if not plan.fast:
        whole = ff_z.transpose(1, 2, 0, 3).reshape(3, mine, width // 128, 128)
        ff_pieces = [whole.transpose(2, 0, 1, 3)]
    upstream = cotangent.reshape(count, width)

    def spread_tokens(own):
        beside, above = swap(own, "batch", 1, plan.batch), swap(own, "batch", 2, plan.batch)
        return [own, beside, above, swap(above, "batch", 1, plan.batch)]

    up_all = spread_tokens(upstream)

    place = jnp.arange(span)
    segment = dot(starts.astype(BF), (place[:, None] <= place[None, :]).astype(BF))
    last = segment[:, span - 1 :]
    keep = (last[:, 0] == 0).astype(F32)
    tail = (segment == last).astype(F32).reshape(count, 1)
    segcol, segrow = segment.reshape(count, 1), segment.reshape(rows_here, 1, span)
    source = tokens.reshape(count, width)
    entry_row, head_row, mid_row = (g.reshape(1, width) for g in (entry_gain, head_gain, middle_gain))

    ahead, behind = kept(keep, 1, seq), kept(keep, -1, seq)

    def scan(own, steps, order, beside):
        own = own.reshape(rows_here, -1, HEAD, 128)
        return chain(own, steps, order, seq, beside).astype(BF).reshape(-1, HEAD, 128)

    early = tie(by_quarter, *(f for pair in ahead + behind for f in pair))
    normed_in, keys, ksig, values, fresh = kv_call(plan, early, source, entry_row, tail, kv)
    state = scan(fresh, ahead, 1, ())
    query, qsig, gate = qg_call(plan, by_quarter, normed_in, qgo)
    attended, gated, middle, normed_mid = attend_call(
        plan, by_quarter, query, keys, values, gate, state, segcol, segrow, head_row, source, mid_row, qgo
    )
    nm_all = spread_tokens(normed_mid)
    mixed_a, back_a, *saved_a = ff_call(by_x, nm_all[:2], up_all[:2], ff_pieces)
    mixed_b, back_b, *saved_b = ff_call(by_x, nm_all[2:], up_all[2:], ff_pieces)

    def collect(mine_a, mine_b):
        other = swap(jnp.stack([mine_a[count:], mine_b[count:]]), "batch", 1, plan.batch)
        return add(mine_a[:count], other[0]), swap(add(mine_b[:count], other[1]), "batch", 2, plan.batch)

    back_own, back_got = collect(back_a, back_b)
    ff_terms = ffgrad_call(by_x, nm_all, up_all, saved_a, saved_b, [p.shape for p in ff_pieces])
    if plan.fast:
        ff_far = swap(ff_terms[1], "seq", 1, seq)
    mixed_own, mixed_got = collect(mixed_a, mixed_b)
    mixed = (middle + (mixed_own.astype(F32) + mixed_got.astype(F32))).astype(BF).reshape(tokens.shape)

    midback, branch, gateback, attback, direct, two_gains = mid_call(
        plan, by_quarter, back_own, back_got, middle, mid_row, upstream, gate, attended, head_row, query, segcol, qgo
    )
    qback, kin, vin = inner_call(plan, query, keys, values, qsig, attback, state, segcol, segrow)
    ogq_terms = grads_call(plan, by_half, [gated, normed_in], (0, 1, 1), [branch, gateback, qback])
    after = scan(direct, behind, -1, ((), (kin,), ogq_terms[:1]))
    kv_terms, (kback, vback) = outer_call(
        plan, by_half, keys, values, ksig, kin, vin, after, segcol, segrow, normed_in
    )

    def from_core(term):
        return [add(mine, swap(other, "batch", 1, 4)) for mine, other in zip(term[:2], term[2:])]

    def finish(part):
        return plan.join(add(part, swap(part, "batch", 2, 4)), 1, 1).astype(F32)

    if plan.fast:
        ff_part = plan.sum_along(add(ff_terms[0], tie(ff_far, kin)))
        ogq_near, ogq_far = from_core(ogq_terms)
        ogq_got = swap(ogq_far, "seq", 1, seq)
        kv_near, kv_far = from_core(kv_terms)
        kv_got = swap(kv_far, "seq", 1, seq)
    else:
        turned = ff_terms[0].transpose(1, 2, 0, 3).reshape(3, mine, seq, plan.rows)
        ff_part = lax.psum_scatter(turned.transpose(2, 0, 1, 3), "seq", scatter_dimension=0)
    input_gradient, entry_term = entry_call(
        plan, tie(by_quarter, kv_far) if plan.fast else by_quarter,
        source, entry_row, midback, qback, kback, vback, gateback, kv, qgo,
    )
    input_gradient = input_gradient.reshape(tokens.shape)
    if plan.fast:
        ogq_part = plan.sum_along(add(ogq_near, ogq_got))
        kv_part = plan.sum_along(add(kv_near, tie(kv_got, entry_term)))
        wide = plan.join(plan.join(tie(ff_part, kv_part), 1, 1), 2, 1).astype(F32)
        output_total, gate_total, query_total = finish(ogq_part)
        key_total, value_total = finish(kv_part)
    else:
        wide = plan.join(plan.join(ff_part, 1, 1), 2, 1).astype(F32)
        output_total, gate_total, query_total, key_total, value_total = (
            total
            for term in (ogq_terms, kv_terms)
            for total in lax.psum(lax.psum_scatter(term[0], "seq", scatter_dimension=0), "batch").astype(F32)
        )
    left_total, right_total, down_total = wide[0].T, wide[1].T, wide[2]
    gains = jnp.concatenate([two_gains, entry_term])
    if plan.fast:
        for axis, size in (("batch", plan.batch), ("seq", seq)):
            step = 1
            while step < size:
                gains = gains + swap(gains, axis, step, size)
                step *= 2
    else:
        gains = lax.psum(gains, ("seq", "batch"))
    gains = lax.dynamic_slice(gains, (0, plan.place * plan.rows), (3, plan.rows))
    return (
        mixed,
        input_gradient,
        gains[2],
        query_total,
        key_total,
        value_total,
        gate_total,
        gains[1],
        output_total,
        gains[0],
        left_total,
        right_total,
        down_total,
    )


def solution(mesh):
    row, cut, wide = P("batch", "seq", None), P("seq", None), P(None, "seq")
    in_specs = (row, P("batch", "seq"), P(), cut, cut, cut, cut, P(), cut, P(), cut, cut, wide, row)
    out_specs = (row, row, P("seq"), cut, cut, cut, cut, P("seq"), cut, P("seq"), cut, cut, wide)
    return jax.shard_map(
        functools.partial(shards, dict(mesh.shape)),
        mesh=mesh,
        in_specs=in_specs,
        out_specs=out_specs,
        check_vma=False,
    )
```

time: 1990 us -> 539 us (0.27)
  waiting for transfers between devices: 1600 us -> 241 us
  matrix products: 161 us -> 0.15 us
  Pallas kernels: 0 us -> 121 us
  starting transfers between devices: 1.3 us -> 64 us
  blocking collectives: 60.4 us -> 0 us
  other arithmetic: 68 us -> 37.4 us
  local copies, waits for them, and re-layouts: 82.6 us -> 53.8 us
    reduce_scatter x8 -> x3, waiting for transfers between devices: 914 us -> 0.04 us  [sum_along(): lax.psum_scatter(near, 'seq', scatter_dimension=0, axis_index_groups=self...]
    all_gather x10 -> x1, waiting for transfers between devices: 658 us -> 0.01 us  [along(): return lax.all_gather(mine, 'seq', axis=0, axis_index_groups=self.groups)]
    ppermute x0 -> x53, waiting for transfers between devices: none -> 216 us  [the longest x43 155 us: swap(): return lax.ppermute(value, axis, [(i, i ^ bit) for i in range(size)])]
    dot_general x44 -> x1, matrix products: 161 us -> 0.15 us  [dot(): return jnp.dot(left, right, preferred_element_type=F32)]
    pallas_call x0 -> x11, Pallas kernels: none -> 121 us  [the longest x2 29.6 us: ff_call(): pl.pallas_call(functools.partial(ff_body, nb), out_shape=[whole, whole, s...]
    unnamed x2 -> x0, blocking collectives: 54.3 us -> none
    ppermute x0 -> x53, starting transfers between devices: none -> 53.6 us  [the longest x43 24 us: swap(): return lax.ppermute(value, axis, [(i, i ^ bit) for i in range(size)])]
    reshape x12 -> x1, local copies, waits for them, and re-layouts: 35.5 us -> 0.01 us  [shards(): segment.reshape(rows_here, 1, span)]
  transfers between devices with their start and end apart: 19 -> 59, of which waited for: 18 -> 24; matrix products, arithmetic and copies ran while one was open for 11% -> 7% of each run, Pallas kernels for 0% -> 20%
where the time goes in v2:
time: 539 us; the launch traced here: 533 us
  waiting for transfers between devices  241 us (45%)
  Pallas kernels  121 us (22%)
  starting transfers between devices  64 us (12%)
  local copies, waits for them, and re-layouts  53.8 us (10%)
  other arithmetic  37.4 us (7%)
  between operations  15.2 us (3%)
    ppermute x43, waiting for transfers between devices, swap(): return lax.ppermute(value, axis, [(i, i ^ bit) for i in range(size)])  155 us
    ppermute x6, waiting for transfers between devices, chain(): got = lax.ppermute(sent, 'seq', beyond(order, 2 ** i, size)).astype(F32)  56.4 us
    unnamed x192, local copies, waits for them, and re-layouts  45.8 us
    pallas_call x2, Pallas kernels, ff_call(): pl.pallas_call(functools.partial(ff_body, nb), out_shape=[whole, whole, s...  29.6 us
    all_to_all x2, waiting for transfers between devices, along(): return lax.all_to_all(copies, 'seq', 0, 0, axis_index_groups=self.groups)  25.1 us
    ppermute x43, starting transfers between devices, swap(): return lax.ppermute(value, axis, [(i, i ^ bit) for i in range(size)])  24 us
    ppermute x6, starting transfers between devices, chain(): got = lax.ppermute(sent, 'seq', beyond(order, 2 ** i, size)).astype(F32)  20.3 us
    convert_element_type x9, other arithmetic, add(): return (left.astype(F32) + right.astype(F32)).astype(BF)  17 us
  transfers between devices with their start and end apart: 59, of which 24 were waited for; matrix products, arithmetic and copies ran while one was open for 7% of the time, Pallas kernels for 20%

profile of v2, /device:TPU:0, one launch (start us, length us, event | category | flops | bytes accessed | tf_op | source)
XLA Modules:
  0.0 532.7 jit_solution(7082897006000412563)
XLA Ops:
  9.2 6.4 %all-to-all-start = ((bf16[4,2,32,1024]{3,2,1,0:T(8,128)(2,1)}), bf16[4,2,32,1024]{3,2,1,0:T(8,128)(2,1)S(1)}, u32[]{:S(2)}, u32[]{:S(2)}) async-start(bf16[4,2,32,1024]{3,2,1,0:T(8,128)(2,1)} %broadcast_in_dim.4), calls=%async_computation | async-start | bytes 1048576 | tf_op jit(solution)/shard_map/all_to_all | solution.py:85
  15.7 14.4 %all-to-all-done.refs_0_ = bf16[4,2,32,1024]{3,2,1,0:T(8,128)(2,1)S(1)} async-done(((bf16[4,2,32,1024]{3,2,1,0:T(8,128)(2,1)}), bf16[4,2,32,1024]{3,2,1,0:T(8,128)(2,1)S(1)}, u32[]{:S(2)}, u32[]{:S(2)}) %all-to-all-start) | async-done | bytes 524320 | tf_op jit(solution)/shard_map/all_to_all | solution.py:85
  31.1 3.5 all-to-all-start.1
  35.4 1.8 fusion.5
  37.3 1.6 collective-permute-start.4
  40.7 9.6 %collective-permute-done.4.refs_1_ = bf16[4,2,32,1024]{3,2,1,0:T(8,128)(2,1)} collective-permute-done((bf16[4,2,32,1024]{3,2,1,0:T(8,128)(2,1)S(1)}, bf16[4,2,32,1024]{3,2,1,0:T(8,128)(2,1)}, u32[]{:S(2)}, u32[]{:S(2)}) %collective-permute-start.4) | collective-permute-done | bytes 524320 | tf_op jit(solution)/shard_map/ppermute | solution.py:39
  51.8 3.4 collective-permute-start
  56.5 10.7 %all-to-all-done.1.refs_0_.refs_8_ = bf16[4,3,32,1024]{3,2,1,0:T(8,128)(2,1)S(1)} async-done(((bf16[4,3,32,1024]{3,2,1,0:T(8,128)(2,1)}), bf16[4,3,32,1024]{3,2,1,0:T(8,128)(2,1)S(1)}, u32[]{:S(2)}, u32[]{:S(2)}) %all-to-all-start.1) | async-done | bytes 786464 | tf_op jit(solution)/shard_map/all_to_all | solution.py:85
  68.8 3.3 collective-permute-start.1
  73.5 4.1 collective-permute-done.3
  84.7 8.9 %keys_values.1 = (bf16[512,1024]{1,0:T(8,128)(2,1)S(1)}, bf16[512,1024]{1,0:T(8,128)(2,1)S(1)}, bf16[512,1024]{1,0:T(8,128)(2,1)S(1)}, bf16[512,1024]{1,0:T(8,128)(2,1)S(1)}, f32[16,64,128]{2,1,0:T(8,128)S(1)}) custom-call(s32[8]{0:T(128)S(1)} %pad_add_fusion.2.base_ref, bf16[512,1024]{1,0:T(8,128)(2,1)S(1)} %bitcast.101, f32[1,1024]{1,0:T(1,128)S(1)} %bitcast.122, ...), custom_call_target="tpu_custom_call" | custom-call | flops 1 | bytes 1 | tf_op jit(solution)/shard_map/keys_values/pallas_call | solution.py:233
  95.6 3.1 collective-permute-start.18
  98.7 5.7 %collective-permute-done.18 = bf16[2,8,64,128]{3,2,1,0:T(8,128)(2,1)S(1)} collective-permute-done((bf16[2,8,64,128]{3,2,1,0:T(8,128)(2,1)S(1)}, bf16[2,8,64,128]{3,2,1,0:T(8,128)(2,1)S(1)}, u32[]{:S(2)}, u32[]{:S(2)}) %collective-permute-start.18) | collective-permute-done | bytes 262176 | tf_op jit(solution)/shard_map/ppermute | solution.py:796
  104.6 6.4 %collective-permute-start.19 = (bf16[2,8,64,128]{3,2,1,0:T(8,128)(2,1)S(1)}, bf16[2,8,64,128]{3,2,1,0:T(8,128)(2,1)S(1)}, u32[]{:S(2)}, u32[]{:S(2)}) collective-permute-start(bf16[2,8,64,128]{3,2,1,0:T(8,128)(2,1)S(1)} %fusion.17), channel_id=1, source_target_pairs={{0,8},{4,12},{8,16},{12,20},{16,24},{20,28},{1,9},{5,13},{9,17},{1... | collective-permute-start | bytes 786440 | tf_op jit(solution)/shard_map/ppermute | solution.py:796
  111.6 4.2 collective-permute-done.13.refs_3_.refs_11_
  116.0 7.0 %collective-permute-start.20 = (bf16[2,8,64,128]{3,2,1,0:T(8,128)(2,1)S(1)}, bf16[2,8,64,128]{3,2,1,0:T(8,128)(2,1)}, u32[]{:S(2)}, u32[]{:S(2)}) collective-permute-start(bf16[2,8,64,128]{3,2,1,0:T(8,128)(2,1)S(1)} %fusion.10), channel_id=1, source_target_pairs={{0,16},{4,20},{8,24},{12,28},{1,17},{5,21},{9,25},{13,29},{2,18},{... | collective-permute-start | bytes 786440 | tf_op jit(solution)/shard_map/ppermute | solution.py:796
  123.1 4.8 collective-permute-done.20
  132.7 6.9 %query_gate.1 = (bf16[512,1024]{1,0:T(8,128)(2,1)S(1)}, bf16[512,1024]{1,0:T(8,128)(2,1)S(1)}, f32[512,1024]{1,0:T(8,128)S(1)}) custom-call(s32[8]{0:T(128)S(1)} %pad_add_fusion.2.base_ref, bf16[512,1024]{1,0:T(8,128)(2,1)S(1)} %copy-done.11, bf16[4,3,32,1024]{3,2,1,0:T(8,128)(2,1)S(1)} %all-to-all-done.1.refs_0_.refs_8_, ...), custom_call_target="tpu_custom_call" | custom-call | flops 1 | bytes 1 | tf_op jit(solution)/shard_map/query_gate/pallas_call | solution.py:279
  140.6 10.4 %attend.1 = (f32[512,1024]{1,0:T(8,128)S(1)}, bf16[512,1024]{1,0:T(8,128)(2,1)S(1)}, f32[512,1024]{1,0:T(8,128)S(1)}, bf16[512,1024]{1,0:T(8,128)(2,1)S(1)}) custom-call(s32[8]{0:T(128)S(1)} %pad_add_fusion.2.base_ref, bf16[512,1024]{1,0:T(8,128)(2,1)S(1)} %get-tuple-element.69.query_ref, bf16[512,1024]{1,0:T(8,128)(2,1)S(1)} %copy-done.5, ...), custom_call_target="tpu_custom_call" | custom-call | flops 1 | bytes 1 | tf_op jit(solution)/shard_map/attend/pallas_call | solution.py:353
  155.7 22.0 %collective-permute-done.24.nm0_ref.refs_2_ = bf16[512,1024]{1,0:T(8,128)(2,1)} collective-permute-done((bf16[512,1024]{1,0:T(8,128)(2,1)S(1)}, bf16[512,1024]{1,0:T(8,128)(2,1)}, u32[]{:S(2)}, u32[]{:S(2)}) %collective-permute-start.24) | collective-permute-done | bytes 1048608 | tf_op jit(solution)/shard_map/ppermute | solution.py:39
  183.3 14.2 %feed_forward.2 = (bf16[1024,1024]{1,0:T(8,128)(2,1)S(1)}, bf16[1024,1024]{1,0:T(8,128)(2,1)S(1)}, bf16[704,1024]{1,0:T(8,128)(2,1)S(1)}, bf16[704,1024]{1,0:T(8,128)(2,1)S(1)}, bf16[704,1024]{1,0:T(8,128)(2,1)S(1)}) custom-call(s32[2]{0:T(128)S(1)} %get-tuple-element.159.base_ref, bf16[512,1024]{1,0:T(8,128)(2,1)S(1)} %copy-done.24, ...), custom_call_target="tpu_custom_call" | custom-call | flops 1 | bytes 1 | tf_op jit(solution)/shard_map/feed_forward/pallas_call | solution.py:723
  204.2 15.4 %feed_forward.3 = (bf16[1024,1024]{1,0:T(8,128)(2,1)S(1)}, bf16[1024,1024]{1,0:T(8,128)(2,1)S(1)}, bf16[704,1024]{1,0:T(8,128)(2,1)S(1)}, bf16[704,1024]{1,0:T(8,128)(2,1)S(1)}, bf16[704,1024]{1,0:T(8,128)(2,1)S(1)}) custom-call(s32[2]{0:T(128)S(1)} %get-tuple-element.159.base_ref, bf16[512,1024]{1,0:T(8,128)(2,1)} %collective-permute-done.24.nm0_ref.refs_2_, ...), custom_call_target="tpu_custom_call" | custom-call | flops 1 | bytes 1 | tf_op jit(solution)/shard_map/feed_forward/pallas_call | solution.py:723
  223.2 3.4 pad_maximum_fusion.1
  231.4 15.3 %feed_forward_gradients.1 = (bf16[4,3,704,128]{3,2,1,0:T(8,128)(2,1)}, bf16[4,3,704,128]{3,2,1,0:T(8,128)(2,1)}) custom-call(s32[2]{0:T(128)S(1)} %get-tuple-element.159.base_ref, bf16[512,1024]{1,0:T(8,128)(2,1)S(1)} %copy-done.25, bf16[512,1024]{1,0:T(8,128)(2,1)S(1)} %copy-done.31, bf16[512,1024]{1,0:T(8,128)(2,1)} %collective-permute-done.24.nm0_ref.refs_2_, ...), custom_call_target="tpu_custom_call" | custom-call | flops 1 | bytes 1 | tf_op jit(solution)/shard_map/feed_forward_gradients/pallas_call | solution.py:762
  248.0 3.2 fusion
  252.3 24.2 %collective-permute-done.31.got_ref = bf16[512,1024]{1,0:T(8,128)(2,1)S(1)} collective-permute-done((bf16[512,1024]{1,0:T(8,128)(2,1)S(1)}, bf16[512,1024]{1,0:T(8,128)(2,1)S(1)}, u32[]{:S(2)}, u32[]{:S(2)}) %collective-permute-start.31) | collective-permute-done | bytes 1048608 | tf_op jit(solution)/shard_map/ppermute | solution.py:39
  276.5 10.6 %middle_back.1 = (f32[512,1024]{1,0:T(8,128)S(1)}, bf16[512,1024]{1,0:T(8,128)(2,1)S(1)}, bf16[512,1024]{1,0:T(8,128)(2,1)S(1)}, bf16[512,1024]{1,0:T(8,128)(2,1...) custom-call(s32[8]{0:T(128)S(1)} %pad_add_fusion.2.base_ref, ...), custom_call_target="tpu_custom_call" | custom-call | flops 1 | bytes 1 | tf_op jit(solution)/shard_map/middle_back/pallas_call | solution.py:433
  287.2 12.2 %attend_back.1 = (bf16[512,1024]{1,0:T(8,128)(2,1)S(1)}, f32[512,1024]{1,0:T(8,128)S(1)}, f32[512,1024]{1,0:T(8,128)S(1)}) custom-call(bf16[512,1024]{1,0:T(8,128)(2,1)S(1)} %get-tuple-element.69.query_ref, bf16[512,1024]{1,0:T(8,128)(2,1)S(1)} %copy-done.5, bf16[512,1024]{1,0:T(8,128)(2,1)S(1)} %copy-done.8, bf16[512,1024]{1,0:T(8,128)(2,1)S(1)} %copy-done.74, ...), custom_call_target="tpu_custom_call" | custom-call | flops 1 | bytes 1 | tf_op jit(solution)/shard_map/attend_back/pallas_call | solution.py:546
  303.1 2.0 add_convert_fusion
  307.6 8.2 %collective-permute-done.32 = bf16[2,8,64,128]{3,2,1,0:T(8,128)(2,1)S(1)} collective-permute-done((bf16[2,8,64,128]{3,2,1,0:T(8,128)(2,1)S(1)}, bf16[2,8,64,128]{3,2,1,0:T(8,128)(2,1)S(1)}, u32[]{:S(2)}, u32[]{:S(2)}) %collective-permute-start.32) | collective-permute-done | bytes 262176 | tf_op jit(solution)/shard_map/ppermute | solution.py:796
  323.3 8.0 %square_gradients.1 = (bf16[4,3,64,1024]{3,2,1,0:T(8,128)(2,1)S(1)}, bf16[4,3,64,1024]{3,2,1,0:T(8,128)(2,1)S(1)}, bf16[4,3,64,1024]{3,2,1,0:T(8,128)(2,1)}, bf16[4,3,64,1024]{3,2,1,0:T(8,128)(2,1)S(1)}) custom-call(s32[4]{0:T(128)S(1)} %pad_add_fusion.3.base_ref, bf16[512,1024]{1,0:T(8,128)(2,1)S(1)} %copy-done.72, bf16[512,1024]{1,0:T(8,128)(2,1)S(1)} %copy-done.12, ...), custom_call_target="tpu_custom_call" | custom-call | flops 1 | bytes 1 | tf_op jit(solution)/shard_map/square_gradients/pallas_call | solution.py:492
  332.6 9.2 %collective-permute-done.33 = bf16[2,8,64,128]{3,2,1,0:T(8,128)(2,1)S(1)} collective-permute-done((bf16[2,8,64,128]{3,2,1,0:T(8,128)(2,1)S(1)}, bf16[2,8,64,128]{3,2,1,0:T(8,128)(2,1)S(1)}, u32[]{:S(2)}, u32[]{:S(2)}) %collective-permute-start.33) | collective-permute-done | bytes 262176 | tf_op jit(solution)/shard_map/ppermute | solution.py:796
  343.3 28.5 %collective-permute-done.34 = bf16[2,8,64,128]{3,2,1,0:T(8,128)(2,1)S(1)} collective-permute-done((bf16[2,8,64,128]{3,2,1,0:T(8,128)(2,1)S(1)}, bf16[2,8,64,128]{3,2,1,0:T(8,128)(2,1)S(1)}, u32[]{:S(2)}, u32[]{:S(2)}) %collective-permute-start.34) | collective-permute-done | bytes 262176 | tf_op jit(solution)/shard_map/ppermute | solution.py:796
  373.2 7.1 %key_value_gradients.1 = (bf16[4,2,64,1024]{3,2,1,0:T(8,128)(2,1)S(1)}, bf16[4,2,64,1024]{3,2,1,0:T(8,128)(2,1)S(1)}, bf16[4,2,64,1024]{3,2,1,0:T(8,128)(2,1)S(1...) custom-call(s32[4]{0:T(128)S(1)} %pad_add_fusion.3.base_ref, ...), custom_call_target="tpu_custom_call" | custom-call | flops 1 | bytes 1 | tf_op jit(solution)/shard_map/key_value_gradients/pallas_call | solution.py:590
  380.9 2.1 collective-permute-done.35
  385.3 1.9 add_convert_fusion.2
  388.1 12.1 %entry_back.1 = (f32[512,1024]{1,0:T(8,128)}, f32[1,1024]{1,0:T(1,128)S(1)}) custom-call(s32[8]{0:T(128)S(1)} %pad_add_fusion.2.base_ref, bf16[512,1024]{1,0:T(8,128)(2,1)S(1)} %bitcast.103, f32[1,1024]{1,0:T(1,128)S(1)} %bitcast.123, f32[512,1024]{1,0:T(8,128)S(1)} %copy-done.41, bf16[512,1024]{1,0:T(8,128)(2,1)S(1)} %copy-done.37, ...), custom_call_target="tpu_custom_call" | custom-call | flops 1 | bytes 1 | tf_op jit(solution)/shard_map/entry_back/pallas_call | solution.py:650
  400.2 9.3 %collective-permute-done.47 = bf16[4,2,64,1024]{3,2,1,0:T(8,128)(2,1)S(1)} collective-permute-done((bf16[4,2,64,1024]{3,2,1,0:T(8,128)(2,1)S(1)}, bf16[4,2,64,1024]{3,2,1,0:T(8,128)(2,1)S(1)}, u32[]{:S(2)}, u32[]{:S(2)}) %collective-permute-start.47) | collective-permute-done | bytes 1048608 | tf_op jit(solution)/shard_map/ppermute | solution.py:39
  409.5 1.6 add_convert_fusion.4
  414.5 28.1 %collective-permute-done.43 = bf16[4,3,64,1024]{3,2,1,0:T(8,128)(2,1)} collective-permute-done((bf16[4,3,64,1024]{3,2,1,0:T(8,128)(2,1)}, bf16[4,3,64,1024]{3,2,1,0:T(8,128)(2,1)}, u32[]{:S(2)}, u32[]{:S(2)}) %collective-permute-start.43) | collective-permute-done | bytes 1572896 | tf_op jit(solution)/shard_map/ppermute | solution.py:39
  442.5 4.1 add_convert_fusion.1
  446.8 2.6 fusion.2
  452.8 22.7 %collective-permute-done.37 = f32[3,1024]{1,0:T(4,128)S(1)} collective-permute-done((f32[3,1024]{1,0:T(4,128)S(1)}, f32[3,1024]{1,0:T(4,128)S(1)}, u32[]{:S(2)}, u32[]{:S(2)}) %collective-permute-start.37) | collective-permute-done | bytes 12320 | tf_op jit(solution)/shard_map/ppermute | solution.py:39
  475.8 3.5 collective-permute-done.38
  482.9 3.3 add_convert_fusion.7
  486.3 2.6 collective-permute-done.48
  493.7 18.4 %collective-permute-done.52 = bf16[3,1408,128]{2,1,0:T(8,128)(2,1)S(1)} collective-permute-done((bf16[3,1408,128]{2,1,0:T(8,128)(2,1)S(1)}, bf16[3,1408,128]{2,1,0:T(8,128)(2,1)S(1)}, u32[]{:S(2)}, u32[]{:S(2)}) %collective-permute-start.52) | collective-permute-done | bytes 1081376 | tf_op jit(solution)/shard_map/ppermute | solution.py:39
  512.8 5.6 %collective-permute-done.44 = bf16[3,64,1024]{2,1,0:T(8,128)(2,1)S(1)} collective-permute-done((bf16[3,64,1024]{2,1,0:T(8,128)(2,1)}, bf16[3,64,1024]{2,1,0:T(8,128)(2,1)S(1)}, u32[]{:S(2)}, u32[]{:S(2)}) %collective-permute-start.44) | collective-permute-done | bytes 393248 | tf_op jit(solution)/shard_map/ppermute | solution.py:39
  (335 shorter events, 100.0 us)
Async XLA Ops:
  9.2 20.9 %all-to-all-start = ((bf16[4,2,32,1024]{3,2,1,0:T(8,128)(2,1)}), bf16[4,2,32,1024]{3,2,1,0:T(8,128)(2,1)S(1)}, u32[]{:S(2)}, u32[]{:S(2)}) async-start(bf16[4,2,32,1024]{3,2,1,0:T(8,128)(2,1)} %broadcast_in_dim.4), calls=%async_computation | async-start | bytes 1048576 | tf_op jit(solution)/shard_map/all_to_all | solution.py:85
  31.1 36.1 %all-to-all-start.1 = ((bf16[4,3,32,1024]{3,2,1,0:T(8,128)(2,1)}), bf16[4,3,32,1024]{3,2,1,0:T(8,128)(2,1)S(1)}, u32[]{:S(2)}, u32[]{:S(2)}) async-start(bf16[4,3,32,1024]{3,2,1,0:T(8,128)(2,1)} %broadcast_in_dim.5), calls=%async_computation.1 | async-start | bytes 1572864 | tf_op jit(solution)/shard_map/all_to_all | solution.py:85
  34.6 93.2 %all-gather.3.cloned.1.call-start = ((), (), s32[]{:S(2)}) async-start(), calls=%async_computation.8 | async-start | bytes 2703360 | tf_op jit(solution)/shard_map/all_gather | solution.py:86
  37.2 409.5 %reduce-scatter.8.cloned.1.call-start = ((), (), s32[]{:S(2)}) async-start(), calls=%async_computation.7 | async-start | bytes 2703360 | tf_op jit(solution)/shard_map/reduce_scatter | solution.py:95
  37.3 13.1 %collective-permute-start.4 = (bf16[4,2,32,1024]{3,2,1,0:T(8,128)(2,1)S(1)}, bf16[4,2,32,1024]{3,2,1,0:T(8,128)(2,1)}, u32[]{:S(2)}, u32[]{:S(2)}) collective-permute-start(bf16[4,2,32,1024]{3,2,1,0:T(8,128)(2,1)S(1)} %all-to-all-done.refs_0_), channel_id=1, source_target_pairs={{0,4},{4,0},{8,12},{12,8},{16,20},{20,16},{24,28},{28,24},{1,5},{5... | collective-permute-start | bytes 1572872 | tf_op jit(solution)/shard_map/ppermute | solution.py:39
  39.2 38.4 %collective-permute-start.5 = (bf16[4,2,32,1024]{3,2,1,0:T(8,128)(2,1)S(1)}, bf16[4,2,32,1024]{3,2,1,0:T(8,128)(2,1)}, u32[]{:S(2)}, u32[]{:S(2)}) collective-permute-start(bf16[4,2,32,1024]{3,2,1,0:T(8,128)(2,1)S(1)} %all-to-all-done.refs_0_), channel_id=1, source_target_pairs={{0,2},{1,3},{2,0},{3,1},{4,6},{5,7},{6,4},{7,5},{8,10},{9,11},{10,... | collective-permute-start | bytes 1572872 | tf_op jit(solution)/shard_map/ppermute | solution.py:39
  50.3 27.7 %collective-permute-start.6 = (bf16[4,2,32,1024]{3,2,1,0:T(8,128)(2,1)}, bf16[4,2,32,1024]{3,2,1,0:T(8,128)(2,1)}, u32[]{:S(2)}, u32[]{:S(2)}) collective-permute-start(bf16[4,2,32,1024]{3,2,1,0:T(8,128)(2,1)} %collective-permute-done.4.refs_1_), channel_id=1, source_target_pairs={{0,2},{1,3},{2,0},{3,1},{4,6},{5,7},{6,4},{7,5},{8,10},{9,11},{10,... | collective-permute-start | bytes 1572872 | tf_op jit(solution)/shard_map/ppermute | solution.py:39
  51.8 17.0 %collective-permute-start = (f32[2]{0:T(128)S(1)}, f32[2]{0:T(128)S(1)}, u32[]{:S(2)}, u32[]{:S(2)}) collective-permute-start(f32[2]{0:T(128)S(1)} %fusion.25), channel_id=1, source_target_pairs={{0,4},{4,8},{8,12},{12,16},{16,20},{20,24},{24,28},{1,5},{5,9},{9,... | collective-permute-start | bytes 32 | tf_op jit(solution)/shard_map/ppermute | solution.py:786
  55.2 13.6 %collective-permute-start.2 = (f32[2]{0:T(128)S(1)}, f32[2]{0:T(128)S(1)}, u32[]{:S(2)}, u32[]{:S(2)}) collective-permute-start(f32[2]{0:T(128)S(1)} %fusion.25), channel_id=1, source_target_pairs={{4,0},{8,4},{12,8},{16,12},{20,16},{24,20},{28,24},{5,1},{9,5},{13... | collective-permute-start | bytes 32 | tf_op jit(solution)/shard_map/ppermute | solution.py:786
  67.2 13.3 %collective-permute-start.11 = (bf16[4,3,32,1024]{3,2,1,0:T(8,128)(2,1)S(1)}, bf16[4,3,32,1024]{3,2,1,0:T(8,128)(2,1)S(1)}, u32[]{:S(2)}, u32[]{:S(2)}) collective-permute-start(bf16[4,3,32,1024]{3,2,1,0:T(8,128)(2,1)S(1)} %all-to-all-done.1.refs_0_.refs_8_), channel_id=1, source_target_pairs={{0,4},{4,0},{8,12},{12,8},{16,20},{20,16},{24,28},{28,24},{1,5},{5... | collective-permute-start | bytes 2359304 | tf_op jit(solution)/shard_map/ppermute | solution.py:39
  72.1 5.5 %collective-permute-start.3 = (f32[2]{0:T(128)S(1)}, f32[2]{0:T(128)S(1)}, u32[]{:S(2)}, u32[]{:S(2)}) collective-permute-start(f32[2]{0:T(128)S(1)} %get-tuple-element.186), channel_id=1, source_target_pairs={{8,0},{12,4},{16,8},{20,12},{24,16},{28,20},{9,1},{13,5},{17,9},{2... | collective-permute-start | bytes 32 | tf_op jit(solution)/shard_map/ppermute | solution.py:786
  79.1 32.5 %collective-permute-start.12 = (bf16[4,3,32,1024]{3,2,1,0:T(8,128)(2,1)S(1)}, bf16[4,3,32,1024]{3,2,1,0:T(8,128)(2,1)S(1)}, u32[]{:S(2)}, u32[]{:S(2)}) collective-permute-start(bf16[4,3,32,1024]{3,2,1,0:T(8,128)(2,1)S(1)} %all-to-all-done.1.refs_0_.refs_8_), channel_id=1, source_target_pairs={{0,2},{1,3},{2,0},{3,1},{4,6},{5,7},{6,4},{7,5},{8,10},{9,11},{10,... | collective-permute-start | bytes 2359304 | tf_op jit(solution)/shard_map/ppermute | solution.py:39
  80.5 35.3 %collective-permute-start.13 = (bf16[4,3,32,1024]{3,2,1,0:T(8,128)(2,1)S(1)}, bf16[4,3,32,1024]{3,2,1,0:T(8,128)(2,1)S(1)}, u32[]{:S(2)}, u32[]{:S(2)}) collective-permute-start(bf16[4,3,32,1024]{3,2,1,0:T(8,128)(2,1)S(1)} %collective-permute-done.11.refs_1_.refs_9_), channel_id=1, source_target_pairs={{0,2},{1,3},{2,0},{3,1},{4,6},{5,7},{6,4},{7,5},{8,10},{9,11},{10,... | collective-permute-start | bytes 2359304 | tf_op jit(solution)/shard_map/ppermute | solution.py:39
  95.6 8.8 %collective-permute-start.18 = (bf16[2,8,64,128]{3,2,1,0:T(8,128)(2,1)S(1)}, bf16[2,8,64,128]{3,2,1,0:T(8,128)(2,1)S(1)}, u32[]{:S(2)}, u32[]{:S(2)}) collective-permute-start(bf16[2,8,64,128]{3,2,1,0:T(8,128)(2,1)S(1)} %convert_element_type.203), channel_id=1, source_target_pairs={{0,4},{4,8},{8,12},{12,16},{16,20},{20,24},{24,28},{1,5},{5,9},{9,... | collective-permute-start | bytes 786440 | tf_op jit(solution)/shard_map/ppermute | solution.py:796
  104.6 11.2 %collective-permute-start.19 = (bf16[2,8,64,128]{3,2,1,0:T(8,128)(2,1)S(1)}, bf16[2,8,64,128]{3,2,1,0:T(8,128)(2,1)S(1)}, u32[]{:S(2)}, u32[]{:S(2)}) collective-permute-start(bf16[2,8,64,128]{3,2,1,0:T(8,128)(2,1)S(1)} %fusion.17), channel_id=1, source_target_pairs={{0,8},{4,12},{8,16},{12,20},{16,24},{20,28},{1,9},{5,13},{9,17},{1... | collective-permute-start | bytes 786440 | tf_op jit(solution)/shard_map/ppermute | solution.py:796
  111.0 19.2 %collective-permute-start.14 = (bf16[4,3,32,1024]{3,2,1,0:T(8,128)(2,1)S(1)}, bf16[4,3,32,1024]{3,2,1,0:T(8,128)(2,1)}, u32[]{:S(2)}, u32[]{:S(2)}) collective-permute-start(bf16[4,3,32,1024]{3,2,1,0:T(8,128)(2,1)S(1)} %all-to-all-done.1.refs_0_.refs_8_), channel_id=1, source_target_pairs={{0,1},{1,0},{2,3},{3,2},{4,5},{5,4},{6,7},{7,6},{8,9},{9,8},{10,11... | collective-permute-start | bytes 2359304 | tf_op jit(solution)/shard_map/ppermute | solution.py:39
  111.0 20.4 %collective-permute-start.15 = (bf16[4,3,32,1024]{3,2,1,0:T(8,128)(2,1)S(1)}, bf16[4,3,32,1024]{3,2,1,0:T(8,128)(2,1)}, u32[]{:S(2)}, u32[]{:S(2)}) collective-permute-start(bf16[4,3,32,1024]{3,2,1,0:T(8,128)(2,1)S(1)} %collective-permute-done.11.refs_1_.refs_9_), channel_id=1, source_target_pairs={{0,1},{1,0},{2,3},{3,2},{4,5},{5,4},{6,7},{7,6},{8,9},{9,8},{10,11... | collective-permute-start | bytes 2359304 | tf_op jit(solution)/shard_map/ppermute | solution.py:39
  111.5 19.9 %collective-permute-start.16 = (bf16[4,3,32,1024]{3,2,1,0:T(8,128)(2,1)S(1)}, bf16[4,3,32,1024]{3,2,1,0:T(8,128)(2,1)}, u32[]{:S(2)}, u32[]{:S(2)}) collective-permute-start(bf16[4,3,32,1024]{3,2,1,0:T(8,128)(2,1)S(1)} %collective-permute-done.12.refs_2_.refs_10_), channel_id=1, source_target_pairs={{0,1},{1,0},{2,3},{3,2},{4,5},{5,4},{6,7},{7,6},{8,9},{9,8},{10,11... | collective-permute-start | bytes 2359304 | tf_op jit(solution)/shard_map/ppermute | solution.py:39
  115.8 15.6 %collective-permute-start.17 = (bf16[4,3,32,1024]{3,2,1,0:T(8,128)(2,1)S(1)}, bf16[4,3,32,1024]{3,2,1,0:T(8,128)(2,1)}, u32[]{:S(2)}, u32[]{:S(2)}) collective-permute-start(bf16[4,3,32,1024]{3,2,1,0:T(8,128)(2,1)S(1)} %collective-permute-done.13.refs_3_.refs_11_), channel_id=1, source_target_pairs={{0,1},{1,0},{2,3},{3,2},{4,5},{5,4},{6,7},{7,6},{8,9},{9,8},{10,11... | collective-permute-start | bytes 2359304 | tf_op jit(solution)/shard_map/ppermute | solution.py:39
  116.0 11.8 %collective-permute-start.20 = (bf16[2,8,64,128]{3,2,1,0:T(8,128)(2,1)S(1)}, bf16[2,8,64,128]{3,2,1,0:T(8,128)(2,1)}, u32[]{:S(2)}, u32[]{:S(2)}) collective-permute-start(bf16[2,8,64,128]{3,2,1,0:T(8,128)(2,1)S(1)} %fusion.10), channel_id=1, source_target_pairs={{0,16},{4,20},{8,24},{12,28},{1,17},{5,21},{9,25},{13,29},{2,18},{... | collective-permute-start | bytes 786440 | tf_op jit(solution)/shard_map/ppermute | solution.py:796
  127.9 51.7 %collective-permute-start.23 = (bf16[4,3,704,128]{3,2,1,0:T(8,128)(2,1)}, bf16[4,3,704,128]{3,2,1,0:T(8,128)(2,1)}, u32[]{:S(2)}, u32[]{:S(2)}) collective-permute-start(bf16[4,3,704,128]{3,2,1,0:T(8,128)(2,1)} %bitcast.124), channel_id=1, source_target_pairs={{0,4},{4,0},{8,12},{12,8},{16,20},{20,16},{24,28},{28,24},{1,5},{5... | collective-permute-start | bytes 6488072 | tf_op jit(solution)/shard_map/ppermute | solution.py:39
  130.2 25.5 %collective-permute-start.26 = (bf16[512,1024]{1,0:T(8,128)(2,1)}, bf16[512,1024]{1,0:T(8,128)(2,1)S(1)}, u32[]{:S(2)}, u32[]{:S(2)}) collective-permute-start(bf16[512,1024]{1,0:T(8,128)(2,1)} %bitcast.96), channel_id=1, source_target_pairs={{0,2},{1,3},{2,0},{3,1},{4,6},{5,7},{6,4},{7,5},{8,10},{9,11},{10,... | collective-permute-start | bytes 3145736 | tf_op jit(solution)/shard_map/ppermute | solution.py:39
  153.3 24.3 %collective-permute-start.24 = (bf16[512,1024]{1,0:T(8,128)(2,1)S(1)}, bf16[512,1024]{1,0:T(8,128)(2,1)}, u32[]{:S(2)}, u32[]{:S(2)}) collective-permute-start(bf16[512,1024]{1,0:T(8,128)(2,1)S(1)} %get-tuple-element.75.nm0_ref.refs_0_), channel_id=1, source_target_pairs={{0,2},{1,3},{2,0},{3,1},{4,6},{5,7},{6,4},{7,5},{8,10},{9,11},{10,... | collective-permute-start | bytes 3145736 | tf_op jit(solution)/shard_map/ppermute | solution.py:39
  154.2 23.5 %collective-permute-start.22 = (bf16[512,1024]{1,0:T(8,128)(2,1)S(1)}, bf16[512,1024]{1,0:T(8,128)(2,1)S(1)}, u32[]{:S(2)}, u32[]{:S(2)}) collective-permute-start(bf16[512,1024]{1,0:T(8,128)(2,1)S(1)} %bitcast.97), channel_id=1, source_target_pairs={{0,1},{1,0},{2,3},{3,2},{4,5},{5,4},{6,7},{7,6},{8,9},{9,8},{10,11... | collective-permute-start | bytes 3145736 | tf_op jit(solution)/shard_map/ppermute | solution.py:39
  154.2 24.4 %collective-permute-start.21 = (bf16[512,1024]{1,0:T(8,128)(2,1)S(1)}, bf16[512,1024]{1,0:T(8,128)(2,1)S(1)}, u32[]{:S(2)}, u32[]{:S(2)}) collective-permute-start(bf16[512,1024]{1,0:T(8,128)(2,1)S(1)} %get-tuple-element.75.nm0_ref.refs_0_), channel_id=1, source_target_pairs={{0,1},{1,0},{2,3},{3,2},{4,5},{5,4},{6,7},{7,6},{8,9},{9,8},{10,11... | collective-permute-start | bytes 3145736 | tf_op jit(solution)/shard_map/ppermute | solution.py:39
  155.7 47.6 %collective-permute-start.27 = (bf16[512,1024]{1,0:T(8,128)(2,1)S(1)}, bf16[512,1024]{1,0:T(8,128)(2,1)}, u32[]{:S(2)}, u32[]{:S(2)}) collective-permute-start(bf16[512,1024]{1,0:T(8,128)(2,1)S(1)} %collective-permute-done.26.up0_ref.refs_6_), channel_id=1, source_target_pairs={{0,1},{1,0},{2,3},{3,2},{4,5},{5,4},{6,7},{7,6},{8,9},{9,8},{10,11... | collective-permute-start | bytes 3145736 | tf_op jit(solution)/shard_map/ppermute | solution.py:39
  177.7 26.3 %collective-permute-start.25 = (bf16[512,1024]{1,0:T(8,128)(2,1)}, bf16[512,1024]{1,0:T(8,128)(2,1)}, u32[]{:S(2)}, u32[]{:S(2)}) collective-permute-start(bf16[512,1024]{1,0:T(8,128)(2,1)} %collective-permute-done.24.nm0_ref.refs_2_), channel_id=1, source_target_pairs={{0,1},{1,0},{2,3},{3,2},{4,5},{5,4},{6,7},{7,6},{8,9},{9,8},{10,11... | collective-permute-start | bytes 3145736 | tf_op jit(solution)/shard_map/ppermute | solution.py:39
  226.5 21.4 %collective-permute-start.30 = (bf16[2,512,1024]{2,1,0:T(8,128)(2,1)}, bf16[2,512,1024]{2,1,0:T(8,128)(2,1)}, u32[]{:S(2)}, u32[]{:S(2)}) collective-permute-start(bf16[2,512,1024]{2,1,0:T(8,128)(2,1)} %pad_maximum_fusion.1), channel_id=1, source_target_pairs={{0,1},{1,0},{2,3},{3,2},{4,5},{5,4},{6,7},{7,6},{8,9},{9,8},{10,11... | collective-permute-start | bytes 6291464 | tf_op jit(solution)/shard_map/ppermute | solution.py:39
  246.7 56.4 %collective-permute-start.50 = (bf16[4,3,704,128]{3,2,1,0:T(8,128)(2,1)}, bf16[4,3,704,128]{3,2,1,0:T(8,128)(2,1)S(1)}, u32[]{:S(2)}, u32[]{:S(2)}) collective-permute-start(bf16[4,3,704,128]{3,2,1,0:T(8,128)(2,1)} %get-tuple-element.116), channel_id=1, source_target_pairs={{0,4},{4,0},{8,12},{12,8},{16,20},{20,16},{24,28},{28,24},{1,5},{5... | collective-permute-start | bytes 6488072 | tf_op jit(solution)/shard_map/ppermute | solution.py:39
  251.2 25.4 %collective-permute-start.31 = (bf16[512,1024]{1,0:T(8,128)(2,1)S(1)}, bf16[512,1024]{1,0:T(8,128)(2,1)S(1)}, u32[]{:S(2)}, u32[]{:S(2)}) collective-permute-start(bf16[512,1024]{1,0:T(8,128)(2,1)S(1)} %get-tuple-element.165), channel_id=1, source_target_pairs={{0,2},{1,3},{2,0},{3,1},{4,6},{5,7},{6,4},{7,5},{8,10},{9,11},{10,... | collective-permute-start | bytes 3145736 | tf_op jit(solution)/shard_map/ppermute | solution.py:39
  305.1 141.6 %reduce-scatter.6.cloned.1.call-start = ((), (), s32[]{:S(2)}) async-start(), calls=%async_computation.6 | async-start | bytes 1310720 | tf_op jit(solution)/shard_map/reduce_scatter | solution.py:95
  306.3 9.5 %collective-permute-start.32 = (bf16[2,8,64,128]{3,2,1,0:T(8,128)(2,1)S(1)}, bf16[2,8,64,128]{3,2,1,0:T(8,128)(2,1)S(1)}, u32[]{:S(2)}, u32[]{:S(2)}) collective-permute-start(bf16[2,8,64,128]{3,2,1,0:T(8,128)(2,1)S(1)} %convert_element_type.229), channel_id=1, source_target_pairs={{4,0},{8,4},{12,8},{16,12},{20,16},{24,20},{28,24},{5,1},{9,5},{13... | collective-permute-start | bytes 786440 | tf_op jit(solution)/shard_map/ppermute | solution.py:796
  317.0 24.7 %collective-permute-start.33 = (bf16[2,8,64,128]{3,2,1,0:T(8,128)(2,1)S(1)}, bf16[2,8,64,128]{3,2,1,0:T(8,128)(2,1)S(1)}, u32[]{:S(2)}, u32[]{:S(2)}) collective-permute-start(bf16[2,8,64,128]{3,2,1,0:T(8,128)(2,1)S(1)} %fusion.16), channel_id=1, source_target_pairs={{8,0},{12,4},{16,8},{20,12},{24,16},{28,20},{9,1},{13,5},{17,9},{2... | collective-permute-start | bytes 786440 | tf_op jit(solution)/shard_map/ppermute | solution.py:796
  342.0 29.8 %collective-permute-start.34 = (bf16[2,8,64,128]{3,2,1,0:T(8,128)(2,1)S(1)}, bf16[2,8,64,128]{3,2,1,0:T(8,128)(2,1)S(1)}, u32[]{:S(2)}, u32[]{:S(2)}) collective-permute-start(bf16[2,8,64,128]{3,2,1,0:T(8,128)(2,1)S(1)} %fusion.15), channel_id=1, source_target_pairs={{16,0},{20,4},{24,8},{28,12},{17,1},{21,5},{25,9},{29,13},{18,2},{... | collective-permute-start | bytes 786440 | tf_op jit(solution)/shard_map/ppermute | solution.py:796
  380.4 4.9 collective-permute-start.42
  383.5 26.1 %collective-permute-start.47 = (bf16[4,2,64,1024]{3,2,1,0:T(8,128)(2,1)S(1)}, bf16[4,2,64,1024]{3,2,1,0:T(8,128)(2,1)S(1)}, u32[]{:S(2)}, u32[]{:S(2)}) collective-permute-start(bf16[4,2,64,1024]{3,2,1,0:T(8,128)(2,1)S(1)} %add_convert_fusion.6), channel_id=1, source_target_pairs={{0,4},{4,0},{8,12},{12,8},{16,20},{20,16},{24,28},{28,24},{1,5},{5... | collective-permute-start | bytes 3145736 | tf_op jit(solution)/shard_map/ppermute | solution.py:39
  383.8 25.8 %collective-permute-start.46 = (bf16[4,2,64,1024]{3,2,1,0:T(8,128)(2,1)S(1)}, bf16[4,2,64,1024]{3,2,1,0:T(8,128)(2,1)S(1)}, u32[]{:S(2)}, u32[]{:S(2)}) collective-permute-start(bf16[4,2,64,1024]{3,2,1,0:T(8,128)(2,1)S(1)} %get-tuple-element.107), channel_id=1, source_target_pairs={{0,1},{1,0},{2,3},{3,2},{4,5},{5,4},{6,7},{7,6},{8,9},{9,8},{10,11... | collective-permute-start | bytes 3145736 | tf_op jit(solution)/shard_map/ppermute | solution.py:39
  383.8 30.7 %collective-permute-start.41 = (bf16[4,3,64,1024]{3,2,1,0:T(8,128)(2,1)}, bf16[4,3,64,1024]{3,2,1,0:T(8,128)(2,1)}, u32[]{:S(2)}, u32[]{:S(2)}) collective-permute-start(bf16[4,3,64,1024]{3,2,1,0:T(8,128)(2,1)} %get-tuple-element.103), channel_id=1, source_target_pairs={{0,1},{1,0},{2,3},{3,2},{4,5},{5,4},{6,7},{7,6},{8,9},{9,8},{10,11... | collective-permute-start | bytes 4718600 | tf_op jit(solution)/shard_map/ppermute | solution.py:39
  387.3 55.3 %collective-permute-start.43 = (bf16[4,3,64,1024]{3,2,1,0:T(8,128)(2,1)}, bf16[4,3,64,1024]{3,2,1,0:T(8,128)(2,1)}, u32[]{:S(2)}, u32[]{:S(2)}) collective-permute-start(bf16[4,3,64,1024]{3,2,1,0:T(8,128)(2,1)} %add_convert_fusion.2), channel_id=1, source_target_pairs={{0,4},{4,0},{8,12},{12,8},{16,20},{20,16},{24,28},{28,24},{1,5},{5... | collective-permute-start | bytes 4718600 | tf_op jit(solution)/shard_map/ppermute | solution.py:39
  411.2 81.5 %reduce-scatter.4.cloned.1.call-start = ((), (), s32[]{:S(2)}) async-start(), calls=%async_computation.5 | async-start | bytes 1966080 | tf_op jit(solution)/shard_map/reduce_scatter | solution.py:95
  414.5 32.4 %collective-permute-start.28 = (bf16[2,512,1024]{2,1,0:T(8,128)(2,1)}, bf16[2,512,1024]{2,1,0:T(8,128)(2,1)}, u32[]{:S(2)}, u32[]{:S(2)}) collective-permute-start(bf16[2,512,1024]{2,1,0:T(8,128)(2,1)} %pad_maximum_fusion), channel_id=1, source_target_pairs={{0,1},{1,0},{2,3},{3,2},{4,5},{5,4},{6,7},{7,6},{8,9},{9,8},{10,11... | collective-permute-start | bytes 6291464 | tf_op jit(solution)/shard_map/ppermute | solution.py:39
  446.7 33.7 %collective-permute-start.51 = (bf16[3,704,128]{2,1,0:T(8,128)(2,1)}, bf16[3,704,128]{2,1,0:T(8,128)(2,1)}, u32[]{:S(2)}, u32[]{:S(2)}) collective-permute-start(bf16[3,704,128]{2,1,0:T(8,128)(2,1)} %bitcast.131), channel_id=1, source_target_pairs={{0,1},{1,0},{2,3},{3,2},{4,5},{5,4},{6,7},{7,6},{8,9},{9,8},{10,11... | collective-permute-start | bytes 1622024 | tf_op jit(solution)/shard_map/ppermute | solution.py:39
  449.5 33.4 %collective-permute-start.29 = (bf16[512,1024]{1,0:T(8,128)(2,1)}, bf16[512,1024]{1,0:T(8,128)(2,1)}, u32[]{:S(2)}, u32[]{:S(2)}) collective-permute-start(bf16[512,1024]{1,0:T(8,128)(2,1)} %fusion.2), channel_id=1, source_target_pairs={{0,2},{1,3},{2,0},{3,1},{4,6},{5,7},{6,4},{7,5},{8,10},{9,11},{10,... | collective-permute-start | bytes 3145736 | tf_op jit(solution)/shard_map/ppermute | solution.py:39
  451.8 23.8 %collective-permute-start.37 = (f32[3,1024]{1,0:T(4,128)S(1)}, f32[3,1024]{1,0:T(4,128)S(1)}, u32[]{:S(2)}, u32[]{:S(2)}) collective-permute-start(f32[3,1024]{1,0:T(4,128)S(1)} %fusion.26), channel_id=1, source_target_pairs={{0,2},{1,3},{2,0},{3,1},{4,6},{5,7},{6,4},{7,5},{8,10},{9,11},{10,... | collective-permute-start | bytes 36872 | tf_op jit(solution)/shard_map/ppermute | solution.py:39
  479.3 6.9 %collective-permute-start.39 = (f32[3,1024]{1,0:T(4,128)S(1)}, f32[3,1024]{1,0:T(4,128)S(1)}, u32[]{:S(2)}, u32[]{:S(2)}) collective-permute-start(f32[3,1024]{1,0:T(4,128)S(1)} %add.204), channel_id=1, source_target_pairs={{0,8},{4,12},{8,0},{12,4},{16,24},{20,28},{24,16},{28,20},{1,9},{5... | collective-permute-start | bytes 36872 | tf_op jit(solution)/shard_map/ppermute | solution.py:39
  479.4 9.5 %collective-permute-start.48 = (bf16[2,64,1024]{2,1,0:T(8,128)(2,1)}, bf16[2,64,1024]{2,1,0:T(8,128)(2,1)S(1)}, u32[]{:S(2)}, u32[]{:S(2)}) collective-permute-start(bf16[2,64,1024]{2,1,0:T(8,128)(2,1)} %bitcast.36), channel_id=1, source_target_pairs={{0,2},{1,3},{2,0},{3,1},{4,6},{5,7},{6,4},{7,5},{8,10},{9,11},{10,... | collective-permute-start | bytes 786440 | tf_op jit(solution)/shard_map/ppermute | solution.py:39
  481.8 30.3 %collective-permute-start.52 = (bf16[3,1408,128]{2,1,0:T(8,128)(2,1)S(1)}, bf16[3,1408,128]{2,1,0:T(8,128)(2,1)S(1)}, u32[]{:S(2)}, u32[]{:S(2)}) collective-permute-start(bf16[3,1408,128]{2,1,0:T(8,128)(2,1)S(1)} %pad_maximum_fusion.2), channel_id=1, source_target_pairs={{0,2},{1,3},{2,0},{3,1},{4,6},{5,7},{6,4},{7,5},{8,10},{9,11},{10,... | collective-permute-start | bytes 3244040 | tf_op jit(solution)/shard_map/ppermute | solution.py:39
  492.7 25.7 %collective-permute-start.44 = (bf16[3,64,1024]{2,1,0:T(8,128)(2,1)}, bf16[3,64,1024]{2,1,0:T(8,128)(2,1)S(1)}, u32[]{:S(2)}, u32[]{:S(2)}) collective-permute-start(bf16[3,64,1024]{2,1,0:T(8,128)(2,1)} %bitcast.133), channel_id=1, source_target_pairs={{0,2},{1,3},{2,0},{3,1},{4,6},{5,7},{6,4},{7,5},{8,10},{9,11},{10,... | collective-permute-start | bytes 1179656 | tf_op jit(solution)/shard_map/ppermute | solution.py:39
  (103 other events, 998.9 us)
Sparse Core Ops, SparseCore 0:
  37.6 51.9 all-gather.2
  305.2 62.8 reduce-scatter.7
  411.3 24.0 reduce-scatter.5
  446.8 32.1 reduce-scatter.3

commit v3 on v2

--- a/solution.py
+++ b/solution.py
@@ -15,8 +15,13 @@
 VMEM = pl.BlockSpec(memory_space=pltpu.VMEM)
 SMEM = pl.BlockSpec(memory_space=pltpu.SMEM)
 ANY = pl.BlockSpec(memory_space=pl.ANY)
-LIMIT = 60 * 1024 * 1024
-LIGHT = pl.CostEstimate(flops=1, bytes_accessed=1, transcendentals=0)
+STAGE = None
+DEAR = {'feed_forward_gradients': 90}
+WAITS = {'first': (), 'qgoz': ('kvz',), 'qgox': ('kvk',), 'qgon': ('kvk',), 'ffg': ('kvx',), 'kvn': (), 'ffa': ('up', 'upb'), 'att': (), 'nmd': ('ffa',), 'ffb': ('bo',), 'ffr': ('bt',), 'fs': ('bg',), 'mid': ('ffr',), 'mo': ('mid',), 'mt1': ('mid',), 's2': ('inn',), 'gra': ('s1',), 's3': ('gra',), 'out': ('oc', 'mg'), 'ent': ('kc',), 'ks': ('ent',), 'os': ('kc',), 'fw': ('ks',), 'up': ('kvf',)}
+
+
+def cost(name):
+    return pl.CostEstimate(flops=1 + DEAR.get(name, 0) * 10**9, bytes_accessed=1, transcendentals=0)
 
 
 def inverse_rms(values):
@@ -91,7 +96,18 @@
     def pair(self, pieces, bit):
         return pieces + [swap(p, "batch", bit, 4) for p in pieces] if self.fast else pieces
 
-    def sum_along(self, near):
+    def sum_along(self, near, direct=False):
+        if direct:
+            z = self.place // 2
+            total = lax.dynamic_index_in_dim(near, z, 0, keepdims=False).astype(F32)
+            for k in range(1, self.nz):
+                sent = lax.dynamic_index_in_dim(near, z ^ k, 0, keepdims=False)
+                pairs = [(i, i ^ (2 * k)) for i in range(self.seq)]
+                total = total + lax.ppermute(sent, "seq", pairs).astype(F32)
+            return total.astype(BF)
+        if near.shape[1] == 3:
+            got = lax.all_to_all(near, "seq", 0, 0, axis_index_groups=self.groups)
+            return jnp.sum(got.astype(F32), axis=0).astype(BF)
         return lax.psum_scatter(near, "seq", scatter_dimension=0, axis_index_groups=self.groups)
 
     def join(self, mine, bit, axis):
@@ -106,6 +122,60 @@
 
 def params(mib):
     return pltpu.CompilerParams(vmem_limit_bytes=mib * 1024 * 1024)
+
+
+def staged(name, body, out_shape, in_specs, out_specs, scratch):
+    ins = [i for i, spec in enumerate(in_specs) if spec is STAGE]
+    outs = [i for i, spec in enumerate(out_specs) if spec is STAGE]
+    n_in, n_out, n_own = len(in_specs), len(out_specs), len(scratch)
+
+    def kernel(*refs):
+        operands, results = list(refs[:n_in]), list(refs[n_in : n_in + n_out])
+        own, extra = refs[n_in + n_out : n_in + n_out + n_own], refs[n_in + n_out + n_own :]
+        in_sem, out_sem = extra[-2:]
+        loads, stores = {}, {}
+        for k, i in enumerate(ins):
+            loads[i] = pltpu.make_async_copy(operands[i], extra[k], in_sem.at[k])
+            operands[i] = extra[k]
+        for k, i in enumerate(outs):
+            held = extra[len(ins) + k]
+            stores[i] = pltpu.make_async_copy(held, results[i], out_sem.at[k])
+            results[i] = held
+        start_all(loads.values())
+        flushed = []
+
+        def ready(*some):
+            for i in some or list(loads):
+                if i in loads:
+                    loads.pop(i).wait()
+
+        def flush(*some):
+            for i in some:
+                if i in stores and i not in flushed:
+                    flushed.append(i)
+                    stores[i].start()
+
+        body(ready, flush, *operands, *results, *own)
+        ready()
+        flush(*stores)
+        wait_all(stores.values())
+
+    def call(*operands):
+        return pl.pallas_call(
+            kernel,
+            out_shape=out_shape,
+            in_specs=[ANY if spec is STAGE else spec for spec in in_specs],
+            out_specs=[ANY if spec is STAGE else spec for spec in out_specs],
+            scratch_shapes=list(scratch)
+            + [pltpu.VMEM(operands[i].shape, operands[i].dtype) for i in ins]
+            + [pltpu.VMEM(out_shape[i].shape, out_shape[i].dtype) for i in outs]
+            + [pltpu.SemaphoreType.DMA((max(1, len(ins)),)), pltpu.SemaphoreType.DMA((max(1, len(outs)),))],
+            compiler_params=params(60),
+            cost_estimate=cost(name),
+            name=name,
+        )(*operands)
+
+    return call
 
 
 def low_lanes():
@@ -184,13 +254,14 @@
     return jnp.maximum(x, 0.0) + jnp.log1p(e), jnp.where(x >= 0.0, 1.0, e) / (1.0 + e)
 
 
-def kv_body(plan, nb, base_ref, tokens_ref, gain_ref, tail_ref, *refs):
+def kv_body(plan, nb, ready, flush, base_ref, tokens_ref, gain_ref, tail_ref, *refs):
     pieces = refs[:nb]
     normed_ref, keys_ref, sig_ref, values_ref, fresh_ref, weight, sem = refs[nb:]
     d = tokens_ref.shape[1]
     copies = fetch(base_ref, pieces, weight, sem, (0, 1))
     for c in copies:
         start_all(c)
+    ready()
 
     def norm(i, _):
         source = tokens_ref[block(i), :].astype(F32)
@@ -198,6 +269,7 @@
         return 0
 
     lax.fori_loop(0, 2, norm, 0)
+    flush(0)
     wait_all(copies[0])
 
     def key_part(j, _):
@@ -208,6 +280,7 @@
         return 0
 
     lax.fori_loop(0, d // 256, key_part, 0)
+    flush(1, 2)
     wait_all(copies[1])
 
     def value_part(j, _):
@@ -216,6 +289,7 @@
         return 0
 
     lax.fori_loop(0, d // 256, value_part, 0)
+    flush(3)
 
     def states(i, _):
         rows, lanes = block(i // 8), block(i % 8, 128)
@@ -230,28 +304,27 @@
     nb = len(pieces)
     count, d = tokens.shape
     shape = jax.ShapeDtypeStruct((count, d), BF)
-    return pl.pallas_call(
+    return staged(
+        "keys_values",
         functools.partial(kv_body, plan, nb),
-        out_shape=[shape] * 4 + [jax.ShapeDtypeStruct((16, HEAD, 128), F32)],
-        in_specs=[SMEM] + [VMEM] * 3 + [ANY] * nb,
-        out_specs=[VMEM] * 5,
-        scratch_shapes=[
+        [shape] * 4 + [jax.ShapeDtypeStruct((16, HEAD, 128), F32)],
+        [SMEM, STAGE, VMEM, VMEM] + [ANY] * nb,
+        [STAGE] * 5,
+        [
             pltpu.VMEM((plan.nz, 2, plan.span, d), BF),
             pltpu.SemaphoreType.DMA((2, nb)),
         ],
-        compiler_params=params(24),
-        cost_estimate=LIGHT,
-        name="keys_values",
     )(bases, tokens, gain, tail, *pieces)
 
 
-def qg_body(plan, nb, base_ref, normed_ref, *refs):
+def qg_body(plan, nb, ready, flush, base_ref, normed_ref, *refs):
     pieces = refs[:nb]
     query_ref, sig_ref, gate_ref, weight, sem = refs[nb:]
     d = normed_ref.shape[1]
     copies = fetch(base_ref, pieces, weight, sem, (0, 1))
     for c in copies:
         start_all(c)
+    ready()
     wait_all(copies[0])
 
     def query_part(j, _):
@@ -262,6 +335,7 @@
         return 0
 
     lax.fori_loop(0, d // 256, query_part, 0)
+    flush(0, 1)
     wait_all(copies[1])
 
     def gate_part(j, _):
@@ -276,18 +350,16 @@
     nb = len(pieces)
     count, d = normed.shape
     shape = jax.ShapeDtypeStruct((count, d), BF)
-    return pl.pallas_call(
+    return staged(
+        "query_gate",
         functools.partial(qg_body, plan, nb),
-        out_shape=[shape, shape, jax.ShapeDtypeStruct((count, d), F32)],
-        in_specs=[SMEM, VMEM] + [ANY] * nb,
-        out_specs=[VMEM] * 3,
-        scratch_shapes=[
+        [shape, shape, jax.ShapeDtypeStruct((count, d), F32)],
+        [SMEM, STAGE] + [ANY] * nb,
+        [STAGE] * 3,
+        [
             pltpu.VMEM((plan.nz, 2, plan.span, d), BF),
             pltpu.SemaphoreType.DMA((2, nb)),
         ],
-        compiler_params=params(24),
-        cost_estimate=LIGHT,
-        name="query_gate",
     )(bases, normed, *pieces)
 
 
@@ -298,7 +370,7 @@
 
 
 def attend_body(
-    plan, nb, base_ref, query_ref, keys_ref, values_ref, gate_ref, state_ref, segcol_ref, segrow_ref,
+    plan, nb, ready, flush, base_ref, query_ref, keys_ref, values_ref, gate_ref, state_ref, segcol_ref, segrow_ref,
     gain_ref, tokens_ref, midgain_ref, *refs
 ):
     pieces = refs[:nb]
@@ -306,6 +378,7 @@
     d = query_ref.shape[1]
     (copies,) = fetch(base_ref, pieces, weight, sem, (2,))
     start_all(copies)
+    ready(1, 2, 3, 4, 5)
     for r in range(2):
         mask_ref[r] = pair_mask(segcol_ref, segrow_ref, r).astype(F32)
 
@@ -329,7 +402,10 @@
         return 0
 
     lax.fori_loop(0, 16, pair, 0, unroll=2)
+    flush(0, 1)
     wait_all(copies)
+
+    ready()
 
     def project(j, _):
         out = dot(gated_ref[...], weight[:, 0, :, block(j)].reshape(d, 256))
@@ -337,6 +413,7 @@
         return 0
 
     lax.fori_loop(0, d // 256, project, 0)
+    flush(2)
 
     def norm(i, _):
         middle = middle_ref[block(i), :]
@@ -350,24 +427,22 @@
     nb = len(pieces)
     count, d = query.shape
     low, high = jax.ShapeDtypeStruct((count, d), BF), jax.ShapeDtypeStruct((count, d), F32)
-    return pl.pallas_call(
+    return staged(
+        "attend",
         functools.partial(attend_body, plan, nb),
-        out_shape=[high, low, high, low],
-        in_specs=[SMEM] + [VMEM] * 10 + [ANY] * nb,
-        out_specs=[VMEM] * 4,
-        scratch_shapes=[
+        [high, low, high, low],
+        [SMEM] + [STAGE] * 5 + [VMEM] * 3 + [STAGE, VMEM] + [ANY] * nb,
+        [STAGE] * 4,
+        [
             pltpu.VMEM((2, 256, 256), F32),
             pltpu.VMEM((plan.nz, 1, plan.span, d), BF),
             pltpu.SemaphoreType.DMA((1, nb)),
         ],
-        compiler_params=params(28),
-        cost_estimate=LIGHT,
-        name="attend",
     )(bases, query, keys, values, gate, state, segcol, segrow, gain, tokens, midgain, *pieces)
 
 
 def mid_body(
-    plan, nb, base_ref, back_ref, got_ref, middle_ref, midgain_ref, upstream_ref, gate_ref, attended_ref,
+    plan, nb, ready, flush, base_ref, back_ref, got_ref, middle_ref, midgain_ref, upstream_ref, gate_ref, attended_ref,
     gain_ref, query_ref, segcol_ref, *refs
 ):
     pieces = refs[:nb]
@@ -375,6 +450,7 @@
     d = query_ref.shape[1]
     (copies,) = fetch(base_ref, pieces, weight, sem, (2,))
     start_all(copies)
+    ready(1, 2, 3, 5)
 
     def norm(i, total):
         rows = block(i, 128)
@@ -389,6 +465,7 @@
         return total + jnp.sum(dy * v * r, axis=0, keepdims=True)
 
     gains_ref[0:1, :] = lax.fori_loop(0, 4, norm, jnp.zeros((1, d), F32))
+    flush(0, 1)
     wait_all(copies)
 
     slabs = 256 // plan.span
@@ -399,6 +476,8 @@
         return 0
 
     lax.fori_loop(0, d // 256, through, 0)
+
+    ready()
 
     def pair(p, _):
         lanes = block(p, 128)
@@ -430,23 +509,21 @@
     nb = len(pieces)
     count, d = query.shape
     low, high = jax.ShapeDtypeStruct((count, d), BF), jax.ShapeDtypeStruct((count, d), F32)
-    return pl.pallas_call(
+    return staged(
+        "middle_back",
         functools.partial(mid_body, plan, nb),
-        out_shape=[
+        [
             high, low, low, low,
             jax.ShapeDtypeStruct((16, HEAD, 128), F32),
             jax.ShapeDtypeStruct((2, d), F32),
         ],
-        in_specs=[SMEM] + [VMEM] * 10 + [ANY] * nb,
-        out_specs=[VMEM] * 6,
-        scratch_shapes=[
+        [SMEM] + [STAGE] * 3 + [VMEM] + [STAGE] * 3 + [VMEM, STAGE, VMEM] + [ANY] * nb,
+        [STAGE] * 5 + [VMEM],
+        [
             pltpu.VMEM((count, d), F32),
             pltpu.VMEM((plan.nz, 1, plan.span, d), BF),
             pltpu.SemaphoreType.DMA((1, nb)),
         ],
-        compiler_params=params(32),
-        cost_estimate=LIGHT,
-        name="middle_back",
     )(bases, back, got, middle, midgain, upstream, gate, attended, gain, query, segcol, *pieces)
 
 
@@ -470,11 +547,12 @@
     lax.fori_loop(0, d // 256, features, 0)
 
 
-def grads_body(plan, which, base_ref, *refs):
+def grads_body(plan, which, ready, flush, base_ref, *refs):
     m, n = len(which), max(which) + 1
     lefts, rights = refs[:n], refs[n : n + m]
     outs = refs[n + m : -3]
     turned, grads, sem = refs[-3:]
+    ready()
     copies = hand_out(base_ref, grads, outs, sem)
     for k in range(m):
         if k == 0 or which[k] != which[k - 1]:
@@ -489,30 +567,30 @@
     m = len(rights)
     count, d = lefts[0].shape
     outs = piece_shapes(plan, m, plan.rows // 2 if plan.fast else plan.rows, d, 4)
-    return pl.pallas_call(
+    return staged(
+        "square_gradients",
         functools.partial(grads_body, plan, which),
-        out_shape=outs,
-        in_specs=[SMEM] + [VMEM] * (len(lefts) + m),
-        out_specs=[ANY] * len(outs),
-        scratch_shapes=[
+        outs,
+        [SMEM] + [STAGE] * (len(lefts) + m),
+        [ANY] * len(outs),
+        [
             pltpu.VMEM((d, count), BF),
             pltpu.VMEM((plan.nz, m, plan.span, d), BF),
             pltpu.SemaphoreType.DMA((m, len(outs))),
         ],
-        compiler_params=params(24),
-        cost_estimate=LIGHT,
-        name="square_gradients",
     )(bases, *lefts, *rights)
 
 
 def inner_body(
-    plan, query_ref, keys_ref, values_ref, qsig_ref, attback_ref, state_ref, segcol_ref, segrow_ref,
+    plan, ready, flush, query_ref, keys_ref, values_ref, qsig_ref, attback_ref, state_ref, segcol_ref, segrow_ref,
     qback_ref, kin_ref, vin_ref, mask_ref, turn_ref
 ):
     for r in range(2):
         mask = pair_mask(segcol_ref, segrow_ref, r).astype(F32)
         mask_ref[r] = mask
         turn_ref[r] = mask.T
+
+    ready()
 
     def pair(i, _):
         r = i // 8
@@ -543,25 +621,27 @@
 def inner_call(plan, query, keys, values, qsig, attback, state, segcol, segrow):
     count, d = query.shape
     low, high = jax.ShapeDtypeStruct((count, d), BF), jax.ShapeDtypeStruct((count, d), F32)
-    return pl.pallas_call(
+    return staged(
+        "attend_back",
         functools.partial(inner_body, plan),
-        out_shape=[low, high, high],
-        in_specs=[VMEM] * 8,
-        out_specs=[VMEM] * 3,
-        scratch_shapes=[pltpu.VMEM((2, 256, 256), F32), pltpu.VMEM((2, 256, 256), F32)],
-        compiler_params=params(20),
-        cost_estimate=LIGHT,
-        name="attend_back",
+        [low, high, high],
+        [STAGE] * 6 + [VMEM] * 2,
+        [STAGE] * 3,
+        [pltpu.VMEM((2, 256, 256), F32), pltpu.VMEM((2, 256, 256), F32)],
     )(query, keys, values, qsig, attback, state, segcol, segrow)
 
 
 def outer_body(
-    plan, sides, base_ref, keys_ref, values_ref, ksig_ref, kin_ref, vin_ref, after_ref, segcol_ref, segrow_ref,
+    plan, sides, ready, flush, base_ref, keys_ref, values_ref, ksig_ref, kin_ref, vin_ref, after_ref, segcol_ref, segrow_ref,
     normed_ref, *refs
 ):
     outs = refs[:sides]
     kback_ref, vback_ref, turned, grads, sem = refs[sides:]
+    ready(9)
     copies = hand_out(base_ref, grads, outs, sem)
+
+    turn_rows(normed_ref, turned)
+    ready()
 
     def pair(i, _):
         r = i // 8
@@ -575,7 +655,7 @@
         return 0
 
     lax.fori_loop(0, 16, pair, 0, unroll=2)
-    turn_rows(normed_ref, turned)
+    flush(sides, sides + 1)
     for k, right in enumerate((kback_ref, vback_ref)):
         gradient_rows(plan, turned, right, grads, k)
         start_all(copies[k])
@@ -587,24 +667,22 @@
     count, d = keys.shape
     outs = piece_shapes(plan, 2, plan.rows // 2 if plan.fast else plan.rows, d, 4)
     low = jax.ShapeDtypeStruct((count, d), BF)
-    got = pl.pallas_call(
+    got = staged(
+        "key_value_gradients",
         functools.partial(outer_body, plan, len(outs)),
-        out_shape=outs + [low] * 2,
-        in_specs=[SMEM] + [VMEM] * 9,
-        out_specs=[ANY] * len(outs) + [VMEM] * 2,
-        scratch_shapes=[
+        outs + [low] * 2,
+        [SMEM] + [STAGE] * 6 + [VMEM] * 2 + [STAGE],
+        [ANY] * len(outs) + [STAGE] * 2,
+        [
             pltpu.VMEM((d, count), BF),
             pltpu.VMEM((plan.nz, 2, plan.span, d), BF),
             pltpu.SemaphoreType.DMA((2, len(outs))),
         ],
-        compiler_params=params(24),
-        cost_estimate=LIGHT,
-        name="key_value_gradients",
     )(bases, keys, values, ksig, kin, vin, after, segcol, segrow, normed)
     return got[: len(outs)], got[len(outs) :]
 
 
-def entry_body(plan, nb, base_ref, tokens_ref, gain_ref, midback_ref, qb_ref, kb_ref, vb_ref, gb_ref, *refs):
+def entry_body(plan, nb, ready, flush, base_ref, tokens_ref, gain_ref, midback_ref, qb_ref, kb_ref, vb_ref, gb_ref, *refs):
     kv, qg = refs[:nb], refs[nb : 2 * nb]
     out_ref, gains_ref, total, weight, more, sem = refs[2 * nb :]
     d = tokens_ref.shape[1]
@@ -619,6 +697,7 @@
     ):
         wait_all(c)
         first = back is qb_ref
+        ready({id(qb_ref): 4, id(kb_ref): 5, id(vb_ref): 6, id(gb_ref): 7}[id(back)])
 
         def through(j, _, back=back, scr=scr, k=k, first=first):
             rows_w = scr[pl.ds(j * slabs, slabs), k].reshape(256, d)
@@ -630,6 +709,8 @@
             return 0
 
         lax.fori_loop(0, d // 256, through, 0)
+
+    ready()
 
     def norm(i, gains):
         rows = block(i, 128)
@@ -647,20 +728,18 @@
 def entry_call(plan, bases, tokens, gain, midback, qb, kb, vb, gb, kv, qg):
     nb = len(kv)
     count, d = tokens.shape
-    return pl.pallas_call(
+    return staged(
+        "entry_back",
         functools.partial(entry_body, plan, nb),
-        out_shape=[jax.ShapeDtypeStruct((count, d), F32), jax.ShapeDtypeStruct((1, d), F32)],
-        in_specs=[SMEM] + [VMEM] * 7 + [ANY] * (2 * nb),
-        out_specs=[VMEM] * 2,
-        scratch_shapes=[
+        [jax.ShapeDtypeStruct((count, d), F32), jax.ShapeDtypeStruct((1, d), F32)],
+        [SMEM, STAGE, VMEM] + [STAGE] * 5 + [ANY] * (2 * nb),
+        [STAGE, VMEM],
+        [
             pltpu.VMEM((count, d), F32),
             pltpu.VMEM((plan.nz, 2, plan.span, d), BF),
             pltpu.VMEM((plan.nz, 2, plan.span, d), BF),
             pltpu.SemaphoreType.DMA((2, 2, nb)),
         ],
-        compiler_params=params(32),
-        cost_estimate=LIGHT,
-        name="entry_back",
     )(bases, tokens, gain, midback, qb, kb, vb, gb, *kv, *qg)
 
 
@@ -678,22 +757,29 @@
     return copies
 
 
-def ff_body(nb, base_ref, nm0_ref, nm1_ref, up0_ref, up1_ref, *refs):
+def ff_body(nb, ready, flush, base_ref, nm0_ref, nm1_ref, up0_ref, up1_ref, *refs):
     pieces = refs[:nb]
-    mixed_ref, back_ref, joined_t, left_t, right_t, weight, joined_s, left_s, right_s, sem = refs[nb:]
+    mixed_refs, back_refs = refs[nb : nb + 2], refs[nb + 2 : nb + 4]
+    joined_t, left_t, right_t, weight, joined_s, left_s, right_s, sem = refs[nb + 4 :]
     count, d = nm0_ref.shape
     hidden = weight.shape[1]
     copies = blocks(base_ref, pieces, weight, sem, True)
     for c in copies:
         start_all(c)
-    for c in copies:
-        wait_all(c)
     for h, (nm_ref, up_ref) in enumerate(((nm0_ref, up0_ref), (nm1_ref, up1_ref))):
         rows = pl.ds(h * count, count)
         for start in range(0, hidden, 256):
             some = slice(start, min(start + 256, hidden))
+            ready(1 + h)
+            if h == 0 and start == 0:
+                wait_all(copies[0])
             left = dot_nt(nm_ref[...], weight[0, some, :])
+            if h == 0 and start == 0:
+                wait_all(copies[1])
             right = dot_nt(nm_ref[...], weight[1, some, :])
+            ready(3 + h)
+            if h == 0 and start == 0:
+                wait_all(copies[2])
             joined_back = dot_nt(up_ref[...], weight[2, some, :])
             for value, straight, turned in (
                 (left * right, joined_s, joined_t),
@@ -704,43 +790,47 @@
                 straight[rows, some] = value
                 turned[some, rows] = value.T
 
-    def through(j, _):
-        for h in range(2):
+    flush(4, 5, 6)
+
+    for h in range(2):
+
+        def through(j, _, h=h):
             rows = pl.ds(h * count, count)
-            mixed_ref[rows, block(j)] = dot(joined_s[rows, :], weight[2, :, block(j)]).astype(BF)
+            mixed_refs[h][:, block(j)] = dot(joined_s[rows, :], weight[2, :, block(j)]).astype(BF)
             back = dot(left_s[rows, :], weight[0, :, block(j)]) + dot(right_s[rows, :], weight[1, :, block(j)])
-            back_ref[rows, block(j)] = back.astype(BF)
-        return 0
-
-    lax.fori_loop(0, d // 256, through, 0)
+            back_refs[h][:, block(j)] = back.astype(BF)
+            return 0
+
+        lax.fori_loop(0, d // 256, through, 0)
+        flush(h, 2 + h)
 
 
 def ff_call(bases, nm, up, pieces):
     nb = len(pieces)
     n, three, hidden, _ = pieces[0].shape
     count, d = nm[0].shape
-    whole, some = jax.ShapeDtypeStruct((2 * count, d), BF), jax.ShapeDtypeStruct((hidden, 2 * count), BF)
-    return pl.pallas_call(
+    whole, some = jax.ShapeDtypeStruct((count, d), BF), jax.ShapeDtypeStruct((hidden, 2 * count), BF)
+    return staged(
+        "feed_forward",
         functools.partial(ff_body, nb),
-        out_shape=[whole, whole, some, some, some],
-        in_specs=[SMEM] + [VMEM] * 4 + [ANY] * nb,
-        out_specs=[VMEM] * 5,
-        scratch_shapes=[pltpu.VMEM((three, hidden, d), BF)]
+        [whole] * 4 + [some] * 3,
+        [SMEM] + [STAGE] * 4 + [ANY] * nb,
+        [STAGE] * 7,
+        [pltpu.VMEM((three, hidden, d), BF)]
         + [pltpu.VMEM((2 * count, hidden), BF)] * 3
         + [pltpu.SemaphoreType.DMA((3, nb, n))],
-        compiler_params=params(40),
-        cost_estimate=LIGHT,
-        name="feed_forward",
     )(bases, *nm, *up, *pieces)
 
 
-def ffgrad_body(base_ref, *refs):
+def ffgrad_body(ready, flush, base_ref, *refs):
     nms, ups = refs[:4], refs[4:8]
     joined, left, right = [refs[8 + k : 14 : 3] for k in range(3)]
     outs, (grads, sem) = refs[14:-2], refs[-2:]
     count, d = nms[0].shape
     copies = blocks(base_ref, outs, grads, sem, False)
     for k, (turned, straight) in enumerate(((left, nms), (right, nms), (joined, ups))):
+
+        ready(*((1, 2, 3, 4, 10, 13), (11, 14), ())[k])
 
         def some(j, _, k=k, turned=turned, straight=straight):
             value = None
@@ -759,18 +849,16 @@
 def ffgrad_call(bases, nms, ups, first, second, shapes):
     hidden = first[0].shape[0]
     d = nms[0].shape[1]
-    return pl.pallas_call(
+    return staged(
+        "feed_forward_gradients",
         ffgrad_body,
-        out_shape=[jax.ShapeDtypeStruct(shape, BF) for shape in shapes],
-        in_specs=[SMEM] + [VMEM] * 14,
-        out_specs=[ANY] * len(shapes),
-        scratch_shapes=[
+        [jax.ShapeDtypeStruct(shape, BF) for shape in shapes],
+        [SMEM] + [STAGE] * 14,
+        [ANY] * len(shapes),
+        [
             pltpu.VMEM((3, hidden, d), BF),
             pltpu.SemaphoreType.DMA((3, len(shapes), shapes[0][0])),
         ],
-        compiler_params=params(40),
-        cost_estimate=LIGHT,
-        name="feed_forward_gradients",
     )(bases, *nms, *ups, *first, *second)
 
 
@@ -778,26 +866,28 @@
     return [(i, i + order * step) for i in range(size) if 0 <= i + order * step < size]
 
 
-def kept(keep, order, size):
-    own, between, steps, step = keep, jnp.ones_like(keep), [], 1
-    while step < size:
-        steps.append((between, own))
-        if step * 2 < size:
-            got = lax.ppermute(own, "seq", beyond(order, step, size))
-            between, own = between * got, own * got
-        step *= 2
-    return steps
-
-
-def chain(own, steps, order, size, beside):
-    total, before = own, jnp.zeros_like(own)
-    for i, (between, whole) in enumerate(steps):
-        sent = tie(total.astype(BF), *beside[i]) if i < len(beside) else total.astype(BF)
-        got = lax.ppermute(sent, "seq", beyond(order, 2**i, size)).astype(F32)
-        shape = between.shape + (1,) * (own.ndim - 1)
-        before = before + between.reshape(shape) * got
-        total = total + whole.reshape(shape) * got
-    return before
+class Chain:
+    def __init__(self, own, keep, order, size):
+        self.total, self.before = own, jnp.zeros_like(own)
+        self.whole, self.between = keep[:, None, None], jnp.ones_like(keep)[:, None, None]
+        self.order, self.size, self.reach = order, size, 1
+
+    def step(self, *others):
+        rows, n, lanes = self.total.shape
+        flags = jnp.broadcast_to(self.whole, (rows, 16, lanes))
+        sent = tie(jnp.concatenate([self.total, flags], axis=1).astype(BF), *others)
+        received = lax.ppermute(sent, "seq", beyond(self.order, self.reach, self.size))
+        got, got_whole = received[:, :n].astype(F32), received[:, n : n + 1, :1].astype(F32)
+        self.before = self.before + self.between * got
+        self.total = self.total + self.whole * got
+        self.between, self.whole = self.between * got_whole, self.whole * got_whole
+        self.reach *= 2
+        return received
+
+    def result(self):
+        while self.reach < self.size:
+            self.step()
+        return self.before.astype(BF).reshape(-1, HEAD, 128)
 
 
 def shards(
@@ -822,32 +912,7 @@
     hidden = left_weight.shape[1]
     plan = Plan(mesh_shape, width)
     seq = plan.seq
-    by_x, by_half, by_quarter = plan.bases(()), plan.bases((1,)), plan.bases((2, 1))
-
-    def square(shards, behind):
-        near = plan.along(tie(plan.mine(jnp.stack(shards), (2, 1)), *behind), True)
-        return near, plan.pair(plan.pair(plan.across(near), 2), 1)
-
-    kv_z, kv = square([key_weight, value_weight], ())
-    mine = hidden // 4
-    stack = lax.dynamic_slice(
-        jnp.stack([left_weight.T, right_weight.T, down_weight]),
-        (0, plan.lane * mine, 0),
-        (3, mine, plan.rows),
-    )
-    ff_z = plan.along(stack, False)
-    qgo_z, qgo = square([query_weight, gate_weight, output_weight], (kv_z,))
-    ff_pieces = plan.across(ff_z)
-    if not plan.fast:
-        whole = ff_z.transpose(1, 2, 0, 3).reshape(3, mine, width // 128, 128)
-        ff_pieces = [whole.transpose(2, 0, 1, 3)]
-    upstream = cotangent.reshape(count, width)
-
-    def spread_tokens(own):
-        beside, above = swap(own, "batch", 1, plan.batch), swap(own, "batch", 2, plan.batch)
-        return [own, beside, above, swap(above, "batch", 1, plan.batch)]
-
-    up_all = spread_tokens(upstream)
+    by_whole, by_half, by_quarter = jnp.zeros((1,), jnp.int32), plan.bases((1,)), plan.bases((2, 1))
 
     place = jnp.arange(span)
     segment = dot(starts.astype(BF), (place[:, None] <= place[None, :]).astype(BF))
@@ -858,79 +923,168 @@
     source = tokens.reshape(count, width)
     entry_row, head_row, mid_row = (g.reshape(1, width) for g in (entry_gain, head_gain, middle_gain))
 
-    ahead, behind = kept(keep, 1, seq), kept(keep, -1, seq)
-
-    def scan(own, steps, order, beside):
-        own = own.reshape(rows_here, -1, HEAD, 128)
-        return chain(own, steps, order, seq, beside).astype(BF).reshape(-1, HEAD, 128)
-
-    early = tie(by_quarter, *(f for pair in ahead + behind for f in pair))
-    normed_in, keys, ksig, values, fresh = kv_call(plan, early, source, entry_row, tail, kv)
-    state = scan(fresh, ahead, 1, ())
-    query, qsig, gate = qg_call(plan, by_quarter, normed_in, qgo)
+    def scan(own, order):
+        return Chain(own.reshape(rows_here, -1, 128), keep, order, seq)
+
+    done = {}
+
+    def held(name, value):
+        return tie(value, *(done[other] for other in WAITS.get(name, ()) if other in done))
+
+    def note(name, value):
+        done[name] = value
+        return value
+
+    def send(name, value, axis, bit):
+        return note(name, swap(held(name, value), axis, bit, plan.seq if axis == "seq" else plan.batch))
+
+    def quarter(weights):
+        return plan.mine(jnp.stack(weights), (2, 1))
+
+    kv_z = note("kvz", plan.along(quarter([key_weight, value_weight]), True))
+    qgo_z = quarter([query_weight, gate_weight, output_weight])
+    qgo_z = note("qgoz", plan.along(held("qgoz", qgo_z), True))
+    mine = hidden // 4
+    stack = lax.dynamic_slice(
+        jnp.stack([left_weight.T, right_weight.T, down_weight]),
+        (0, plan.lane * mine, 0),
+        (3, mine, plan.rows),
+    )
+    ff_seq = lax.all_gather(held("ffg", stack), "seq", axis=0)
+    if plan.rows != 128:
+        ff_seq = ff_seq.transpose(1, 2, 0, 3).reshape(3, mine, width // 128, 128).transpose(2, 0, 1, 3)
+    upstream = cotangent.reshape(count, width)
+    kv, qgo = [kv_z], [qgo_z]
+    if "up" in WAITS.get("first", ()):
+        up_above = send("up", upstream, "batch", 2)
+    if plan.fast:
+        kv.append(send("kvx", kv_z, "seq", 1))
+        kv += [send("kvn", kv_z, "batch", 2), send("kvf", kv[1], "batch", 2)]
+        kv += [send("kvc", piece, "batch", 1) for piece in kv]
+    if plan.fast and "qgox" in WAITS.get("first", ()):
+        qgo.append(send("qgox", qgo_z, "seq", 1))
+        qgo.append(send("qgon", qgo_z, "batch", 2))
+
+    normed_in, keys, ksig, values, fresh = kv_call(
+        plan, held("kvk", by_quarter), source, entry_row, tail, kv
+    )
+    note("kvk", keys)
+    chain = scan(fresh, 1)
+    if "r1" in WAITS.get("first", ()):
+        note("r1", chain.step(*(done[other] for other in WAITS.get("r1", ()))))
+    if plan.fast and len(qgo) == 1:
+        qgo.append(send("qgox", qgo_z, "seq", 1))
+        qgo.append(send("qgon", qgo_z, "batch", 2))
+    if "r1" not in done:
+        note("r1", chain.step(*(done[other] for other in WAITS.get("r1", ()) if other in done)))
+    if plan.fast:
+        qgo.append(send("qgof", qgo[1], "batch", 2))
+    note("r2", chain.step(*(done[other] for other in WAITS.get("r2", ()) if other in done)))
+    if plan.fast:
+        qgo += [send("qgoc", piece, "batch", 1) for piece in qgo]
+    if "up" not in done:
+        up_above = send("up", upstream, "batch", 2)
+    up_all = [upstream, send("upb", upstream, "batch", 1), up_above, send("upd", up_above, "batch", 1)]
+    note("r3", chain.step(*(done[other] for other in WAITS.get("r3", ()) if other in done)))
+    state = chain.result()
+    query, qsig, gate = qg_call(plan, held("qgk", by_quarter), normed_in, qgo)
+    note("qgk", query)
     attended, gated, middle, normed_mid = attend_call(
-        plan, by_quarter, query, keys, values, gate, state, segcol, segrow, head_row, source, mid_row, qgo
+        plan, held("att", by_quarter), query, keys, values, gate, state, segcol, segrow, head_row, source, mid_row, qgo
     )
-    nm_all = spread_tokens(normed_mid)
-    mixed_a, back_a, *saved_a = ff_call(by_x, nm_all[:2], up_all[:2], ff_pieces)
-    mixed_b, back_b, *saved_b = ff_call(by_x, nm_all[2:], up_all[2:], ff_pieces)
-
-    def collect(mine_a, mine_b):
-        other = swap(jnp.stack([mine_a[count:], mine_b[count:]]), "batch", 1, plan.batch)
-        return add(mine_a[:count], other[0]), swap(add(mine_b[:count], other[1]), "batch", 2, plan.batch)
-
-    back_own, back_got = collect(back_a, back_b)
-    ff_terms = ffgrad_call(by_x, nm_all, up_all, saved_a, saved_b, [p.shape for p in ff_pieces])
-    if plan.fast:
-        ff_far = swap(ff_terms[1], "seq", 1, seq)
-    mixed_own, mixed_got = collect(mixed_a, mixed_b)
-    mixed = (middle + (mixed_own.astype(F32) + mixed_got.astype(F32))).astype(BF).reshape(tokens.shape)
+    note("att", gated)
+    nm_above = send("nma", normed_mid, "batch", 2)
+    nm_all = [normed_mid, send("nmb", normed_mid, "batch", 1)]
+    mixed_0, mixed_1, back_0, back_1, *saved_a = ff_call(held("ffa", by_whole), nm_all, up_all[:2], [ff_seq])
+    note("ffa", back_0)
+    nm_above = held("nmd", nm_above)
+    nm_all += [nm_above, send("nmd", nm_above, "batch", 1)]
+    back_own = note("bo", add(back_0, send("bo1", back_1, "batch", 1)))
+    mixed_2, mixed_3, back_2, back_3, *saved_b = ff_call(held("ffb", by_whole), nm_all[2:], up_all[2:], [ff_seq])
+    note("ffb", back_2)
+    back_there = note("bt", add(back_2, send("bt1", back_3, "batch", 1)))
+    back_got = send("bg", back_there, "batch", 2)
+    ff_terms = ffgrad_call(held("ffr", by_whole), nm_all, up_all, saved_a, saved_b, [ff_seq.shape])
+    note("ffr", ff_terms[0])
+    ff_share = held("fs", ff_terms[0])
+    if plan.rows != 128:
+        ff_share = ff_share.transpose(1, 2, 0, 3).reshape(3, mine, seq, plan.rows).transpose(2, 0, 1, 3)
+    ff_part = note("fs", lax.psum_scatter(ff_share, "seq", scatter_dimension=0))
 
     midback, branch, gateback, attback, direct, two_gains = mid_call(
-        plan, by_quarter, back_own, back_got, middle, mid_row, upstream, gate, attended, head_row, query, segcol, qgo
+        plan, held("mid", by_quarter), back_own, back_got, middle, mid_row, upstream, gate, attended, head_row,
+        query, segcol, qgo,
     )
-    qback, kin, vin = inner_call(plan, query, keys, values, qsig, attback, state, segcol, segrow)
-    ogq_terms = grads_call(plan, by_half, [gated, normed_in], (0, 1, 1), [branch, gateback, qback])
-    after = scan(direct, behind, -1, ((), (kin,), ogq_terms[:1]))
-    kv_terms, (kback, vback) = outer_call(
-        plan, by_half, keys, values, ksig, kin, vin, after, segcol, segrow, normed_in
+    note("mid", attback)
+    chain = scan(direct, -1)
+    note("s1", chain.step())
+    qback, kin, vin = inner_call(plan, query, keys, values, held("inn", qsig), attback, state, segcol, segrow)
+    note("inn", kin)
+    mixed_own = add(mixed_0, send("mo", mixed_1, "batch", 1))
+    mixed_there = note("mt", add(mixed_2, send("mt1", mixed_3, "batch", 1)))
+    mixed_got = send("mg", mixed_there, "batch", 2)
+    note("s2", chain.step(*(done[other] for other in WAITS.get("s2", ()) if other in done)))
+    ogq_terms = grads_call(
+        plan, held("gra", by_half), [gated, normed_in], (0, 1, 1), [branch, gateback, qback]
     )
-
-    def from_core(term):
-        return [add(mine, swap(other, "batch", 1, 4)) for mine, other in zip(term[:2], term[2:])]
+    note("gra", ogq_terms[0])
 
     def finish(part):
         return plan.join(add(part, swap(part, "batch", 2, 4)), 1, 1).astype(F32)
 
+    def quarters(part):
+        above = swap(part, "batch", 2, plan.batch)
+        lower = plan.half(2) == 0
+        mine = jnp.stack([jnp.where(lower, part, above), jnp.where(lower, above, part)])
+        return mine, swap(mine, "batch", 1, plan.batch)
+
+    if plan.fast and "oc" in WAITS.get("first", ()):
+        ogq_far = note("oc", add(ogq_terms[1], send("oc1", ogq_terms[3], "batch", 1)))
+        ogq_near = add(ogq_terms[0], send("oc0", ogq_terms[2], "batch", 1))
+        ogq_got = send("ox", ogq_far, "seq", 1)
+    note("s3", chain.step(*(done[other] for other in WAITS.get("s3", ()) if other in done)))
+    if plan.fast and "oc" not in done:
+        ogq_far = note("oc", add(ogq_terms[1], send("oc1", ogq_terms[3], "batch", 1)))
+        ogq_near = add(ogq_terms[0], send("oc0", ogq_terms[2], "batch", 1))
+        ogq_got = send("ox", ogq_far, "seq", 1)
+    after = chain.result()
+    kv_terms, (kback, vback) = outer_call(
+        plan, held("out", by_half), keys, values, ksig, kin, vin, after, segcol, segrow, normed_in
+    )
+    note("out", kback)
     if plan.fast:
-        ff_part = plan.sum_along(add(ff_terms[0], tie(ff_far, kin)))
-        ogq_near, ogq_far = from_core(ogq_terms)
-        ogq_got = swap(ogq_far, "seq", 1, seq)
-        kv_near, kv_far = from_core(kv_terms)
-        kv_got = swap(kv_far, "seq", 1, seq)
+        kv_far = note("kc", add(kv_terms[1], send("kc1", kv_terms[3], "batch", 1)))
+        kv_got = send("kx", kv_far, "seq", 1)
+        kv_near = add(kv_terms[0], send("kc0", kv_terms[2], "batch", 1))
+    input_gradient, entry_term = entry_call(
+        plan, held("ent", by_quarter), source, entry_row, midback, qback, kback, vback, gateback, kv, qgo
+    )
+    note("ent", entry_term)
+    input_gradient = input_gradient.reshape(tokens.shape)
+    mixed = (middle + (mixed_own.astype(F32) + held("mx", mixed_got).astype(F32))).astype(BF)
+    mixed = mixed.reshape(tokens.shape)
+    if plan.fast:
+        kv_sum = note("ks", add(kv_near, held("ks", kv_got)))
+        kv_part = note("kz", plan.sum_along(kv_sum, True))
+        ogq_sum = note("os", add(ogq_near, held("os", ogq_got)))
+        ogq_part = note("oz", plan.sum_along(ogq_sum))
+        wide = quarters(held("fw", ff_part))
+        note("fw", wide[0])
+        output_total, gate_total, query_total = finish(held("of", ogq_part))
+        key_total, value_total = finish(held("kf", kv_part))
     else:
-        turned = ff_terms[0].transpose(1, 2, 0, 3).reshape(3, mine, seq, plan.rows)
-        ff_part = lax.psum_scatter(turned.transpose(2, 0, 1, 3), "seq", scatter_dimension=0)
-    input_gradient, entry_term = entry_call(
-        plan, tie(by_quarter, kv_far) if plan.fast else by_quarter,
-        source, entry_row, midback, qback, kback, vback, gateback, kv, qgo,
-    )
-    input_gradient = input_gradient.reshape(tokens.shape)
-    if plan.fast:
-        ogq_part = plan.sum_along(add(ogq_near, ogq_got))
-        kv_part = plan.sum_along(add(kv_near, tie(kv_got, entry_term)))
-        wide = plan.join(plan.join(tie(ff_part, kv_part), 1, 1), 2, 1).astype(F32)
-        output_total, gate_total, query_total = finish(ogq_part)
-        key_total, value_total = finish(kv_part)
-    else:
-        wide = plan.join(plan.join(ff_part, 1, 1), 2, 1).astype(F32)
+        wide = quarters(ff_part)
         output_total, gate_total, query_total, key_total, value_total = (
             total
             for term in (ogq_terms, kv_terms)
             for total in lax.psum(lax.psum_scatter(term[0], "seq", scatter_dimension=0), "batch").astype(F32)
         )
+    own, other = wide
+    lower = plan.half(1) == 0
+    first, second = jnp.where(lower, own, other), jnp.where(lower, other, own)
+    wide = jnp.concatenate([first[0], second[0], first[1], second[1]], axis=1).astype(F32)
     left_total, right_total, down_total = wide[0].T, wide[1].T, wide[2]
-    gains = jnp.concatenate([two_gains, entry_term])
+    gains = held("gains", jnp.concatenate([two_gains, entry_term]))
     if plan.fast:
         for axis, size in (("batch", plan.batch), ("seq", seq)):
             step = 1

time: 539 us -> 471 us (0.87)
  waiting for transfers between devices: 241 us -> 142 us
  Pallas kernels: 121 us -> 163 us
  local copies, waits for them, and re-layouts: 53.8 us -> 20.5 us
  blocking collectives: 0 us -> 30.8 us
    ppermute x43, waiting for transfers between devices: 155 us -> 65.4 us  [swap(): return lax.ppermute(value, axis, [(i, i ^ bit) for i in range(size)])]
    pallas_call x11, Pallas kernels: 121 us -> 163 us  [call(): pl.pallas_call(kernel, out_shape=out_shape, in_specs=[ANY if spec is STAG...]
    unnamed x192 -> x80, local copies, waits for them, and re-layouts: 45.8 us -> 14.7 us
    all_to_all x0 -> x1, blocking collectives: none -> 30.8 us  [along(): return lax.all_to_all(copies, 'seq', 0, 0, axis_index_groups=self.groups)]
    all_to_all x2 -> x1, waiting for transfers between devices: 25.1 us -> 7.71 us  [along(): return lax.all_to_all(copies, 'seq', 0, 0, axis_index_groups=self.groups)]
    ppermute x10 -> x9, starting transfers between devices: 29.6 us -> 20.1 us  [the longest x6 16.2 us: step(): lax.ppermute(sent, 'seq', beyond(self.order, self.reach, self.size))]
    ppermute x10 -> x9, waiting for transfers between devices: 60.5 us -> 69 us  [the longest x6 52.9 us: step(): lax.ppermute(sent, 'seq', beyond(self.order, self.reach, self.size))]
    all_to_all x2 -> x1, starting transfers between devices: 9.94 us -> 3.49 us  [along(): return lax.all_to_all(copies, 'seq', 0, 0, axis_index_groups=self.groups)]
  transfers between devices with their start and end apart: 59 -> 56, of which waited for: 24 -> 27; matrix products, arithmetic and copies ran while one was open for 7% -> 8% of each run, Pallas kernels for 20% -> 31%
where the time goes in v3:
time: 471 us; the launch traced here: 465 us
  Pallas kernels  163 us (35%)
  waiting for transfers between devices  142 us (30%)
  starting transfers between devices  59.1 us (13%)
  other arithmetic  34.3 us (7%)
  blocking collectives  30.8 us (7%)
  local copies, waits for them, and re-layouts  20.5 us (4%)
  between operations  15.2 us (3%)
    pallas_call x11, Pallas kernels, call(): pl.pallas_call(kernel, out_shape=out_shape, in_specs=[ANY if spec is STAG...  163 us
    ppermute x43, waiting for transfers between devices, swap(): return lax.ppermute(value, axis, [(i, i ^ bit) for i in range(size)])  65.4 us
    ppermute x6, waiting for transfers between devices, step(): lax.ppermute(sent, 'seq', beyond(self.order, self.reach, self.size))  52.9 us
    all_to_all x1, blocking collectives, along(): return lax.all_to_all(copies, 'seq', 0, 0, axis_index_groups=self.groups)  30.8 us
    ppermute x43, starting transfers between devices, swap(): return lax.ppermute(value, axis, [(i, i ^ bit) for i in range(size)])  29.5 us
    convert_element_type x9, other arithmetic, add(): return (left.astype(F32) + right.astype(F32)).astype(BF)  17.8 us
    ppermute x6, starting transfers between devices, step(): lax.ppermute(sent, 'seq', beyond(self.order, self.reach, self.size))  16.2 us
    ppermute x3, waiting for transfers between devices, sum_along(): total = total + lax.ppermute(sent, 'seq', pairs).astype(F32)  16.1 us
  transfers between devices with their start and end apart: 56, of which 27 were waited for; matrix products, arithmetic and copies ran while one was open for 8% of the time, Pallas kernels for 31%

profile of v3, /device:TPU:0, one launch (start us, length us, event | category | flops | bytes accessed | tf_op | source)
XLA Modules:
  0.0 465.3 jit_solution(4697686949683482736)
XLA Ops:
  11.4 30.8 %all_to_all.15.refs_4_.refs_8_ = bf16[4,2,32,1024]{3,2,1,0:T(8,128)(2,1)S(1)} all-to-all(bf16[4,2,32,1024]{3,2,1,0:T(8,128)(2,1)S(1)} %broadcast_in_dim.22), channel_id=1, replica_groups={{0,8,16,24},{4,12,20,28},{1,9,17,25},{5,13,21,29},{2,10,18,26},{6,14,22..., dimensions={0} | all-to-all | bytes 1048576 | tf_op jit(solution)/shard_map/all_to_all | solution.py:90
  46.5 3.5 all-to-all-start.1
  54.3 3.5 collective-permute-done.1.refs_6_.refs_10_
  57.8 6.6 %collective-permute-done.2.refs_7_.refs_11_ = bf16[4,2,32,1024]{3,2,1,0:T(8,128)(2,1)S(1)} collective-permute-done((bf16[4,2,32,1024]{3,2,1,0:T(8,128)(2,1)S(1)}, bf16[4,2,32,1024]{3,2,1,0:T(8,128)(2,1)S(1)}, u32[]{:S(2)}, u32[]{:S(2)}) %collective-permute-start.2) | collective-permute-done | bytes 524320 | tf_op jit(solution)/shard_map/ppermute | solution.py:44
  66.4 11.8 %keys_values.1 = (bf16[512,1024]{1,0:T(8,128)(2,1)}, bf16[512,1024]{1,0:T(8,128)(2,1)}, bf16[512,1024]{1,0:T(8,128)(2,1)}, bf16[512,1024]{1,0:T(8,128)(2,1)}, f32[16,64,128]{2,1,0:T(8,128)}) custom-call(s32[8]{0:T(128)} %pad_add_fusion.2.refs_0_, bf16[512,1024]{1,0:T(8,128)(2,1)} %bitcast.136, f32[1,1024]{1,0:T(1,128)} %bitcast.177, f32[512,1]{1,0:T(8,128)} %bitcast.159, ...), custom_call_target="tpu_custom_call" | custom-call | flops 1 | bytes 1 | tf_op jit(solution)/shard_map/keys_values/pallas_call | solution.py:164
  78.2 7.7 %all-to-all-done.1.refs_2_.refs_11_.refs_16_ = bf16[4,3,32,1024]{3,2,1,0:T(8,128)(2,1)S(1)} async-done(((bf16[4,3,32,1024]{3,2,1,0:T(8,128)(2,1)}), bf16[4,3,32,1024]{3,2,1,0:T(8,128)(2,1)S(1)}, u32[]{:S(2)}, u32[]{:S(2)}) %all-to-all-start.1) | async-done | bytes 786464 | tf_op jit(solution)/shard_map/all_to_all | solution.py:90
  87.6 3.5 collective-permute-start.14
  91.7 10.4 %collective-permute-done.14 = bf16[2,528,128]{2,1,0:T(8,128)(2,1)S(1)} collective-permute-done((bf16[2,528,128]{2,1,0:T(8,128)(2,1)S(1)}, bf16[2,528,128]{2,1,0:T(8,128)(2,1)S(1)}, u32[]{:S(2)}, u32[]{:S(2)}) %collective-permute-start.14) | collective-permute-done | bytes 270368 | tf_op jit(solution)/shard_map/ppermute | solution.py:879
  105.3 3.9 collective-permute-start.15
  109.3 3.9 collective-permute-done.15
  115.9 4.3 collective-permute-done.9.refs_5_.refs_14_.refs_19_
  121.1 4.9 %collective-permute-start.16 = (bf16[2,528,128]{2,1,0:T(8,128)(2,1)}, bf16[2,528,128]{2,1,0:T(8,128)(2,1)}, u32[]{:S(2)}, u32[]{:S(2)}) collective-permute-start(bf16[2,528,128]{2,1,0:T(8,128)(2,1)} %pad_maximum_fusion.4), channel_id=1, source_target_pairs={{0,16},{4,20},{8,24},{12,28},{1,17},{5,21},{9,25},{13,29},{2,18},{... | collective-permute-start | bytes 811016 | tf_op jit(solution)/shard_map/ppermute | solution.py:879
  127.5 3.9 collective-permute-done.16
  135.1 9.2 %query_gate.1 = (bf16[512,1024]{1,0:T(8,128)(2,1)}, bf16[512,1024]{1,0:T(8,128)(2,1)}, f32[512,1024]{1,0:T(8,128)}) custom-call(s32[8]{0:T(128)} %pad_add_fusion.2.refs_0_, bf16[512,1024]{1,0:T(8,128)(2,1)} %get-tuple-element.80.refs_1_.refs_2_.refs_9_, bf16[4,3,32,1024]{3,2,1,0:T(8,128)(2,1)} %copy-done, bf16[4,3,32,1024]{3,2,1,0:T(8,128)(2,1)} %copy-done.1, ...), custom_call_target="tpu_custom_call" | custom-call | flops 1 | bytes 1 | tf_op jit(solution)/shard_map/query_gate/pallas_call | solution.py:164
  144.3 15.3 %attend.1 = (f32[512,1024]{1,0:T(8,128)}, bf16[512,1024]{1,0:T(8,128)(2,1)}, f32[512,1024]{1,0:T(8,128)}, bf16[512,1024]{1,0:T(8,128)(2,1)}) custom-call(s32[8]{0:T(128)} %pad_add_fusion.2.refs_0_, bf16[512,1024]{1,0:T(8,128)(2,1)} %get-tuple-element.84.refs_1_.refs_9_.refs_0_, bf16[512,1024]{1,0:T(8,128)(2,1)} %get-tuple-element.82.refs_2_.refs_1_, ...), custom_call_target="tpu_custom_call" | custom-call | flops 1 | bytes 1 | tf_op jit(solution)/shard_map/attend/pallas_call | solution.py:164
  160.2 2.3 collective-permute-done.19.refs_2_
  163.6 17.4 %feed_forward.2 = (bf16[512,1024]{1,0:T(8,128)(2,1)}, bf16[512,1024]{1,0:T(8,128)(2,1)}, bf16[512,1024]{1,0:T(8,128)(2,1)}, bf16[512,1024]{1,0:T(8,128)(2,1)}, b...) custom-call(s32[1]{0:T(128)} %constant.149.clone.1.refs_0_, ...), custom_call_target="tpu_custom_call" | custom-call | flops 1 | bytes 1 | tf_op jit(solution)/shard_map/feed_forward/pallas_call | solution.py:164
  181.6 3.9 collective-permute-done.21.refs_1_.refs_3_
  185.5 3.0 add_convert_fusion.10.refs_1_
  190.5 17.4 %feed_forward.3 = (bf16[512,1024]{1,0:T(8,128)(2,1)}, bf16[512,1024]{1,0:T(8,128)(2,1)}, bf16[512,1024]{1,0:T(8,128)(2,1)}, bf16[512,1024]{1,0:T(8,128)(2,1)}, b...) custom-call(s32[1]{0:T(128)} %constant.149.clone.1.refs_0_, ...), custom_call_target="tpu_custom_call" | custom-call | flops 1 | bytes 1 | tf_op jit(solution)/shard_map/feed_forward/pallas_call | solution.py:164
  208.1 2.7 collective-permute-done.24
  212.9 18.2 %feed_forward_gradients.1 = bf16[8,3,704,128]{3,2,1,0:T(8,128)(2,1)} custom-call(s32[1]{0:T(128)} %constant.149.clone.1.refs_0_, bf16[512,1024]{1,0:T(8,128)(2,1)} %get-tuple-element.91.refs_1_, bf16[512,1024]{1,0:T(8,128)(2,1)} %copy-done.14, bf16[512,1024]{1,0:T(8,128)(2,1)} %copy-done.15, bf16[512,1024]{1,0:T(8,128)(2,1)} %copy-done.17, ...), custom_call_target="tpu_custom_call" | custom-call | flops 89999998976 | bytes 1 | tf_op jit(solution)/shard_map/feed_forward_gradients/pallas_call | solution.py:164
  231.1 6.7 %collective-permute-done.25.refs_2_ = bf16[512,1024]{1,0:T(8,128)(2,1)S(1)} collective-permute-done((bf16[512,1024]{1,0:T(8,128)(2,1)S(1)}, bf16[512,1024]{1,0:T(8,128)(2,1)S(1)}, u32[]{:S(2)}, u32[]{:S(2)}) %collective-permute-start.25) | collective-permute-done | bytes 1048608 | tf_op jit(solution)/shard_map/ppermute | solution.py:44
  238.8 16.2 %middle_back.1 = (f32[512,1024]{1,0:T(8,128)}, bf16[512,1024]{1,0:T(8,128)(2,1)}, bf16[512,1024]{1,0:T(8,128)(2,1)}, bf16[512,1024]{1,0:T(8,128)(2,1)}, f32[16,64,128]{2,1,0:T(8,128)}, /*index=5*/f32[2,1024]{1,0:T(2,128)}) custom-call(s32[8]{0:T(128)} %pad_add_fusion.2.refs_0_, bf16[512,1024]{1,0:T(8,128)(2,1)} %add_convert_fusion.10.refs_1_, ...), custom_call_target="tpu_custom_call" | custom-call | flops 1 | bytes 1 | tf_op jit(solution)/shard_map/middle_back/pallas_call | solution.py:164
  258.1 18.0 %attend_back.1 = (bf16[512,1024]{1,0:T(8,128)(2,1)}, f32[512,1024]{1,0:T(8,128)}, f32[512,1024]{1,0:T(8,128)}) custom-call(bf16[512,1024]{1,0:T(8,128)(2,1)} %get-tuple-element.84.refs_1_.refs_9_.refs_0_, bf16[512,1024]{1,0:T(8,128)(2,1)} %get-tuple-element.82.refs_2_.refs_1_, bf16[512,1024]{1,0:T(8,128)(2,1)} %get-tuple-element.85.refs_3_.refs_2_, ...), custom_call_target="tpu_custom_call" | custom-call | flops 1 | bytes 1 | tf_op jit(solution)/shard_map/attend_back/pallas_call | solution.py:164
  276.1 11.1 %square_gradients.1 = (bf16[4,3,64,1024]{3,2,1,0:T(8,128)(2,1)}, bf16[4,3,64,1024]{3,2,1,0:T(8,128)(2,1)}, bf16[4,3,64,1024]{3,2,1,0:T(8,128)(2,1)}, bf16[4,3,64,1024]{3,2,1,0:T(8,128)(2,1)}) custom-call(s32[4]{0:T(128)} %pad_add_fusion.3.refs_0_, bf16[512,1024]{1,0:T(8,128)(2,1)} %get-tuple-element.117.refs_1_, ...), custom_call_target="tpu_custom_call" | custom-call | flops 1 | bytes 1 | tf_op jit(solution)/shard_map/square_gradients/pallas_call | solution.py:164
  289.5 15.1 %collective-permute-done.31 = bf16[2,528,128]{2,1,0:T(8,128)(2,1)S(1)} collective-permute-done((bf16[2,528,128]{2,1,0:T(8,128)(2,1)S(1)}, bf16[2,528,128]{2,1,0:T(8,128)(2,1)S(1)}, u32[]{:S(2)}, u32[]{:S(2)}) %collective-permute-start.31) | collective-permute-done | bytes 270368 | tf_op jit(solution)/shard_map/ppermute | solution.py:879
  309.1 3.3 add_convert_fusion.2
  312.4 3.3 collective-permute-start.40
  315.7 19.6 %collective-permute-done.32 = bf16[2,528,128]{2,1,0:T(8,128)(2,1)S(1)} collective-permute-done((bf16[2,528,128]{2,1,0:T(8,128)(2,1)S(1)}, bf16[2,528,128]{2,1,0:T(8,128)(2,1)S(1)}, u32[]{:S(2)}, u32[]{:S(2)}) %collective-permute-start.32) | collective-permute-done | bytes 270368 | tf_op jit(solution)/shard_map/ppermute | solution.py:879
  337.3 12.1 %key_value_gradients.1 = (bf16[4,2,64,1024]{3,2,1,0:T(8,128)(2,1)}, bf16[4,2,64,1024]{3,2,1,0:T(8,128)(2,1)}, bf16[4,2,64,1024]{3,2,1,0:T(8,128)(2,1)}, bf16[4,2...) custom-call(s32[4]{0:T(128)} %pad_add_fusion.3.refs_0_, ...), custom_call_target="tpu_custom_call" | custom-call | flops 1 | bytes 1 | tf_op jit(solution)/shard_map/key_value_gradients/pallas_call | solution.py:164
  349.5 2.9 collective-permute-done.33
  353.9 2.0 collective-permute-done.40
  356.0 3.6 add_convert_fusion
  359.6 6.0 %all-to-all-start.2 = ((bf16[4,3,64,1024]{3,2,1,0:T(8,128)(2,1)}), bf16[4,3,64,1024]{3,2,1,0:T(8,128)(2,1)S(1)}, u32[]{:S(2)}, u32[]{:S(2)}) async-start(bf16[4,3,64,1024]{3,2,1,0:T(8,128)(2,1)} %add_convert_fusion), calls=%async_computation.2 | async-start | bytes 3145728 | tf_op jit(solution)/shard_map/all_to_all | solution.py:109
  367.5 16.2 %entry_back.1 = (f32[512,1024]{1,0:T(8,128)}, f32[1,1024]{1,0:T(1,128)}) custom-call(s32[8]{0:T(128)} %pad_add_fusion.2.refs_0_, bf16[512,1024]{1,0:T(8,128)(2,1)} %bitcast.138, f32[1,1024]{1,0:T(1,128)} %bitcast.178, f32[512,1024]{1,0:T(8,128)} %get-tuple-element.134.refs_3_, bf16[512,1024]{1,0:T(8,128)(2,1)} %get-tuple-element.121.refs_5_.refs_4_, ...), custom_call_target="tpu_custom_call" | custom-call | flops 1 | bytes 1 | tf_op jit(solution)/shard_map/entry_back/pallas_call | solution.py:164
  387.3 2.0 collective-permute-done.35
  390.2 3.0 collective-permute-done.36
  395.2 2.7 add_convert_fusion.3
  398.0 3.8 collective-permute-start.47
  401.9 3.0 add_convert_fusion.6
  404.8 3.0 collective-permute-start.38
  407.8 4.0 collective-permute-done.45
  411.9 2.7 collective-permute-done.47
  414.5 9.4 %collective-permute-done.46 = bf16[2,64,1024]{2,1,0:T(8,128)(2,1)S(1)} collective-permute-done((bf16[2,64,1024]{2,1,0:T(8,128)(2,1)S(1)}, bf16[2,64,1024]{2,1,0:T(8,128)(2,1)S(1)}, u32[]{:S(2)}, u32[]{:S(2)}) %collective-permute-start.46) | collective-permute-done | bytes 262176 | tf_op jit(solution)/shard_map/ppermute | solution.py:106
  428.5 4.9 %collective-permute-done.48 = bf16[2,64,1024]{2,1,0:T(8,128)(2,1)S(1)} collective-permute-done((bf16[2,64,1024]{2,1,0:T(8,128)(2,1)S(1)}, bf16[2,64,1024]{2,1,0:T(8,128)(2,1)S(1)}, u32[]{:S(2)}, u32[]{:S(2)}) %collective-permute-start.48) | collective-permute-done | bytes 262176 | tf_op jit(solution)/shard_map/ppermute | solution.py:44
  433.6 8.3 %collective-permute-done.41 = bf16[3,64,1024]{2,1,0:T(8,128)(2,1)S(1)} collective-permute-done((bf16[3,64,1024]{2,1,0:T(8,128)(2,1)S(1)}, bf16[3,64,1024]{2,1,0:T(8,128)(2,1)S(1)}, u32[]{:S(2)}, u32[]{:S(2)}) %collective-permute-start.41) | collective-permute-done | bytes 393248 | tf_op jit(solution)/shard_map/ppermute | solution.py:44
  442.1 8.1 %collective-permute-done.50 = bf16[3,704,128]{2,1,0:T(8,128)(2,1)S(1)} collective-permute-done((bf16[3,704,128]{2,1,0:T(8,128)(2,1)}, bf16[3,704,128]{2,1,0:T(8,128)(2,1)S(1)}, u32[]{:S(2)}, u32[]{:S(2)}) %collective-permute-start.50) | collective-permute-done | bytes 540704 | tf_op jit(solution)/shard_map/ppermute | solution.py:44
  (234 shorter events, 70.9 us)
Async XLA Ops:
  7.2 155.4 %all-gather.3.cloned.1.call-start = ((), (), s32[]{:S(2)}) async-start(), calls=%async_computation.5 | async-start | bytes 4866048 | tf_op jit(solution)/shard_map/all_gather | solution.py:953
  42.2 9.2 %collective-permute-start = (bf16[4,2,32,1024]{3,2,1,0:T(8,128)(2,1)S(1)}, bf16[4,2,32,1024]{3,2,1,0:T(8,128)(2,1)S(1)}, u32[]{:S(2)}, u32[]{:S(2)}) collective-permute-start(bf16[4,2,32,1024]{3,2,1,0:T(8,128)(2,1)S(1)} %all_to_all.15.refs_4_.refs_8_), channel_id=1, source_target_pairs={{0,4},{4,0},{8,12},{12,8},{16,20},{20,16},{24,28},{28,24},{1,5},{5... | collective-permute-start | bytes 1572872 | tf_op jit(solution)/shard_map/ppermute | solution.py:44
  43.9 13.9 %collective-permute-start.1 = (bf16[4,2,32,1024]{3,2,1,0:T(8,128)(2,1)S(1)}, bf16[4,2,32,1024]{3,2,1,0:T(8,128)(2,1)S(1)}, u32[]{:S(2)}, u32[]{:S(2)}) collective-permute-start(bf16[4,2,32,1024]{3,2,1,0:T(8,128)(2,1)S(1)} %all_to_all.15.refs_4_.refs_8_), channel_id=1, source_target_pairs={{0,2},{1,3},{2,0},{3,1},{4,6},{5,7},{6,4},{7,5},{8,10},{9,11},{10,... | collective-permute-start | bytes 1572872 | tf_op jit(solution)/shard_map/ppermute | solution.py:44
  46.5 39.5 %all-to-all-start.1 = ((bf16[4,3,32,1024]{3,2,1,0:T(8,128)(2,1)}), bf16[4,3,32,1024]{3,2,1,0:T(8,128)(2,1)S(1)}, u32[]{:S(2)}, u32[]{:S(2)}) async-start(bf16[4,3,32,1024]{3,2,1,0:T(8,128)(2,1)} %broadcast_in_dim.23), calls=%async_computation.1 | async-start | bytes 1572864 | tf_op jit(solution)/shard_map/all_to_all | solution.py:90
  50.0 376.6 %reduce-scatter.2.cloned.1.call-start = ((), (), s32[]{:S(2)}) async-start(), calls=%async_computation.4 | async-start | bytes 4866048 | tf_op jit(solution)/shard_map/reduce_scatter | solution.py:1012
  51.4 13.0 %collective-permute-start.2 = (bf16[4,2,32,1024]{3,2,1,0:T(8,128)(2,1)S(1)}, bf16[4,2,32,1024]{3,2,1,0:T(8,128)(2,1)S(1)}, u32[]{:S(2)}, u32[]{:S(2)}) collective-permute-start(bf16[4,2,32,1024]{3,2,1,0:T(8,128)(2,1)S(1)} %collective-permute-done.refs_5_.refs_9_), channel_id=1, source_target_pairs={{0,2},{1,3},{2,0},{3,1},{4,6},{5,7},{6,4},{7,5},{8,10},{9,11},{10,... | collective-permute-start | bytes 1572872 | tf_op jit(solution)/shard_map/ppermute | solution.py:44
  53.8 11.7 %collective-permute-start.3 = (bf16[4,2,32,1024]{3,2,1,0:T(8,128)(2,1)S(1)}, bf16[4,2,32,1024]{3,2,1,0:T(8,128)(2,1)S(1)}, u32[]{:S(2)}, u32[]{:S(2)}) collective-permute-start(bf16[4,2,32,1024]{3,2,1,0:T(8,128)(2,1)S(1)} %all_to_all.15.refs_4_.refs_8_), channel_id=1, source_target_pairs={{0,1},{1,0},{2,3},{3,2},{4,5},{5,4},{6,7},{7,6},{8,9},{9,8},{10,11... | collective-permute-start | bytes 1572872 | tf_op jit(solution)/shard_map/ppermute | solution.py:44
  53.8 11.7 %collective-permute-start.4 = (bf16[4,2,32,1024]{3,2,1,0:T(8,128)(2,1)S(1)}, bf16[4,2,32,1024]{3,2,1,0:T(8,128)(2,1)}, u32[]{:S(2)}, u32[]{:S(2)}) collective-permute-start(bf16[4,2,32,1024]{3,2,1,0:T(8,128)(2,1)S(1)} %collective-permute-done.refs_5_.refs_9_), channel_id=1, source_target_pairs={{0,1},{1,0},{2,3},{3,2},{4,5},{5,4},{6,7},{7,6},{8,9},{9,8},{10,11... | collective-permute-start | bytes 1572872 | tf_op jit(solution)/shard_map/ppermute | solution.py:44
  57.8 7.7 %collective-permute-start.5 = (bf16[4,2,32,1024]{3,2,1,0:T(8,128)(2,1)S(1)}, bf16[4,2,32,1024]{3,2,1,0:T(8,128)(2,1)}, u32[]{:S(2)}, u32[]{:S(2)}) collective-permute-start(bf16[4,2,32,1024]{3,2,1,0:T(8,128)(2,1)S(1)} %collective-permute-done.1.refs_6_.refs_10_), channel_id=1, source_target_pairs={{0,1},{1,0},{2,3},{3,2},{4,5},{5,4},{6,7},{7,6},{8,9},{9,8},{10,11... | collective-permute-start | bytes 1572872 | tf_op jit(solution)/shard_map/ppermute | solution.py:44
  85.9 17.4 %collective-permute-start.7 = (bf16[4,3,32,1024]{3,2,1,0:T(8,128)(2,1)S(1)}, bf16[4,3,32,1024]{3,2,1,0:T(8,128)(2,1)S(1)}, u32[]{:S(2)}, u32[]{:S(2)}) collective-permute-start(bf16[4,3,32,1024]{3,2,1,0:T(8,128)(2,1)S(1)} %all-to-all-done.1.refs_2_.refs_11_.refs_16_), channel_id=1, source_target_pairs={{0,4},{4,0},{8,12},{12,8},{16,20},{20,16},{24,28},{28,24},{1,5},{5... | collective-permute-start | bytes 2359304 | tf_op jit(solution)/shard_map/ppermute | solution.py:44
  87.6 14.5 %collective-permute-start.14 = (bf16[2,528,128]{2,1,0:T(8,128)(2,1)S(1)}, bf16[2,528,128]{2,1,0:T(8,128)(2,1)S(1)}, u32[]{:S(2)}, u32[]{:S(2)}) collective-permute-start(bf16[2,528,128]{2,1,0:T(8,128)(2,1)S(1)} %pad_maximum_fusion.2), channel_id=1, source_target_pairs={{0,4},{4,8},{8,12},{12,16},{16,20},{20,24},{24,28},{1,5},{5,9},{9,... | collective-permute-start | bytes 811016 | tf_op jit(solution)/shard_map/ppermute | solution.py:879
  91.3 24.1 %collective-permute-start.8 = (bf16[4,3,32,1024]{3,2,1,0:T(8,128)(2,1)S(1)}, bf16[4,3,32,1024]{3,2,1,0:T(8,128)(2,1)S(1)}, u32[]{:S(2)}, u32[]{:S(2)}) collective-permute-start(bf16[4,3,32,1024]{3,2,1,0:T(8,128)(2,1)S(1)} %all-to-all-done.1.refs_2_.refs_11_.refs_16_), channel_id=1, source_target_pairs={{0,2},{1,3},{2,0},{3,1},{4,6},{5,7},{6,4},{7,5},{8,10},{9,11},{10,... | collective-permute-start | bytes 2359304 | tf_op jit(solution)/shard_map/ppermute | solution.py:44
  103.4 16.8 %collective-permute-start.9 = (bf16[4,3,32,1024]{3,2,1,0:T(8,128)(2,1)S(1)}, bf16[4,3,32,1024]{3,2,1,0:T(8,128)(2,1)S(1)}, u32[]{:S(2)}, u32[]{:S(2)}) collective-permute-start(bf16[4,3,32,1024]{3,2,1,0:T(8,128)(2,1)S(1)} %collective-permute-done.7.refs_3_.refs_12_.refs_17_), channel_id=1, source_target_pairs={{0,2},{1,3},{2,0},{3,1},{4,6},{5,7},{6,4},{7,5},{8,10},{9,11},{10,... | collective-permute-start | bytes 2359304 | tf_op jit(solution)/shard_map/ppermute | solution.py:44
  105.3 7.9 %collective-permute-start.15 = (bf16[2,528,128]{2,1,0:T(8,128)(2,1)S(1)}, bf16[2,528,128]{2,1,0:T(8,128)(2,1)S(1)}, u32[]{:S(2)}, u32[]{:S(2)}) collective-permute-start(bf16[2,528,128]{2,1,0:T(8,128)(2,1)S(1)} %pad_maximum_fusion.3), channel_id=1, source_target_pairs={{0,8},{4,12},{8,16},{12,20},{16,24},{20,28},{1,9},{5,13},{9,17},{1... | collective-permute-start | bytes 811016 | tf_op jit(solution)/shard_map/ppermute | solution.py:879
  109.2 24.1 %collective-permute-start.10 = (bf16[4,3,32,1024]{3,2,1,0:T(8,128)(2,1)S(1)}, bf16[4,3,32,1024]{3,2,1,0:T(8,128)(2,1)}, u32[]{:S(2)}, u32[]{:S(2)}) collective-permute-start(bf16[4,3,32,1024]{3,2,1,0:T(8,128)(2,1)S(1)} %all-to-all-done.1.refs_2_.refs_11_.refs_16_), channel_id=1, source_target_pairs={{0,1},{1,0},{2,3},{3,2},{4,5},{5,4},{6,7},{7,6},{8,9},{9,8},{10,11... | collective-permute-start | bytes 2359304 | tf_op jit(solution)/shard_map/ppermute | solution.py:44
  115.3 19.8 %collective-permute-start.11 = (bf16[4,3,32,1024]{3,2,1,0:T(8,128)(2,1)S(1)}, bf16[4,3,32,1024]{3,2,1,0:T(8,128)(2,1)}, u32[]{:S(2)}, u32[]{:S(2)}) collective-permute-start(bf16[4,3,32,1024]{3,2,1,0:T(8,128)(2,1)S(1)} %collective-permute-done.7.refs_3_.refs_12_.refs_17_), channel_id=1, source_target_pairs={{0,1},{1,0},{2,3},{3,2},{4,5},{5,4},{6,7},{7,6},{8,9},{9,8},{10,11... | collective-permute-start | bytes 2359304 | tf_op jit(solution)/shard_map/ppermute | solution.py:44
  115.4 19.7 %collective-permute-start.12 = (bf16[4,3,32,1024]{3,2,1,0:T(8,128)(2,1)S(1)}, bf16[4,3,32,1024]{3,2,1,0:T(8,128)(2,1)}, u32[]{:S(2)}, u32[]{:S(2)}) collective-permute-start(bf16[4,3,32,1024]{3,2,1,0:T(8,128)(2,1)S(1)} %collective-permute-done.8.refs_4_.refs_13_.refs_18_), channel_id=1, source_target_pairs={{0,1},{1,0},{2,3},{3,2},{4,5},{5,4},{6,7},{7,6},{8,9},{9,8},{10,11... | collective-permute-start | bytes 2359304 | tf_op jit(solution)/shard_map/ppermute | solution.py:44
  120.2 14.9 %collective-permute-start.13 = (bf16[4,3,32,1024]{3,2,1,0:T(8,128)(2,1)S(1)}, bf16[4,3,32,1024]{3,2,1,0:T(8,128)(2,1)}, u32[]{:S(2)}, u32[]{:S(2)}) collective-permute-start(bf16[4,3,32,1024]{3,2,1,0:T(8,128)(2,1)S(1)} %collective-permute-done.9.refs_5_.refs_14_.refs_19_), channel_id=1, source_target_pairs={{0,1},{1,0},{2,3},{3,2},{4,5},{5,4},{6,7},{7,6},{8,9},{9,8},{10,11... | collective-permute-start | bytes 2359304 | tf_op jit(solution)/shard_map/ppermute | solution.py:44
  121.1 10.3 %collective-permute-start.16 = (bf16[2,528,128]{2,1,0:T(8,128)(2,1)}, bf16[2,528,128]{2,1,0:T(8,128)(2,1)}, u32[]{:S(2)}, u32[]{:S(2)}) collective-permute-start(bf16[2,528,128]{2,1,0:T(8,128)(2,1)} %pad_maximum_fusion.4), channel_id=1, source_target_pairs={{0,16},{4,20},{8,24},{12,28},{1,17},{5,21},{9,25},{13,29},{2,18},{... | collective-permute-start | bytes 811016 | tf_op jit(solution)/shard_map/ppermute | solution.py:879
  131.4 28.9 %collective-permute-start.18 = (bf16[512,1024]{1,0:T(8,128)(2,1)}, bf16[512,1024]{1,0:T(8,128)(2,1)}, u32[]{:S(2)}, u32[]{:S(2)}) collective-permute-start(bf16[512,1024]{1,0:T(8,128)(2,1)} %bitcast.149), channel_id=1, source_target_pairs={{0,1},{1,0},{2,3},{3,2},{4,5},{5,4},{6,7},{7,6},{8,9},{9,8},{10,11... | collective-permute-start | bytes 3145736 | tf_op jit(solution)/shard_map/ppermute | solution.py:44
  133.3 26.9 %collective-permute-start.17 = (bf16[512,1024]{1,0:T(8,128)(2,1)}, bf16[512,1024]{1,0:T(8,128)(2,1)}, u32[]{:S(2)}, u32[]{:S(2)}) collective-permute-start(bf16[512,1024]{1,0:T(8,128)(2,1)} %bitcast.150), channel_id=1, source_target_pairs={{0,2},{1,3},{2,0},{3,1},{4,6},{5,7},{6,4},{7,5},{8,10},{9,11},{10,... | collective-permute-start | bytes 3145736 | tf_op jit(solution)/shard_map/ppermute | solution.py:44
  159.9 25.6 %collective-permute-start.21 = (bf16[512,1024]{1,0:T(8,128)(2,1)}, bf16[512,1024]{1,0:T(8,128)(2,1)S(1)}, u32[]{:S(2)}, u32[]{:S(2)}) collective-permute-start(bf16[512,1024]{1,0:T(8,128)(2,1)} %get-tuple-element.91.refs_1_), channel_id=1, source_target_pairs={{0,2},{1,3},{2,0},{3,1},{4,6},{5,7},{6,4},{7,5},{8,10},{9,11},{10,... | collective-permute-start | bytes 3145736 | tf_op jit(solution)/shard_map/ppermute | solution.py:44
  181.0 4.5 collective-permute-start.20
  181.3 7.2 %collective-permute-start.23 = (bf16[512,1024]{1,0:T(8,128)(2,1)}, bf16[512,1024]{1,0:T(8,128)(2,1)S(1)}, u32[]{:S(2)}, u32[]{:S(2)}) collective-permute-start(bf16[512,1024]{1,0:T(8,128)(2,1)} %collective-permute-done.17.refs_3_.refs_7_), channel_id=1, source_target_pairs={{0,1},{1,0},{2,3},{3,2},{4,5},{5,4},{6,7},{7,6},{8,9},{9,8},{10,11... | collective-permute-start | bytes 3145736 | tf_op jit(solution)/shard_map/ppermute | solution.py:44
  212.5 25.3 %collective-permute-start.25 = (bf16[512,1024]{1,0:T(8,128)(2,1)S(1)}, bf16[512,1024]{1,0:T(8,128)(2,1)S(1)}, u32[]{:S(2)}, u32[]{:S(2)}) collective-permute-start(bf16[512,1024]{1,0:T(8,128)(2,1)S(1)} %add_convert_fusion.9), channel_id=1, source_target_pairs={{0,2},{1,3},{2,0},{3,1},{4,6},{5,7},{6,4},{7,5},{8,10},{9,11},{10,... | collective-permute-start | bytes 3145736 | tf_op jit(solution)/shard_map/ppermute | solution.py:44
  256.1 20.0 %collective-permute-start.29 = (bf16[2,528,128]{2,1,0:T(8,128)(2,1)S(1)}, bf16[2,528,128]{2,1,0:T(8,128)(2,1)S(1)}, u32[]{:S(2)}, u32[]{:S(2)}) collective-permute-start(bf16[2,528,128]{2,1,0:T(8,128)(2,1)S(1)} %pad_maximum_fusion.1), channel_id=1, source_target_pairs={{4,0},{8,4},{12,8},{16,12},{20,16},{24,20},{28,24},{5,1},{9,5},{13... | collective-permute-start | bytes 811016 | tf_op jit(solution)/shard_map/ppermute | solution.py:879
  257.4 48.0 %collective-permute-start.27 = (bf16[512,1024]{1,0:T(8,128)(2,1)}, bf16[512,1024]{1,0:T(8,128)(2,1)}, u32[]{:S(2)}, u32[]{:S(2)}) collective-permute-start(bf16[512,1024]{1,0:T(8,128)(2,1)} %get-tuple-element.114), channel_id=1, source_target_pairs={{0,1},{1,0},{2,3},{3,2},{4,5},{5,4},{6,7},{7,6},{8,9},{9,8},{10,11... | collective-permute-start | bytes 3145736 | tf_op jit(solution)/shard_map/ppermute | solution.py:44
  287.3 21.8 %collective-permute-start.30 = (bf16[4,3,64,1024]{3,2,1,0:T(8,128)(2,1)}, bf16[4,3,64,1024]{3,2,1,0:T(8,128)(2,1)}, u32[]{:S(2)}, u32[]{:S(2)}) collective-permute-start(bf16[4,3,64,1024]{3,2,1,0:T(8,128)(2,1)} %get-tuple-element.123), channel_id=1, source_target_pairs={{0,1},{1,0},{2,3},{3,2},{4,5},{5,4},{6,7},{7,6},{8,9},{9,8},{10,11... | collective-permute-start | bytes 4718600 | tf_op jit(solution)/shard_map/ppermute | solution.py:44
  288.1 16.5 %collective-permute-start.31 = (bf16[2,528,128]{2,1,0:T(8,128)(2,1)S(1)}, bf16[2,528,128]{2,1,0:T(8,128)(2,1)S(1)}, u32[]{:S(2)}, u32[]{:S(2)}) collective-permute-start(bf16[2,528,128]{2,1,0:T(8,128)(2,1)S(1)} %pad_maximum_fusion.5), channel_id=1, source_target_pairs={{8,0},{12,4},{16,8},{20,12},{24,16},{28,20},{9,1},{13,5},{17,9},{2... | collective-permute-start | bytes 811016 | tf_op jit(solution)/shard_map/ppermute | solution.py:879
  289.4 66.6 %collective-permute-start.39 = (bf16[4,3,64,1024]{3,2,1,0:T(8,128)(2,1)}, bf16[4,3,64,1024]{3,2,1,0:T(8,128)(2,1)S(1)}, u32[]{:S(2)}, u32[]{:S(2)}) collective-permute-start(bf16[4,3,64,1024]{3,2,1,0:T(8,128)(2,1)} %get-tuple-element.140), channel_id=1, source_target_pairs={{0,1},{1,0},{2,3},{3,2},{4,5},{5,4},{6,7},{7,6},{8,9},{9,8},{10,11... | collective-permute-start | bytes 4718600 | tf_op jit(solution)/shard_map/ppermute | solution.py:44
  307.2 29.1 %collective-permute-start.28 = (bf16[512,1024]{1,0:T(8,128)(2,1)S(1)}, bf16[512,1024]{1,0:T(8,128)(2,1)S(1)}, u32[]{:S(2)}, u32[]{:S(2)}) collective-permute-start(bf16[512,1024]{1,0:T(8,128)(2,1)S(1)} %add_convert_fusion.7), channel_id=1, source_target_pairs={{0,2},{1,3},{2,0},{3,1},{4,6},{5,7},{6,4},{7,5},{8,10},{9,11},{10,... | collective-permute-start | bytes 3145736 | tf_op jit(solution)/shard_map/ppermute | solution.py:44
  307.8 27.6 %collective-permute-start.32 = (bf16[2,528,128]{2,1,0:T(8,128)(2,1)S(1)}, bf16[2,528,128]{2,1,0:T(8,128)(2,1)S(1)}, u32[]{:S(2)}, u32[]{:S(2)}) collective-permute-start(bf16[2,528,128]{2,1,0:T(8,128)(2,1)S(1)} %pad_maximum_fusion.6), channel_id=1, source_target_pairs={{16,0},{20,4},{24,8},{28,12},{17,1},{21,5},{25,9},{29,13},{18,2},{... | collective-permute-start | bytes 811016 | tf_op jit(solution)/shard_map/ppermute | solution.py:879
  312.4 43.6 %collective-permute-start.40 = (bf16[4,3,64,1024]{3,2,1,0:T(8,128)(2,1)}, bf16[4,3,64,1024]{3,2,1,0:T(8,128)(2,1)}, u32[]{:S(2)}, u32[]{:S(2)}) collective-permute-start(bf16[4,3,64,1024]{3,2,1,0:T(8,128)(2,1)} %add_convert_fusion.2), channel_id=1, source_target_pairs={{0,4},{4,0},{8,12},{12,8},{16,20},{20,16},{24,28},{28,24},{1,5},{5... | collective-permute-start | bytes 4718600 | tf_op jit(solution)/shard_map/ppermute | solution.py:44
  359.6 66.0 %all-to-all-start.2 = ((bf16[4,3,64,1024]{3,2,1,0:T(8,128)(2,1)}), bf16[4,3,64,1024]{3,2,1,0:T(8,128)(2,1)S(1)}, u32[]{:S(2)}, u32[]{:S(2)}) async-start(bf16[4,3,64,1024]{3,2,1,0:T(8,128)(2,1)} %add_convert_fusion), calls=%async_computation.2 | async-start | bytes 3145728 | tf_op jit(solution)/shard_map/all_to_all | solution.py:109
  365.6 29.5 %collective-permute-start.44 = (bf16[4,2,64,1024]{3,2,1,0:T(8,128)(2,1)S(1)}, bf16[4,2,64,1024]{3,2,1,0:T(8,128)(2,1)}, u32[]{:S(2)}, u32[]{:S(2)}) collective-permute-start(bf16[4,2,64,1024]{3,2,1,0:T(8,128)(2,1)S(1)} %add_convert_fusion.5), channel_id=1, source_target_pairs={{0,4},{4,0},{8,12},{12,8},{16,20},{20,16},{24,28},{28,24},{1,5},{5... | collective-permute-start | bytes 3145736 | tf_op jit(solution)/shard_map/ppermute | solution.py:44
  367.0 28.2 %collective-permute-start.43 = (bf16[4,2,64,1024]{3,2,1,0:T(8,128)(2,1)}, bf16[4,2,64,1024]{3,2,1,0:T(8,128)(2,1)}, u32[]{:S(2)}, u32[]{:S(2)}) collective-permute-start(bf16[4,2,64,1024]{3,2,1,0:T(8,128)(2,1)} %get-tuple-element.143), channel_id=1, source_target_pairs={{0,1},{1,0},{2,3},{3,2},{4,5},{5,4},{6,7},{7,6},{8,9},{9,8},{10,11... | collective-permute-start | bytes 3145736 | tf_op jit(solution)/shard_map/ppermute | solution.py:44
  367.0 34.8 %collective-permute-start.26 = (bf16[512,1024]{1,0:T(8,128)(2,1)}, bf16[512,1024]{1,0:T(8,128)(2,1)}, u32[]{:S(2)}, u32[]{:S(2)}) collective-permute-start(bf16[512,1024]{1,0:T(8,128)(2,1)} %get-tuple-element.111), channel_id=1, source_target_pairs={{0,1},{1,0},{2,3},{3,2},{4,5},{5,4},{6,7},{7,6},{8,9},{9,8},{10,11... | collective-permute-start | bytes 3145736 | tf_op jit(solution)/shard_map/ppermute | solution.py:44
  385.6 3.7 collective-permute-start.35
  393.1 11.7 %collective-permute-start.37 = (f32[3,1024]{1,0:T(4,128)S(1)}, f32[3,1024]{1,0:T(4,128)S(1)}, u32[]{:S(2)}, u32[]{:S(2)}) collective-permute-start(f32[3,1024]{1,0:T(4,128)S(1)} %add.220), channel_id=1, source_target_pairs={{0,8},{4,12},{8,0},{12,4},{16,24},{20,28},{24,16},{28,20},{1,9},{5... | collective-permute-start | bytes 36872 | tf_op jit(solution)/shard_map/ppermute | solution.py:44
  398.0 13.9 %collective-permute-start.45 = (bf16[2,64,1024]{2,1,0:T(8,128)(2,1)S(1)}, bf16[2,64,1024]{2,1,0:T(8,128)(2,1)S(1)}, u32[]{:S(2)}, u32[]{:S(2)}) collective-permute-start(bf16[2,64,1024]{2,1,0:T(8,128)(2,1)S(1)} %get-tuple-element.208), channel_id=1, source_target_pairs={{0,8},{4,12},{8,0},{12,4},{16,24},{20,28},{24,16},{28,20},{1,9},{5... | collective-permute-start | bytes 786440 | tf_op jit(solution)/shard_map/ppermute | solution.py:106
  398.0 16.5 %collective-permute-start.47 = (bf16[2,64,1024]{2,1,0:T(8,128)(2,1)S(1)}, bf16[2,64,1024]{2,1,0:T(8,128)(2,1)S(1)}, u32[]{:S(2)}, u32[]{:S(2)}) collective-permute-start(bf16[2,64,1024]{2,1,0:T(8,128)(2,1)S(1)} %get-tuple-element.209), channel_id=1, source_target_pairs={{0,24},{4,28},{8,16},{12,20},{16,8},{20,12},{24,0},{28,4},{1,25},{... | collective-permute-start | bytes 786440 | tf_op jit(solution)/shard_map/ppermute | solution.py:106
  401.8 22.1 %collective-permute-start.46 = (bf16[2,64,1024]{2,1,0:T(8,128)(2,1)S(1)}, bf16[2,64,1024]{2,1,0:T(8,128)(2,1)S(1)}, u32[]{:S(2)}, u32[]{:S(2)}) collective-permute-start(bf16[2,64,1024]{2,1,0:T(8,128)(2,1)S(1)} %get-tuple-element.210), channel_id=1, source_target_pairs={{0,16},{4,20},{8,24},{12,28},{16,0},{20,4},{24,8},{28,12},{1,17},{... | collective-permute-start | bytes 786440 | tf_op jit(solution)/shard_map/ppermute | solution.py:106
  404.8 20.7 %collective-permute-start.38 = (f32[3,1024]{1,0:T(4,128)S(1)}, f32[3,1024]{1,0:T(4,128)S(1)}, u32[]{:S(2)}, u32[]{:S(2)}) collective-permute-start(f32[3,1024]{1,0:T(4,128)S(1)} %add.221), channel_id=1, source_target_pairs={{0,16},{4,20},{8,24},{12,28},{16,0},{20,4},{24,8},{28,12},{1,17},{... | collective-permute-start | bytes 36872 | tf_op jit(solution)/shard_map/ppermute | solution.py:44
  424.1 9.3 %collective-permute-start.48 = (bf16[2,64,1024]{2,1,0:T(8,128)(2,1)S(1)}, bf16[2,64,1024]{2,1,0:T(8,128)(2,1)S(1)}, u32[]{:S(2)}, u32[]{:S(2)}) collective-permute-start(bf16[2,64,1024]{2,1,0:T(8,128)(2,1)S(1)} %fusion.14), channel_id=1, source_target_pairs={{0,2},{1,3},{2,0},{3,1},{4,6},{5,7},{6,4},{7,5},{8,10},{9,11},{10,... | collective-permute-start | bytes 786440 | tf_op jit(solution)/shard_map/ppermute | solution.py:44
  425.9 15.9 %collective-permute-start.41 = (bf16[3,64,1024]{2,1,0:T(8,128)(2,1)S(1)}, bf16[3,64,1024]{2,1,0:T(8,128)(2,1)S(1)}, u32[]{:S(2)}, u32[]{:S(2)}) collective-permute-start(bf16[3,64,1024]{2,1,0:T(8,128)(2,1)S(1)} %reduce_sum.12), channel_id=1, source_target_pairs={{0,2},{1,3},{2,0},{3,1},{4,6},{5,7},{6,4},{7,5},{8,10},{9,11},{10,... | collective-permute-start | bytes 1179656 | tf_op jit(solution)/shard_map/ppermute | solution.py:44
  426.6 23.6 %collective-permute-start.50 = (bf16[3,704,128]{2,1,0:T(8,128)(2,1)}, bf16[3,704,128]{2,1,0:T(8,128)(2,1)S(1)}, u32[]{:S(2)}, u32[]{:S(2)}) collective-permute-start(bf16[3,704,128]{2,1,0:T(8,128)(2,1)} %bitcast.162), channel_id=1, source_target_pairs={{0,2},{1,3},{2,0},{3,1},{4,6},{5,7},{6,4},{7,5},{8,10},{9,11},{10,... | collective-permute-start | bytes 1622024 | tf_op jit(solution)/shard_map/ppermute | solution.py:44
  433.5 17.0 %collective-permute-start.49 = (bf16[2,64,1024]{2,1,0:T(8,128)(2,1)S(1)}, bf16[2,64,1024]{2,1,0:T(8,128)(2,1)S(1)}, u32[]{:S(2)}, u32[]{:S(2)}) collective-permute-start(bf16[2,64,1024]{2,1,0:T(8,128)(2,1)S(1)} %add_convert_fusion.12), channel_id=1, source_target_pairs={{0,1},{1,0},{2,3},{3,2},{4,5},{5,4},{6,7},{7,6},{8,9},{9,8},{10,11... | collective-permute-start | bytes 786440 | tf_op jit(solution)/shard_map/ppermute | solution.py:44
  442.0 8.6 %collective-permute-start.42 = (bf16[3,64,1024]{2,1,0:T(8,128)(2,1)S(1)}, bf16[3,64,1024]{2,1,0:T(8,128)(2,1)S(1)}, u32[]{:S(2)}, u32[]{:S(2)}) collective-permute-start(bf16[3,64,1024]{2,1,0:T(8,128)(2,1)S(1)} %add_convert_fusion.11), channel_id=1, source_target_pairs={{0,1},{1,0},{2,3},{3,2},{4,5},{5,4},{6,7},{7,6},{8,9},{9,8},{10,11... | collective-permute-start | bytes 1179656 | tf_op jit(solution)/shard_map/ppermute | solution.py:44
  (42 other events, 428.0 us)
Sparse Core Ops, SparseCore 0:
  11.3 90.3 all-gather.2
  237.9 106.3 reduce-scatter.1

commit v4 on v3

--- a/solution.py
+++ b/solution.py
@@ -17,7 +17,7 @@
 ANY = pl.BlockSpec(memory_space=pl.ANY)
 STAGE = None
 DEAR = {'feed_forward_gradients': 90}
-WAITS = {'first': (), 'qgoz': ('kvz',), 'qgox': ('kvk',), 'qgon': ('kvk',), 'ffg': ('kvx',), 'kvn': (), 'ffa': ('up', 'upb'), 'att': (), 'nmd': ('ffa',), 'ffb': ('bo',), 'ffr': ('bt',), 'fs': ('bg',), 'mid': ('ffr',), 'mo': ('mid',), 'mt1': ('mid',), 's2': ('inn',), 'gra': ('s1',), 's3': ('gra',), 'out': ('oc', 'mg'), 'ent': ('kc',), 'ks': ('ent',), 'os': ('kc',), 'fw': ('ks',), 'up': ('kvf',)}
+WAITS = {'first': (), 'qgoz': ('kvz',), 'qgox': ('kvk',), 'qgon': ('kvk',), 'ffg': ('kvx',), 'kvn': (), 'ffa': ('up', 'upb'), 'att': (), 'nmd': ('ffa',), 'ffb': ('bo',), 'ffr': ('bt',), 'fs': ('bg',), 'mid': ('ffr',), 'mo': ('mid',), 'mt1': ('mid',), 's2': ('inn',), 'gra': ('s1',), 's3': ('gra',), 'out': ('oc', 'mg'), 'ent': ('kc',), 'ks': ('ent',), 'os': ('kc',), 'fw': ('ks',), 'up': ('kvf',), 'of': ('fw',)}
 
 
 def cost(name):
@@ -792,17 +792,15 @@
 
     flush(4, 5, 6)
 
-    for h in range(2):
-
-        def through(j, _, h=h):
+    def through(j, _):
+        for h in range(2):
             rows = pl.ds(h * count, count)
             mixed_refs[h][:, block(j)] = dot(joined_s[rows, :], weight[2, :, block(j)]).astype(BF)
             back = dot(left_s[rows, :], weight[0, :, block(j)]) + dot(right_s[rows, :], weight[1, :, block(j)])
             back_refs[h][:, block(j)] = back.astype(BF)
-            return 0
-
-        lax.fori_loop(0, d // 256, through, 0)
-        flush(h, 2 + h)
+        return 0
+
+    lax.fori_loop(0, d // 256, through, 0)
 
 
 def ff_call(bases, nm, up, pieces):

time: 471 us -> 461 us (0.979)
  waiting for transfers between devices: 142 us -> 132 us
    ppermute x43, waiting for transfers between devices: 65.4 us -> 49.4 us  [swap(): return lax.ppermute(value, axis, [(i, i ^ bit) for i in range(size)])]
    ppermute x3, waiting for transfers between devices: 16.1 us -> 21.4 us  [sum_along(): total = total + lax.ppermute(sent, 'seq', pairs).astype(F32)]
  transfers between devices with their start and end apart: 56 -> 56, of which waited for: 27 -> 26; matrix products, arithmetic and copies ran while one was open for 8% -> 9% of each run, Pallas kernels for 31% -> 32%
where the time goes in v4:
time: 461 us; the launch traced here: 455 us
  Pallas kernels  162 us (35%)
  waiting for transfers between devices  132 us (29%)
  starting transfers between devices  57 us (12%)
  other arithmetic  37.4 us (8%)
  blocking collectives  30.8 us (7%)
  local copies, waits for them, and re-layouts  21.3 us (5%)
  between operations  15.2 us (3%)
    pallas_call x11, Pallas kernels, call(): pl.pallas_call(kernel, out_shape=out_shape, in_specs=[ANY if spec is STAG...  162 us
    ppermute x6, waiting for transfers between devices, step(): lax.ppermute(sent, 'seq', beyond(self.order, self.reach, self.size))  53 us
    ppermute x43, waiting for transfers between devices, swap(): return lax.ppermute(value, axis, [(i, i ^ bit) for i in range(size)])  49.4 us
    all_to_all x1, blocking collectives, along(): return lax.all_to_all(copies, 'seq', 0, 0, axis_index_groups=self.groups)  30.8 us
    ppermute x43, starting transfers between devices, swap(): return lax.ppermute(value, axis, [(i, i ^ bit) for i in range(size)])  27.4 us
    ppermute x3, waiting for transfers between devices, sum_along(): total = total + lax.ppermute(sent, 'seq', pairs).astype(F32)  21.4 us
    convert_element_type x9, other arithmetic, add(): return (left.astype(F32) + right.astype(F32)).astype(BF)  18.6 us
    ppermute x6, starting transfers between devices, step(): lax.ppermute(sent, 'seq', beyond(self.order, self.reach, self.size))  16.2 us
  transfers between devices with their start and end apart: 56, of which 26 were waited for; matrix products, arithmetic and copies ran while one was open for 9% of the time, Pallas kernels for 32%

profile of v4, /device:TPU:0, one launch (start us, length us, event | category | flops | bytes accessed | tf_op | source)
XLA Modules:
  0.0 455.2 jit_solution(5786797525168445776)
XLA Ops:
  11.4 30.8 %all_to_all.15.refs_4_.refs_8_ = bf16[4,2,32,1024]{3,2,1,0:T(8,128)(2,1)S(1)} all-to-all(bf16[4,2,32,1024]{3,2,1,0:T(8,128)(2,1)S(1)} %broadcast_in_dim.22), channel_id=1, replica_groups={{0,8,16,24},{4,12,20,28},{1,9,17,25},{5,13,21,29},{2,10,18,26},{6,14,22..., dimensions={0} | all-to-all | bytes 1048576 | tf_op jit(solution)/shard_map/all_to_all | solution.py:90
  46.5 3.5 all-to-all-start.1
  54.3 3.5 collective-permute-done.1.refs_6_.refs_10_
  57.8 6.6 %collective-permute-done.2.refs_7_.refs_11_ = bf16[4,2,32,1024]{3,2,1,0:T(8,128)(2,1)S(1)} collective-permute-done((bf16[4,2,32,1024]{3,2,1,0:T(8,128)(2,1)S(1)}, bf16[4,2,32,1024]{3,2,1,0:T(8,128)(2,1)S(1)}, u32[]{:S(2)}, u32[]{:S(2)}) %collective-permute-start.2) | collective-permute-done | bytes 524320 | tf_op jit(solution)/shard_map/ppermute | solution.py:44
  66.4 11.8 %keys_values.1 = (bf16[512,1024]{1,0:T(8,128)(2,1)}, bf16[512,1024]{1,0:T(8,128)(2,1)}, bf16[512,1024]{1,0:T(8,128)(2,1)}, bf16[512,1024]{1,0:T(8,128)(2,1)}, f32[16,64,128]{2,1,0:T(8,128)}) custom-call(s32[8]{0:T(128)} %pad_add_fusion.2.refs_0_, bf16[512,1024]{1,0:T(8,128)(2,1)} %bitcast.136, f32[1,1024]{1,0:T(1,128)} %bitcast.177, f32[512,1]{1,0:T(8,128)} %bitcast.159, ...), custom_call_target="tpu_custom_call" | custom-call | flops 1 | bytes 1 | tf_op jit(solution)/shard_map/keys_values/pallas_call | solution.py:164
  78.2 7.7 %all-to-all-done.1.refs_2_.refs_11_.refs_16_ = bf16[4,3,32,1024]{3,2,1,0:T(8,128)(2,1)S(1)} async-done(((bf16[4,3,32,1024]{3,2,1,0:T(8,128)(2,1)}), bf16[4,3,32,1024]{3,2,1,0:T(8,128)(2,1)S(1)}, u32[]{:S(2)}, u32[]{:S(2)}) %all-to-all-start.1) | async-done | bytes 786464 | tf_op jit(solution)/shard_map/all_to_all | solution.py:90
  87.6 3.5 collective-permute-start.14
  91.7 10.4 %collective-permute-done.14 = bf16[2,528,128]{2,1,0:T(8,128)(2,1)S(1)} collective-permute-done((bf16[2,528,128]{2,1,0:T(8,128)(2,1)S(1)}, bf16[2,528,128]{2,1,0:T(8,128)(2,1)S(1)}, u32[]{:S(2)}, u32[]{:S(2)}) %collective-permute-start.14) | collective-permute-done | bytes 270368 | tf_op jit(solution)/shard_map/ppermute | solution.py:877
  105.3 3.9 collective-permute-start.15
  109.3 3.9 collective-permute-done.15
  115.9 4.3 collective-permute-done.9.refs_5_.refs_14_.refs_19_
  121.1 4.9 %collective-permute-start.16 = (bf16[2,528,128]{2,1,0:T(8,128)(2,1)}, bf16[2,528,128]{2,1,0:T(8,128)(2,1)}, u32[]{:S(2)}, u32[]{:S(2)}) collective-permute-start(bf16[2,528,128]{2,1,0:T(8,128)(2,1)} %pad_maximum_fusion.4), channel_id=1, source_target_pairs={{0,16},{4,20},{8,24},{12,28},{1,17},{5,21},{9,25},{13,29},{2,18},{... | collective-permute-start | bytes 811016 | tf_op jit(solution)/shard_map/ppermute | solution.py:877
  127.5 3.9 collective-permute-done.16
  131.4 1.9 fusion.4
  135.1 9.2 %query_gate.1 = (bf16[512,1024]{1,0:T(8,128)(2,1)}, bf16[512,1024]{1,0:T(8,128)(2,1)}, f32[512,1024]{1,0:T(8,128)}) custom-call(s32[8]{0:T(128)} %pad_add_fusion.2.refs_0_, bf16[512,1024]{1,0:T(8,128)(2,1)} %get-tuple-element.81.refs_1_.refs_2_.refs_9_, bf16[4,3,32,1024]{3,2,1,0:T(8,128)(2,1)} %copy-done, bf16[4,3,32,1024]{3,2,1,0:T(8,128)(2,1)} %copy-done.1, ...), custom_call_target="tpu_custom_call" | custom-call | flops 1 | bytes 1 | tf_op jit(solution)/shard_map/query_gate/pallas_call | solution.py:164
  144.3 15.3 %attend.1 = (f32[512,1024]{1,0:T(8,128)}, bf16[512,1024]{1,0:T(8,128)(2,1)}, f32[512,1024]{1,0:T(8,128)}, bf16[512,1024]{1,0:T(8,128)(2,1)}) custom-call(s32[8]{0:T(128)} %pad_add_fusion.2.refs_0_, bf16[512,1024]{1,0:T(8,128)(2,1)} %get-tuple-element.85.refs_1_.refs_9_.refs_0_, bf16[512,1024]{1,0:T(8,128)(2,1)} %get-tuple-element.83.refs_2_.refs_1_, ...), custom_call_target="tpu_custom_call" | custom-call | flops 1 | bytes 1 | tf_op jit(solution)/shard_map/attend/pallas_call | solution.py:164
  160.2 2.3 collective-permute-done.19.refs_2_
  163.5 16.8 %feed_forward.2 = (bf16[512,1024]{1,0:T(8,128)(2,1)}, bf16[512,1024]{1,0:T(8,128)(2,1)}, bf16[512,1024]{1,0:T(8,128)(2,1)}, bf16[512,1024]{1,0:T(8,128)(2,1)}, b...) custom-call(s32[1]{0:T(128)} %constant.149.clone.1.refs_0_, ...), custom_call_target="tpu_custom_call" | custom-call | flops 1 | bytes 1 | tf_op jit(solution)/shard_map/feed_forward/pallas_call | solution.py:164
  180.9 4.5 collective-permute-done.21.refs_1_.refs_3_
  185.5 3.0 add_convert_fusion.10.refs_1_
  190.5 16.9 %feed_forward.3 = (bf16[512,1024]{1,0:T(8,128)(2,1)}, bf16[512,1024]{1,0:T(8,128)(2,1)}, bf16[512,1024]{1,0:T(8,128)(2,1)}, bf16[512,1024]{1,0:T(8,128)(2,1)}, b...) custom-call(s32[1]{0:T(128)} %constant.149.clone.1.refs_0_, ...), custom_call_target="tpu_custom_call" | custom-call | flops 1 | bytes 1 | tf_op jit(solution)/shard_map/feed_forward/pallas_call | solution.py:164
  207.5 2.7 collective-permute-done.24
  212.3 18.1 %feed_forward_gradients.1 = bf16[8,3,704,128]{3,2,1,0:T(8,128)(2,1)} custom-call(s32[1]{0:T(128)} %constant.149.clone.1.refs_0_, bf16[512,1024]{1,0:T(8,128)(2,1)} %get-tuple-element.92.refs_1_, bf16[512,1024]{1,0:T(8,128)(2,1)} %copy-done.14, bf16[512,1024]{1,0:T(8,128)(2,1)} %copy-done.15, bf16[512,1024]{1,0:T(8,128)(2,1)} %copy-done.17, ...), custom_call_target="tpu_custom_call" | custom-call | flops 89999998976 | bytes 1 | tf_op jit(solution)/shard_map/feed_forward_gradients/pallas_call | solution.py:164
  230.4 6.8 %collective-permute-done.25.refs_2_ = bf16[512,1024]{1,0:T(8,128)(2,1)S(1)} collective-permute-done((bf16[512,1024]{1,0:T(8,128)(2,1)S(1)}, bf16[512,1024]{1,0:T(8,128)(2,1)S(1)}, u32[]{:S(2)}, u32[]{:S(2)}) %collective-permute-start.25) | collective-permute-done | bytes 1048608 | tf_op jit(solution)/shard_map/ppermute | solution.py:44
  238.1 16.3 %middle_back.1 = (f32[512,1024]{1,0:T(8,128)}, bf16[512,1024]{1,0:T(8,128)(2,1)}, bf16[512,1024]{1,0:T(8,128)(2,1)}, bf16[512,1024]{1,0:T(8,128)(2,1)}, f32[16,64,128]{2,1,0:T(8,128)}, /*index=5*/f32[2,1024]{1,0:T(2,128)}) custom-call(s32[8]{0:T(128)} %pad_add_fusion.2.refs_0_, bf16[512,1024]{1,0:T(8,128)(2,1)} %add_convert_fusion.10.refs_1_, ...), custom_call_target="tpu_custom_call" | custom-call | flops 1 | bytes 1 | tf_op jit(solution)/shard_map/middle_back/pallas_call | solution.py:164
  257.6 18.0 %attend_back.1 = (bf16[512,1024]{1,0:T(8,128)(2,1)}, f32[512,1024]{1,0:T(8,128)}, f32[512,1024]{1,0:T(8,128)}) custom-call(bf16[512,1024]{1,0:T(8,128)(2,1)} %get-tuple-element.85.refs_1_.refs_9_.refs_0_, bf16[512,1024]{1,0:T(8,128)(2,1)} %get-tuple-element.83.refs_2_.refs_1_, bf16[512,1024]{1,0:T(8,128)(2,1)} %get-tuple-element.86.refs_3_.refs_2_, ...), custom_call_target="tpu_custom_call" | custom-call | flops 1 | bytes 1 | tf_op jit(solution)/shard_map/attend_back/pallas_call | solution.py:164
  275.6 11.1 %square_gradients.1 = (bf16[4,3,64,1024]{3,2,1,0:T(8,128)(2,1)}, bf16[4,3,64,1024]{3,2,1,0:T(8,128)(2,1)}, bf16[4,3,64,1024]{3,2,1,0:T(8,128)(2,1)}, bf16[4,3,64,1024]{3,2,1,0:T(8,128)(2,1)}) custom-call(s32[4]{0:T(128)} %pad_add_fusion.3.refs_0_, bf16[512,1024]{1,0:T(8,128)(2,1)} %get-tuple-element.118.refs_1_, ...), custom_call_target="tpu_custom_call" | custom-call | flops 1 | bytes 1 | tf_op jit(solution)/shard_map/square_gradients/pallas_call | solution.py:164
  288.9 15.1 %collective-permute-done.31 = bf16[2,528,128]{2,1,0:T(8,128)(2,1)S(1)} collective-permute-done((bf16[2,528,128]{2,1,0:T(8,128)(2,1)S(1)}, bf16[2,528,128]{2,1,0:T(8,128)(2,1)S(1)}, u32[]{:S(2)}, u32[]{:S(2)}) %collective-permute-start.31) | collective-permute-done | bytes 270368 | tf_op jit(solution)/shard_map/ppermute | solution.py:877
  308.6 3.3 add_convert_fusion.2
  311.9 3.3 collective-permute-start.40
  315.2 19.7 %collective-permute-done.32 = bf16[2,528,128]{2,1,0:T(8,128)(2,1)S(1)} collective-permute-done((bf16[2,528,128]{2,1,0:T(8,128)(2,1)S(1)}, bf16[2,528,128]{2,1,0:T(8,128)(2,1)S(1)}, u32[]{:S(2)}, u32[]{:S(2)}) %collective-permute-start.32) | collective-permute-done | bytes 270368 | tf_op jit(solution)/shard_map/ppermute | solution.py:877
  336.8 12.1 %key_value_gradients.1 = (bf16[4,2,64,1024]{3,2,1,0:T(8,128)(2,1)}, bf16[4,2,64,1024]{3,2,1,0:T(8,128)(2,1)}, bf16[4,2,64,1024]{3,2,1,0:T(8,128)(2,1)}, bf16[4,2...) custom-call(s32[4]{0:T(128)} %pad_add_fusion.3.refs_0_, ...), custom_call_target="tpu_custom_call" | custom-call | flops 1 | bytes 1 | tf_op jit(solution)/shard_map/key_value_gradients/pallas_call | solution.py:164
  349.0 2.9 collective-permute-done.33
  353.5 2.0 collective-permute-done.40
  355.5 3.6 add_convert_fusion
  359.1 6.0 %all-to-all-start.2 = ((bf16[4,3,64,1024]{3,2,1,0:T(8,128)(2,1)}), bf16[4,3,64,1024]{3,2,1,0:T(8,128)(2,1)S(1)}, u32[]{:S(2)}, u32[]{:S(2)}) async-start(bf16[4,3,64,1024]{3,2,1,0:T(8,128)(2,1)} %add_convert_fusion), calls=%async_computation.2 | async-start | bytes 3145728 | tf_op jit(solution)/shard_map/all_to_all | solution.py:109
  366.3 16.2 %entry_back.1 = (f32[512,1024]{1,0:T(8,128)}, f32[1,1024]{1,0:T(1,128)}) custom-call(s32[8]{0:T(128)} %pad_add_fusion.2.refs_0_, bf16[512,1024]{1,0:T(8,128)(2,1)} %bitcast.138, f32[1,1024]{1,0:T(1,128)} %bitcast.178, f32[512,1024]{1,0:T(8,128)} %get-tuple-element.135.refs_3_, bf16[512,1024]{1,0:T(8,128)(2,1)} %get-tuple-element.122.refs_5_.refs_4_, ...), custom_call_target="tpu_custom_call" | custom-call | flops 1 | bytes 1 | tf_op jit(solution)/shard_map/entry_back/pallas_call | solution.py:164
  386.4 2.0 collective-permute-done.35
  389.3 2.8 collective-permute-done.36
  392.1 2.0 collective-permute-start.37
  394.2 2.5 add_convert_fusion.3
  399.4 3.8 collective-permute-start.48
  403.2 8.0 %collective-permute-done.46 = bf16[2,64,1024]{2,1,0:T(8,128)(2,1)} collective-permute-done((bf16[2,64,1024]{2,1,0:T(8,128)(2,1)}, bf16[2,64,1024]{2,1,0:T(8,128)(2,1)}, u32[]{:S(2)}, u32[]{:S(2)}) %collective-permute-start.46) | collective-permute-done | bytes 262176 | tf_op jit(solution)/shard_map/ppermute | solution.py:106
  411.3 4.9 %collective-permute-done.48 = bf16[2,64,1024]{2,1,0:T(8,128)(2,1)} collective-permute-done((bf16[2,64,1024]{2,1,0:T(8,128)(2,1)}, bf16[2,64,1024]{2,1,0:T(8,128)(2,1)}, u32[]{:S(2)}, u32[]{:S(2)}) %collective-permute-start.48) | collective-permute-done | bytes 262176 | tf_op jit(solution)/shard_map/ppermute | solution.py:106
  416.2 8.5 %collective-permute-done.47 = bf16[2,64,1024]{2,1,0:T(8,128)(2,1)} collective-permute-done((bf16[2,64,1024]{2,1,0:T(8,128)(2,1)S(1)}, bf16[2,64,1024]{2,1,0:T(8,128)(2,1)}, u32[]{:S(2)}, u32[]{:S(2)}) %collective-permute-start.47) | collective-permute-done | bytes 262176 | tf_op jit(solution)/shard_map/ppermute | solution.py:106
  429.9 3.0 add_convert_fusion.6
  432.9 2.3 collective-permute-done.49
  436.3 3.0 collective-permute-done.44
  (234 shorter events, 71.3 us)
Async XLA Ops:
  7.2 155.3 %all-gather.3.cloned.1.call-start = ((), (), s32[]{:S(2)}) async-start(), calls=%async_computation.5 | async-start | bytes 4866048 | tf_op jit(solution)/shard_map/all_gather | solution.py:951
  42.2 9.2 %collective-permute-start = (bf16[4,2,32,1024]{3,2,1,0:T(8,128)(2,1)S(1)}, bf16[4,2,32,1024]{3,2,1,0:T(8,128)(2,1)S(1)}, u32[]{:S(2)}, u32[]{:S(2)}) collective-permute-start(bf16[4,2,32,1024]{3,2,1,0:T(8,128)(2,1)S(1)} %all_to_all.15.refs_4_.refs_8_), channel_id=1, source_target_pairs={{0,4},{4,0},{8,12},{12,8},{16,20},{20,16},{24,28},{28,24},{1,5},{5... | collective-permute-start | bytes 1572872 | tf_op jit(solution)/shard_map/ppermute | solution.py:44
  43.9 13.9 %collective-permute-start.1 = (bf16[4,2,32,1024]{3,2,1,0:T(8,128)(2,1)S(1)}, bf16[4,2,32,1024]{3,2,1,0:T(8,128)(2,1)S(1)}, u32[]{:S(2)}, u32[]{:S(2)}) collective-permute-start(bf16[4,2,32,1024]{3,2,1,0:T(8,128)(2,1)S(1)} %all_to_all.15.refs_4_.refs_8_), channel_id=1, source_target_pairs={{0,2},{1,3},{2,0},{3,1},{4,6},{5,7},{6,4},{7,5},{8,10},{9,11},{10,... | collective-permute-start | bytes 1572872 | tf_op jit(solution)/shard_map/ppermute | solution.py:44
  46.5 39.5 %all-to-all-start.1 = ((bf16[4,3,32,1024]{3,2,1,0:T(8,128)(2,1)}), bf16[4,3,32,1024]{3,2,1,0:T(8,128)(2,1)S(1)}, u32[]{:S(2)}, u32[]{:S(2)}) async-start(bf16[4,3,32,1024]{3,2,1,0:T(8,128)(2,1)} %broadcast_in_dim.23), calls=%async_computation.1 | async-start | bytes 1572864 | tf_op jit(solution)/shard_map/all_to_all | solution.py:90
  50.0 346.7 %reduce-scatter.2.cloned.1.call-start = ((), (), s32[]{:S(2)}) async-start(), calls=%async_computation.4 | async-start | bytes 4866048 | tf_op jit(solution)/shard_map/reduce_scatter | solution.py:1010
  51.4 13.0 %collective-permute-start.2 = (bf16[4,2,32,1024]{3,2,1,0:T(8,128)(2,1)S(1)}, bf16[4,2,32,1024]{3,2,1,0:T(8,128)(2,1)S(1)}, u32[]{:S(2)}, u32[]{:S(2)}) collective-permute-start(bf16[4,2,32,1024]{3,2,1,0:T(8,128)(2,1)S(1)} %collective-permute-done.refs_5_.refs_9_), channel_id=1, source_target_pairs={{0,2},{1,3},{2,0},{3,1},{4,6},{5,7},{6,4},{7,5},{8,10},{9,11},{10,... | collective-permute-start | bytes 1572872 | tf_op jit(solution)/shard_map/ppermute | solution.py:44
  53.8 11.7 %collective-permute-start.3 = (bf16[4,2,32,1024]{3,2,1,0:T(8,128)(2,1)S(1)}, bf16[4,2,32,1024]{3,2,1,0:T(8,128)(2,1)S(1)}, u32[]{:S(2)}, u32[]{:S(2)}) collective-permute-start(bf16[4,2,32,1024]{3,2,1,0:T(8,128)(2,1)S(1)} %all_to_all.15.refs_4_.refs_8_), channel_id=1, source_target_pairs={{0,1},{1,0},{2,3},{3,2},{4,5},{5,4},{6,7},{7,6},{8,9},{9,8},{10,11... | collective-permute-start | bytes 1572872 | tf_op jit(solution)/shard_map/ppermute | solution.py:44
  53.8 11.7 %collective-permute-start.4 = (bf16[4,2,32,1024]{3,2,1,0:T(8,128)(2,1)S(1)}, bf16[4,2,32,1024]{3,2,1,0:T(8,128)(2,1)}, u32[]{:S(2)}, u32[]{:S(2)}) collective-permute-start(bf16[4,2,32,1024]{3,2,1,0:T(8,128)(2,1)S(1)} %collective-permute-done.refs_5_.refs_9_), channel_id=1, source_target_pairs={{0,1},{1,0},{2,3},{3,2},{4,5},{5,4},{6,7},{7,6},{8,9},{9,8},{10,11... | collective-permute-start | bytes 1572872 | tf_op jit(solution)/shard_map/ppermute | solution.py:44
  57.8 7.7 %collective-permute-start.5 = (bf16[4,2,32,1024]{3,2,1,0:T(8,128)(2,1)S(1)}, bf16[4,2,32,1024]{3,2,1,0:T(8,128)(2,1)}, u32[]{:S(2)}, u32[]{:S(2)}) collective-permute-start(bf16[4,2,32,1024]{3,2,1,0:T(8,128)(2,1)S(1)} %collective-permute-done.1.refs_6_.refs_10_), channel_id=1, source_target_pairs={{0,1},{1,0},{2,3},{3,2},{4,5},{5,4},{6,7},{7,6},{8,9},{9,8},{10,11... | collective-permute-start | bytes 1572872 | tf_op jit(solution)/shard_map/ppermute | solution.py:44
  85.9 17.4 %collective-permute-start.7 = (bf16[4,3,32,1024]{3,2,1,0:T(8,128)(2,1)S(1)}, bf16[4,3,32,1024]{3,2,1,0:T(8,128)(2,1)S(1)}, u32[]{:S(2)}, u32[]{:S(2)}) collective-permute-start(bf16[4,3,32,1024]{3,2,1,0:T(8,128)(2,1)S(1)} %all-to-all-done.1.refs_2_.refs_11_.refs_16_), channel_id=1, source_target_pairs={{0,4},{4,0},{8,12},{12,8},{16,20},{20,16},{24,28},{28,24},{1,5},{5... | collective-permute-start | bytes 2359304 | tf_op jit(solution)/shard_map/ppermute | solution.py:44
  87.6 14.5 %collective-permute-start.14 = (bf16[2,528,128]{2,1,0:T(8,128)(2,1)S(1)}, bf16[2,528,128]{2,1,0:T(8,128)(2,1)S(1)}, u32[]{:S(2)}, u32[]{:S(2)}) collective-permute-start(bf16[2,528,128]{2,1,0:T(8,128)(2,1)S(1)} %pad_maximum_fusion.2), channel_id=1, source_target_pairs={{0,4},{4,8},{8,12},{12,16},{16,20},{20,24},{24,28},{1,5},{5,9},{9,... | collective-permute-start | bytes 811016 | tf_op jit(solution)/shard_map/ppermute | solution.py:877
  91.3 24.1 %collective-permute-start.8 = (bf16[4,3,32,1024]{3,2,1,0:T(8,128)(2,1)S(1)}, bf16[4,3,32,1024]{3,2,1,0:T(8,128)(2,1)S(1)}, u32[]{:S(2)}, u32[]{:S(2)}) collective-permute-start(bf16[4,3,32,1024]{3,2,1,0:T(8,128)(2,1)S(1)} %all-to-all-done.1.refs_2_.refs_11_.refs_16_), channel_id=1, source_target_pairs={{0,2},{1,3},{2,0},{3,1},{4,6},{5,7},{6,4},{7,5},{8,10},{9,11},{10,... | collective-permute-start | bytes 2359304 | tf_op jit(solution)/shard_map/ppermute | solution.py:44
  103.4 16.8 %collective-permute-start.9 = (bf16[4,3,32,1024]{3,2,1,0:T(8,128)(2,1)S(1)}, bf16[4,3,32,1024]{3,2,1,0:T(8,128)(2,1)S(1)}, u32[]{:S(2)}, u32[]{:S(2)}) collective-permute-start(bf16[4,3,32,1024]{3,2,1,0:T(8,128)(2,1)S(1)} %collective-permute-done.7.refs_3_.refs_12_.refs_17_), channel_id=1, source_target_pairs={{0,2},{1,3},{2,0},{3,1},{4,6},{5,7},{6,4},{7,5},{8,10},{9,11},{10,... | collective-permute-start | bytes 2359304 | tf_op jit(solution)/shard_map/ppermute | solution.py:44
  105.3 7.9 %collective-permute-start.15 = (bf16[2,528,128]{2,1,0:T(8,128)(2,1)S(1)}, bf16[2,528,128]{2,1,0:T(8,128)(2,1)S(1)}, u32[]{:S(2)}, u32[]{:S(2)}) collective-permute-start(bf16[2,528,128]{2,1,0:T(8,128)(2,1)S(1)} %pad_maximum_fusion.3), channel_id=1, source_target_pairs={{0,8},{4,12},{8,16},{12,20},{16,24},{20,28},{1,9},{5,13},{9,17},{1... | collective-permute-start | bytes 811016 | tf_op jit(solution)/shard_map/ppermute | solution.py:877
  109.2 24.1 %collective-permute-start.10 = (bf16[4,3,32,1024]{3,2,1,0:T(8,128)(2,1)S(1)}, bf16[4,3,32,1024]{3,2,1,0:T(8,128)(2,1)}, u32[]{:S(2)}, u32[]{:S(2)}) collective-permute-start(bf16[4,3,32,1024]{3,2,1,0:T(8,128)(2,1)S(1)} %all-to-all-done.1.refs_2_.refs_11_.refs_16_), channel_id=1, source_target_pairs={{0,1},{1,0},{2,3},{3,2},{4,5},{5,4},{6,7},{7,6},{8,9},{9,8},{10,11... | collective-permute-start | bytes 2359304 | tf_op jit(solution)/shard_map/ppermute | solution.py:44
  115.3 19.8 %collective-permute-start.11 = (bf16[4,3,32,1024]{3,2,1,0:T(8,128)(2,1)S(1)}, bf16[4,3,32,1024]{3,2,1,0:T(8,128)(2,1)}, u32[]{:S(2)}, u32[]{:S(2)}) collective-permute-start(bf16[4,3,32,1024]{3,2,1,0:T(8,128)(2,1)S(1)} %collective-permute-done.7.refs_3_.refs_12_.refs_17_), channel_id=1, source_target_pairs={{0,1},{1,0},{2,3},{3,2},{4,5},{5,4},{6,7},{7,6},{8,9},{9,8},{10,11... | collective-permute-start | bytes 2359304 | tf_op jit(solution)/shard_map/ppermute | solution.py:44
  115.4 19.7 %collective-permute-start.12 = (bf16[4,3,32,1024]{3,2,1,0:T(8,128)(2,1)S(1)}, bf16[4,3,32,1024]{3,2,1,0:T(8,128)(2,1)}, u32[]{:S(2)}, u32[]{:S(2)}) collective-permute-start(bf16[4,3,32,1024]{3,2,1,0:T(8,128)(2,1)S(1)} %collective-permute-done.8.refs_4_.refs_13_.refs_18_), channel_id=1, source_target_pairs={{0,1},{1,0},{2,3},{3,2},{4,5},{5,4},{6,7},{7,6},{8,9},{9,8},{10,11... | collective-permute-start | bytes 2359304 | tf_op jit(solution)/shard_map/ppermute | solution.py:44
  120.2 14.9 %collective-permute-start.13 = (bf16[4,3,32,1024]{3,2,1,0:T(8,128)(2,1)S(1)}, bf16[4,3,32,1024]{3,2,1,0:T(8,128)(2,1)}, u32[]{:S(2)}, u32[]{:S(2)}) collective-permute-start(bf16[4,3,32,1024]{3,2,1,0:T(8,128)(2,1)S(1)} %collective-permute-done.9.refs_5_.refs_14_.refs_19_), channel_id=1, source_target_pairs={{0,1},{1,0},{2,3},{3,2},{4,5},{5,4},{6,7},{7,6},{8,9},{9,8},{10,11... | collective-permute-start | bytes 2359304 | tf_op jit(solution)/shard_map/ppermute | solution.py:44
  121.1 10.3 %collective-permute-start.16 = (bf16[2,528,128]{2,1,0:T(8,128)(2,1)}, bf16[2,528,128]{2,1,0:T(8,128)(2,1)}, u32[]{:S(2)}, u32[]{:S(2)}) collective-permute-start(bf16[2,528,128]{2,1,0:T(8,128)(2,1)} %pad_maximum_fusion.4), channel_id=1, source_target_pairs={{0,16},{4,20},{8,24},{12,28},{1,17},{5,21},{9,25},{13,29},{2,18},{... | collective-permute-start | bytes 811016 | tf_op jit(solution)/shard_map/ppermute | solution.py:877
  131.4 28.8 %collective-permute-start.18 = (bf16[512,1024]{1,0:T(8,128)(2,1)}, bf16[512,1024]{1,0:T(8,128)(2,1)}, u32[]{:S(2)}, u32[]{:S(2)}) collective-permute-start(bf16[512,1024]{1,0:T(8,128)(2,1)} %bitcast.149), channel_id=1, source_target_pairs={{0,1},{1,0},{2,3},{3,2},{4,5},{5,4},{6,7},{7,6},{8,9},{9,8},{10,11... | collective-permute-start | bytes 3145736 | tf_op jit(solution)/shard_map/ppermute | solution.py:44
  133.3 26.9 %collective-permute-start.17 = (bf16[512,1024]{1,0:T(8,128)(2,1)}, bf16[512,1024]{1,0:T(8,128)(2,1)}, u32[]{:S(2)}, u32[]{:S(2)}) collective-permute-start(bf16[512,1024]{1,0:T(8,128)(2,1)} %bitcast.150), channel_id=1, source_target_pairs={{0,2},{1,3},{2,0},{3,1},{4,6},{5,7},{6,4},{7,5},{8,10},{9,11},{10,... | collective-permute-start | bytes 3145736 | tf_op jit(solution)/shard_map/ppermute | solution.py:44
  159.9 25.6 %collective-permute-start.21 = (bf16[512,1024]{1,0:T(8,128)(2,1)}, bf16[512,1024]{1,0:T(8,128)(2,1)S(1)}, u32[]{:S(2)}, u32[]{:S(2)}) collective-permute-start(bf16[512,1024]{1,0:T(8,128)(2,1)} %get-tuple-element.92.refs_1_), channel_id=1, source_target_pairs={{0,2},{1,3},{2,0},{3,1},{4,6},{5,7},{6,4},{7,5},{8,10},{9,11},{10,... | collective-permute-start | bytes 3145736 | tf_op jit(solution)/shard_map/ppermute | solution.py:44
  180.3 5.1 %collective-permute-start.20 = (bf16[512,1024]{1,0:T(8,128)(2,1)}, bf16[512,1024]{1,0:T(8,128)(2,1)S(1)}, u32[]{:S(2)}, u32[]{:S(2)}) collective-permute-start(bf16[512,1024]{1,0:T(8,128)(2,1)} %get-tuple-element.96), channel_id=1, source_target_pairs={{0,1},{1,0},{2,3},{3,2},{4,5},{5,4},{6,7},{7,6},{8,9},{9,8},{10,11... | collective-permute-start | bytes 3145736 | tf_op jit(solution)/shard_map/ppermute | solution.py:44
  180.6 7.9 %collective-permute-start.23 = (bf16[512,1024]{1,0:T(8,128)(2,1)}, bf16[512,1024]{1,0:T(8,128)(2,1)S(1)}, u32[]{:S(2)}, u32[]{:S(2)}) collective-permute-start(bf16[512,1024]{1,0:T(8,128)(2,1)} %collective-permute-done.17.refs_3_.refs_7_), channel_id=1, source_target_pairs={{0,1},{1,0},{2,3},{3,2},{4,5},{5,4},{6,7},{7,6},{8,9},{9,8},{10,11... | collective-permute-start | bytes 3145736 | tf_op jit(solution)/shard_map/ppermute | solution.py:44
  211.9 25.3 %collective-permute-start.25 = (bf16[512,1024]{1,0:T(8,128)(2,1)S(1)}, bf16[512,1024]{1,0:T(8,128)(2,1)S(1)}, u32[]{:S(2)}, u32[]{:S(2)}) collective-permute-start(bf16[512,1024]{1,0:T(8,128)(2,1)S(1)} %add_convert_fusion.9), channel_id=1, source_target_pairs={{0,2},{1,3},{2,0},{3,1},{4,6},{5,7},{6,4},{7,5},{8,10},{9,11},{10,... | collective-permute-start | bytes 3145736 | tf_op jit(solution)/shard_map/ppermute | solution.py:44
  255.6 20.0 %collective-permute-start.29 = (bf16[2,528,128]{2,1,0:T(8,128)(2,1)S(1)}, bf16[2,528,128]{2,1,0:T(8,128)(2,1)S(1)}, u32[]{:S(2)}, u32[]{:S(2)}) collective-permute-start(bf16[2,528,128]{2,1,0:T(8,128)(2,1)S(1)} %pad_maximum_fusion.1), channel_id=1, source_target_pairs={{4,0},{8,4},{12,8},{16,12},{20,16},{24,20},{28,24},{5,1},{9,5},{13... | collective-permute-start | bytes 811016 | tf_op jit(solution)/shard_map/ppermute | solution.py:877
  256.9 48.0 %collective-permute-start.27 = (bf16[512,1024]{1,0:T(8,128)(2,1)}, bf16[512,1024]{1,0:T(8,128)(2,1)}, u32[]{:S(2)}, u32[]{:S(2)}) collective-permute-start(bf16[512,1024]{1,0:T(8,128)(2,1)} %get-tuple-element.115), channel_id=1, source_target_pairs={{0,1},{1,0},{2,3},{3,2},{4,5},{5,4},{6,7},{7,6},{8,9},{9,8},{10,11... | collective-permute-start | bytes 3145736 | tf_op jit(solution)/shard_map/ppermute | solution.py:44
  286.8 21.8 %collective-permute-start.30 = (bf16[4,3,64,1024]{3,2,1,0:T(8,128)(2,1)}, bf16[4,3,64,1024]{3,2,1,0:T(8,128)(2,1)}, u32[]{:S(2)}, u32[]{:S(2)}) collective-permute-start(bf16[4,3,64,1024]{3,2,1,0:T(8,128)(2,1)} %get-tuple-element.124), channel_id=1, source_target_pairs={{0,1},{1,0},{2,3},{3,2},{4,5},{5,4},{6,7},{7,6},{8,9},{9,8},{10,11... | collective-permute-start | bytes 4718600 | tf_op jit(solution)/shard_map/ppermute | solution.py:44
  287.5 16.5 %collective-permute-start.31 = (bf16[2,528,128]{2,1,0:T(8,128)(2,1)S(1)}, bf16[2,528,128]{2,1,0:T(8,128)(2,1)S(1)}, u32[]{:S(2)}, u32[]{:S(2)}) collective-permute-start(bf16[2,528,128]{2,1,0:T(8,128)(2,1)S(1)} %pad_maximum_fusion.5), channel_id=1, source_target_pairs={{8,0},{12,4},{16,8},{20,12},{24,16},{28,20},{9,1},{13,5},{17,9},{2... | collective-permute-start | bytes 811016 | tf_op jit(solution)/shard_map/ppermute | solution.py:877
  288.8 66.6 %collective-permute-start.39 = (bf16[4,3,64,1024]{3,2,1,0:T(8,128)(2,1)}, bf16[4,3,64,1024]{3,2,1,0:T(8,128)(2,1)S(1)}, u32[]{:S(2)}, u32[]{:S(2)}) collective-permute-start(bf16[4,3,64,1024]{3,2,1,0:T(8,128)(2,1)} %get-tuple-element.141), channel_id=1, source_target_pairs={{0,1},{1,0},{2,3},{3,2},{4,5},{5,4},{6,7},{7,6},{8,9},{9,8},{10,11... | collective-permute-start | bytes 4718600 | tf_op jit(solution)/shard_map/ppermute | solution.py:44
  306.7 29.1 %collective-permute-start.28 = (bf16[512,1024]{1,0:T(8,128)(2,1)S(1)}, bf16[512,1024]{1,0:T(8,128)(2,1)S(1)}, u32[]{:S(2)}, u32[]{:S(2)}) collective-permute-start(bf16[512,1024]{1,0:T(8,128)(2,1)S(1)} %add_convert_fusion.7), channel_id=1, source_target_pairs={{0,2},{1,3},{2,0},{3,1},{4,6},{5,7},{6,4},{7,5},{8,10},{9,11},{10,... | collective-permute-start | bytes 3145736 | tf_op jit(solution)/shard_map/ppermute | solution.py:44
  307.3 27.6 %collective-permute-start.32 = (bf16[2,528,128]{2,1,0:T(8,128)(2,1)S(1)}, bf16[2,528,128]{2,1,0:T(8,128)(2,1)S(1)}, u32[]{:S(2)}, u32[]{:S(2)}) collective-permute-start(bf16[2,528,128]{2,1,0:T(8,128)(2,1)S(1)} %pad_maximum_fusion.6), channel_id=1, source_target_pairs={{16,0},{20,4},{24,8},{28,12},{17,1},{21,5},{25,9},{29,13},{18,2},{... | collective-permute-start | bytes 811016 | tf_op jit(solution)/shard_map/ppermute | solution.py:877
  311.9 43.5 %collective-permute-start.40 = (bf16[4,3,64,1024]{3,2,1,0:T(8,128)(2,1)}, bf16[4,3,64,1024]{3,2,1,0:T(8,128)(2,1)}, u32[]{:S(2)}, u32[]{:S(2)}) collective-permute-start(bf16[4,3,64,1024]{3,2,1,0:T(8,128)(2,1)} %add_convert_fusion.2), channel_id=1, source_target_pairs={{0,4},{4,0},{8,12},{12,8},{16,20},{20,16},{24,28},{28,24},{1,5},{5... | collective-permute-start | bytes 4718600 | tf_op jit(solution)/shard_map/ppermute | solution.py:44
  359.1 67.5 %all-to-all-start.2 = ((bf16[4,3,64,1024]{3,2,1,0:T(8,128)(2,1)}), bf16[4,3,64,1024]{3,2,1,0:T(8,128)(2,1)S(1)}, u32[]{:S(2)}, u32[]{:S(2)}) async-start(bf16[4,3,64,1024]{3,2,1,0:T(8,128)(2,1)} %add_convert_fusion), calls=%async_computation.2 | async-start | bytes 3145728 | tf_op jit(solution)/shard_map/all_to_all | solution.py:109
  365.1 29.0 %collective-permute-start.42 = (bf16[4,2,64,1024]{3,2,1,0:T(8,128)(2,1)S(1)}, bf16[4,2,64,1024]{3,2,1,0:T(8,128)(2,1)}, u32[]{:S(2)}, u32[]{:S(2)}) collective-permute-start(bf16[4,2,64,1024]{3,2,1,0:T(8,128)(2,1)S(1)} %add_convert_fusion.5), channel_id=1, source_target_pairs={{0,4},{4,0},{8,12},{12,8},{16,20},{20,16},{24,28},{28,24},{1,5},{5... | collective-permute-start | bytes 3145736 | tf_op jit(solution)/shard_map/ppermute | solution.py:44
  366.3 27.8 %collective-permute-start.41 = (bf16[4,2,64,1024]{3,2,1,0:T(8,128)(2,1)}, bf16[4,2,64,1024]{3,2,1,0:T(8,128)(2,1)}, u32[]{:S(2)}, u32[]{:S(2)}) collective-permute-start(bf16[4,2,64,1024]{3,2,1,0:T(8,128)(2,1)} %get-tuple-element.145), channel_id=1, source_target_pairs={{0,1},{1,0},{2,3},{3,2},{4,5},{5,4},{6,7},{7,6},{8,9},{9,8},{10,11... | collective-permute-start | bytes 3145736 | tf_op jit(solution)/shard_map/ppermute | solution.py:44
  384.6 3.7 collective-permute-start.35
  388.4 3.7 collective-permute-start.36
  389.3 40.6 %collective-permute-start.26 = (bf16[512,1024]{1,0:T(8,128)(2,1)}, bf16[512,1024]{1,0:T(8,128)(2,1)}, u32[]{:S(2)}, u32[]{:S(2)}) collective-permute-start(bf16[512,1024]{1,0:T(8,128)(2,1)} %get-tuple-element.112), channel_id=1, source_target_pairs={{0,1},{1,0},{2,3},{3,2},{4,5},{5,4},{6,7},{7,6},{8,9},{9,8},{10,11... | collective-permute-start | bytes 3145736 | tf_op jit(solution)/shard_map/ppermute | solution.py:44
  392.1 11.0 %collective-permute-start.37 = (f32[3,1024]{1,0:T(4,128)S(1)}, f32[3,1024]{1,0:T(4,128)S(1)}, u32[]{:S(2)}, u32[]{:S(2)}) collective-permute-start(f32[3,1024]{1,0:T(4,128)S(1)} %add.220), channel_id=1, source_target_pairs={{0,8},{4,12},{8,0},{12,4},{16,24},{20,28},{24,16},{28,20},{1,9},{5... | collective-permute-start | bytes 36872 | tf_op jit(solution)/shard_map/ppermute | solution.py:44
  396.7 30.2 %collective-permute-start.43 = (bf16[3,704,128]{2,1,0:T(8,128)(2,1)}, bf16[3,704,128]{2,1,0:T(8,128)(2,1)}, u32[]{:S(2)}, u32[]{:S(2)}) collective-permute-start(bf16[3,704,128]{2,1,0:T(8,128)(2,1)} %bitcast.162), channel_id=1, source_target_pairs={{0,2},{1,3},{2,0},{3,1},{4,6},{5,7},{6,4},{7,5},{8,10},{9,11},{10,... | collective-permute-start | bytes 1622024 | tf_op jit(solution)/shard_map/ppermute | solution.py:44
  399.4 11.8 %collective-permute-start.46 = (bf16[2,64,1024]{2,1,0:T(8,128)(2,1)}, bf16[2,64,1024]{2,1,0:T(8,128)(2,1)}, u32[]{:S(2)}, u32[]{:S(2)}) collective-permute-start(bf16[2,64,1024]{2,1,0:T(8,128)(2,1)} %get-tuple-element.210), channel_id=1, source_target_pairs={{0,8},{4,12},{8,0},{12,4},{16,24},{20,28},{24,16},{28,20},{1,9},{5... | collective-permute-start | bytes 786440 | tf_op jit(solution)/shard_map/ppermute | solution.py:106
  399.4 16.8 %collective-permute-start.48 = (bf16[2,64,1024]{2,1,0:T(8,128)(2,1)}, bf16[2,64,1024]{2,1,0:T(8,128)(2,1)}, u32[]{:S(2)}, u32[]{:S(2)}) collective-permute-start(bf16[2,64,1024]{2,1,0:T(8,128)(2,1)} %get-tuple-element.211), channel_id=1, source_target_pairs={{0,24},{4,28},{8,16},{12,20},{16,8},{20,12},{24,0},{28,4},{1,25},{... | collective-permute-start | bytes 786440 | tf_op jit(solution)/shard_map/ppermute | solution.py:106
  403.2 21.5 %collective-permute-start.47 = (bf16[2,64,1024]{2,1,0:T(8,128)(2,1)S(1)}, bf16[2,64,1024]{2,1,0:T(8,128)(2,1)}, u32[]{:S(2)}, u32[]{:S(2)}) collective-permute-start(bf16[2,64,1024]{2,1,0:T(8,128)(2,1)S(1)} %get-tuple-element.212), channel_id=1, source_target_pairs={{0,16},{4,20},{8,24},{12,28},{16,0},{20,4},{24,8},{28,12},{1,17},{... | collective-permute-start | bytes 786440 | tf_op jit(solution)/shard_map/ppermute | solution.py:106
  411.2 21.7 %collective-permute-start.38 = (f32[3,1024]{1,0:T(4,128)S(1)}, f32[3,1024]{1,0:T(4,128)S(1)}, u32[]{:S(2)}, u32[]{:S(2)}) collective-permute-start(f32[3,1024]{1,0:T(4,128)S(1)} %add.221), channel_id=1, source_target_pairs={{0,16},{4,20},{8,24},{12,28},{16,0},{20,4},{24,8},{28,12},{1,17},{... | collective-permute-start | bytes 36872 | tf_op jit(solution)/shard_map/ppermute | solution.py:44
  425.9 9.3 %collective-permute-start.49 = (bf16[2,64,1024]{2,1,0:T(8,128)(2,1)S(1)}, bf16[2,64,1024]{2,1,0:T(8,128)(2,1)}, u32[]{:S(2)}, u32[]{:S(2)}) collective-permute-start(bf16[2,64,1024]{2,1,0:T(8,128)(2,1)S(1)} %fusion.14), channel_id=1, source_target_pairs={{0,2},{1,3},{2,0},{3,1},{4,6},{5,7},{6,4},{7,5},{8,10},{9,11},{10,... | collective-permute-start | bytes 786440 | tf_op jit(solution)/shard_map/ppermute | solution.py:44
  428.3 11.0 %collective-permute-start.44 = (bf16[3,64,1024]{2,1,0:T(8,128)(2,1)S(1)}, bf16[3,64,1024]{2,1,0:T(8,128)(2,1)S(1)}, u32[]{:S(2)}, u32[]{:S(2)}) collective-permute-start(bf16[3,64,1024]{2,1,0:T(8,128)(2,1)S(1)} %reduce_sum.12), channel_id=1, source_target_pairs={{0,2},{1,3},{2,0},{3,1},{4,6},{5,7},{6,4},{7,5},{8,10},{9,11},{10,... | collective-permute-start | bytes 1179656 | tf_op jit(solution)/shard_map/ppermute | solution.py:44
  436.2 4.3 collective-permute-start.50
  (42 other events, 422.0 us)
Sparse Core Ops, SparseCore 0:
  11.3 90.3 all-gather.2
  237.3 106.4 reduce-scatter.1

commit v5 on v4

--- a/solution.py
+++ b/solution.py
@@ -552,11 +552,12 @@
     lefts, rights = refs[:n], refs[n : n + m]
     outs = refs[n + m : -3]
     turned, grads, sem = refs[-3:]
-    ready()
     copies = hand_out(base_ref, grads, outs, sem)
     for k in range(m):
         if k == 0 or which[k] != which[k - 1]:
+            ready(1 + which[k])
             turn_rows(lefts[which[k]], turned)
+        ready(1 + n + k)
         gradient_rows(plan, turned, rights[k], grads, k)
         start_all(copies[k])
     for k in range(m):
@@ -615,7 +616,7 @@
         vin_ref[rows, lanes] = vb
         return 0
 
-    lax.fori_loop(0, 16, pair, 0)
+    lax.fori_loop(0, 16, pair, 0, unroll=2)
 
 
 def inner_call(plan, query, keys, values, qsig, attback, state, segcol, segrow):

time: 461 us -> 459 us (level)
    ppermute x43, waiting for transfers between devices: 49.4 us -> 57.8 us  [swap(): return lax.ppermute(value, axis, [(i, i ^ bit) for i in range(size)])]
    ppermute x6, waiting for transfers between devices: 53 us -> 45.7 us  [step(): lax.ppermute(sent, 'seq', beyond(self.order, self.reach, self.size))]
  transfers between devices with their start and end apart: 56 -> 56, of which waited for: 26 -> 27; matrix products, arithmetic and copies ran while one was open for 9% -> 9% of each run, Pallas kernels for 32% -> 31%
where the time goes in v5:
time: 459 us; the launch traced here: 454 us
  Pallas kernels  159 us (35%)
  waiting for transfers between devices  133 us (29%)
  starting transfers between devices  57.1 us (12%)
  other arithmetic  37.4 us (8%)
  blocking collectives  30.8 us (7%)
  local copies, waits for them, and re-layouts  21.3 us (5%)
  between operations  15.2 us (3%)
    pallas_call x11, Pallas kernels, call(): pl.pallas_call(kernel, out_shape=out_shape, in_specs=[ANY if spec is STAG...  159 us
    ppermute x43, waiting for transfers between devices, swap(): return lax.ppermute(value, axis, [(i, i ^ bit) for i in range(size)])  57.8 us
    ppermute x6, waiting for transfers between devices, step(): lax.ppermute(sent, 'seq', beyond(self.order, self.reach, self.size))  45.7 us
    all_to_all x1, blocking collectives, along(): return lax.all_to_all(copies, 'seq', 0, 0, axis_index_groups=self.groups)  30.8 us
    ppermute x43, starting transfers between devices, swap(): return lax.ppermute(value, axis, [(i, i ^ bit) for i in range(size)])  28.1 us
    ppermute x3, waiting for transfers between devices, sum_along(): total = total + lax.ppermute(sent, 'seq', pairs).astype(F32)  21.3 us
    convert_element_type x9, other arithmetic, add(): return (left.astype(F32) + right.astype(F32)).astype(BF)  18.6 us
    ppermute x6, starting transfers between devices, step(): lax.ppermute(sent, 'seq', beyond(self.order, self.reach, self.size))  16.2 us
  transfers between devices with their start and end apart: 56, of which 27 were waited for; matrix products, arithmetic and copies ran while one was open for 9% of the time, Pallas kernels for 31%

profile of v5, /device:TPU:0, one launch (start us, length us, event | category | flops | bytes accessed | tf_op | source)
XLA Modules:
  0.0 454.0 jit_solution(1000562413610102993)
XLA Ops:
  11.4 30.8 %all_to_all.15.refs_4_.refs_8_ = bf16[4,2,32,1024]{3,2,1,0:T(8,128)(2,1)S(1)} all-to-all(bf16[4,2,32,1024]{3,2,1,0:T(8,128)(2,1)S(1)} %broadcast_in_dim.22), channel_id=1, replica_groups={{0,8,16,24},{4,12,20,28},{1,9,17,25},{5,13,21,29},{2,10,18,26},{6,14,22..., dimensions={0} | all-to-all | bytes 1048576 | tf_op jit(solution)/shard_map/all_to_all | solution.py:90
  46.5 3.5 all-to-all-start.1
  54.3 3.5 collective-permute-done.1.refs_6_.refs_10_
  57.8 6.6 %collective-permute-done.2.refs_7_.refs_11_ = bf16[4,2,32,1024]{3,2,1,0:T(8,128)(2,1)S(1)} collective-permute-done((bf16[4,2,32,1024]{3,2,1,0:T(8,128)(2,1)S(1)}, bf16[4,2,32,1024]{3,2,1,0:T(8,128)(2,1)S(1)}, u32[]{:S(2)}, u32[]{:S(2)}) %collective-permute-start.2) | collective-permute-done | bytes 524320 | tf_op jit(solution)/shard_map/ppermute | solution.py:44
  66.4 11.8 %keys_values.1 = (bf16[512,1024]{1,0:T(8,128)(2,1)}, bf16[512,1024]{1,0:T(8,128)(2,1)}, bf16[512,1024]{1,0:T(8,128)(2,1)}, bf16[512,1024]{1,0:T(8,128)(2,1)}, f32[16,64,128]{2,1,0:T(8,128)}) custom-call(s32[8]{0:T(128)} %pad_add_fusion.2.refs_0_, bf16[512,1024]{1,0:T(8,128)(2,1)} %bitcast.136, f32[1,1024]{1,0:T(1,128)} %bitcast.177, f32[512,1]{1,0:T(8,128)} %bitcast.159, ...), custom_call_target="tpu_custom_call" | custom-call | flops 1 | bytes 1 | tf_op jit(solution)/shard_map/keys_values/pallas_call | solution.py:164
  78.2 7.7 %all-to-all-done.1.refs_2_.refs_11_.refs_16_ = bf16[4,3,32,1024]{3,2,1,0:T(8,128)(2,1)S(1)} async-done(((bf16[4,3,32,1024]{3,2,1,0:T(8,128)(2,1)}), bf16[4,3,32,1024]{3,2,1,0:T(8,128)(2,1)S(1)}, u32[]{:S(2)}, u32[]{:S(2)}) %all-to-all-start.1) | async-done | bytes 786464 | tf_op jit(solution)/shard_map/all_to_all | solution.py:90
  87.6 3.5 collective-permute-start.14
  91.7 10.4 %collective-permute-done.14 = bf16[2,528,128]{2,1,0:T(8,128)(2,1)S(1)} collective-permute-done((bf16[2,528,128]{2,1,0:T(8,128)(2,1)S(1)}, bf16[2,528,128]{2,1,0:T(8,128)(2,1)S(1)}, u32[]{:S(2)}, u32[]{:S(2)}) %collective-permute-start.14) | collective-permute-done | bytes 270368 | tf_op jit(solution)/shard_map/ppermute | solution.py:878
  105.3 3.9 collective-permute-start.15
  109.3 3.9 collective-permute-done.15
  115.9 4.3 collective-permute-done.9.refs_5_.refs_14_.refs_19_
  121.1 4.9 %collective-permute-start.16 = (bf16[2,528,128]{2,1,0:T(8,128)(2,1)}, bf16[2,528,128]{2,1,0:T(8,128)(2,1)}, u32[]{:S(2)}, u32[]{:S(2)}) collective-permute-start(bf16[2,528,128]{2,1,0:T(8,128)(2,1)} %pad_maximum_fusion.4), channel_id=1, source_target_pairs={{0,16},{4,20},{8,24},{12,28},{1,17},{5,21},{9,25},{13,29},{2,18},{... | collective-permute-start | bytes 811016 | tf_op jit(solution)/shard_map/ppermute | solution.py:878
  127.5 3.9 collective-permute-done.16
  135.1 9.2 %query_gate.1 = (bf16[512,1024]{1,0:T(8,128)(2,1)}, bf16[512,1024]{1,0:T(8,128)(2,1)}, f32[512,1024]{1,0:T(8,128)}) custom-call(s32[8]{0:T(128)} %pad_add_fusion.2.refs_0_, bf16[512,1024]{1,0:T(8,128)(2,1)} %get-tuple-element.81.refs_1_.refs_2_.refs_9_, bf16[4,3,32,1024]{3,2,1,0:T(8,128)(2,1)} %copy-done, bf16[4,3,32,1024]{3,2,1,0:T(8,128)(2,1)} %copy-done.1, ...), custom_call_target="tpu_custom_call" | custom-call | flops 1 | bytes 1 | tf_op jit(solution)/shard_map/query_gate/pallas_call | solution.py:164
  144.3 15.3 %attend.1 = (f32[512,1024]{1,0:T(8,128)}, bf16[512,1024]{1,0:T(8,128)(2,1)}, f32[512,1024]{1,0:T(8,128)}, bf16[512,1024]{1,0:T(8,128)(2,1)}) custom-call(s32[8]{0:T(128)} %pad_add_fusion.2.refs_0_, bf16[512,1024]{1,0:T(8,128)(2,1)} %get-tuple-element.85.refs_1_.refs_9_.refs_0_, bf16[512,1024]{1,0:T(8,128)(2,1)} %get-tuple-element.83.refs_2_.refs_1_, ...), custom_call_target="tpu_custom_call" | custom-call | flops 1 | bytes 1 | tf_op jit(solution)/shard_map/attend/pallas_call | solution.py:164
  160.2 2.3 collective-permute-done.19.refs_2_
  163.5 16.8 %feed_forward.2 = (bf16[512,1024]{1,0:T(8,128)(2,1)}, bf16[512,1024]{1,0:T(8,128)(2,1)}, bf16[512,1024]{1,0:T(8,128)(2,1)}, bf16[512,1024]{1,0:T(8,128)(2,1)}, b...) custom-call(s32[1]{0:T(128)} %constant.149.clone.1.refs_0_, ...), custom_call_target="tpu_custom_call" | custom-call | flops 1 | bytes 1 | tf_op jit(solution)/shard_map/feed_forward/pallas_call | solution.py:164
  180.9 4.5 collective-permute-done.21.refs_1_.refs_3_
  185.5 3.0 add_convert_fusion.10.refs_1_
  190.5 16.9 %feed_forward.3 = (bf16[512,1024]{1,0:T(8,128)(2,1)}, bf16[512,1024]{1,0:T(8,128)(2,1)}, bf16[512,1024]{1,0:T(8,128)(2,1)}, bf16[512,1024]{1,0:T(8,128)(2,1)}, b...) custom-call(s32[1]{0:T(128)} %constant.149.clone.1.refs_0_, ...), custom_call_target="tpu_custom_call" | custom-call | flops 1 | bytes 1 | tf_op jit(solution)/shard_map/feed_forward/pallas_call | solution.py:164
  207.5 2.7 collective-permute-done.24
  212.3 18.1 %feed_forward_gradients.1 = bf16[8,3,704,128]{3,2,1,0:T(8,128)(2,1)} custom-call(s32[1]{0:T(128)} %constant.149.clone.1.refs_0_, bf16[512,1024]{1,0:T(8,128)(2,1)} %get-tuple-element.92.refs_1_, bf16[512,1024]{1,0:T(8,128)(2,1)} %copy-done.14, bf16[512,1024]{1,0:T(8,128)(2,1)} %copy-done.15, bf16[512,1024]{1,0:T(8,128)(2,1)} %copy-done.17, ...), custom_call_target="tpu_custom_call" | custom-call | flops 89999998976 | bytes 1 | tf_op jit(solution)/shard_map/feed_forward_gradients/pallas_call | solution.py:164
  230.4 6.8 %collective-permute-done.25.refs_2_ = bf16[512,1024]{1,0:T(8,128)(2,1)S(1)} collective-permute-done((bf16[512,1024]{1,0:T(8,128)(2,1)S(1)}, bf16[512,1024]{1,0:T(8,128)(2,1)S(1)}, u32[]{:S(2)}, u32[]{:S(2)}) %collective-permute-start.25) | collective-permute-done | bytes 1048608 | tf_op jit(solution)/shard_map/ppermute | solution.py:44
  238.1 16.3 %middle_back.1 = (f32[512,1024]{1,0:T(8,128)}, bf16[512,1024]{1,0:T(8,128)(2,1)}, bf16[512,1024]{1,0:T(8,128)(2,1)}, bf16[512,1024]{1,0:T(8,128)(2,1)}, f32[16,64,128]{2,1,0:T(8,128)}, /*index=5*/f32[2,1024]{1,0:T(2,128)}) custom-call(s32[8]{0:T(128)} %pad_add_fusion.2.refs_0_, bf16[512,1024]{1,0:T(8,128)(2,1)} %add_convert_fusion.10.refs_1_, ...), custom_call_target="tpu_custom_call" | custom-call | flops 1 | bytes 1 | tf_op jit(solution)/shard_map/middle_back/pallas_call | solution.py:164
  257.6 16.6 %attend_back.1 = (bf16[512,1024]{1,0:T(8,128)(2,1)}, f32[512,1024]{1,0:T(8,128)}, f32[512,1024]{1,0:T(8,128)}) custom-call(bf16[512,1024]{1,0:T(8,128)(2,1)} %get-tuple-element.85.refs_1_.refs_9_.refs_0_, bf16[512,1024]{1,0:T(8,128)(2,1)} %get-tuple-element.83.refs_2_.refs_1_, bf16[512,1024]{1,0:T(8,128)(2,1)} %get-tuple-element.86.refs_3_.refs_2_, ...), custom_call_target="tpu_custom_call" | custom-call | flops 1 | bytes 1 | tf_op jit(solution)/shard_map/attend_back/pallas_call | solution.py:164
  274.2 10.1 %square_gradients.1 = (bf16[4,3,64,1024]{3,2,1,0:T(8,128)(2,1)}, bf16[4,3,64,1024]{3,2,1,0:T(8,128)(2,1)}, bf16[4,3,64,1024]{3,2,1,0:T(8,128)(2,1)}, bf16[4,3,64,1024]{3,2,1,0:T(8,128)(2,1)}) custom-call(s32[4]{0:T(128)} %pad_add_fusion.3.refs_0_, bf16[512,1024]{1,0:T(8,128)(2,1)} %get-tuple-element.118.refs_1_, ...), custom_call_target="tpu_custom_call" | custom-call | flops 1 | bytes 1 | tf_op jit(solution)/shard_map/square_gradients/pallas_call | solution.py:164
  286.6 15.6 %collective-permute-done.31 = bf16[2,528,128]{2,1,0:T(8,128)(2,1)S(1)} collective-permute-done((bf16[2,528,128]{2,1,0:T(8,128)(2,1)S(1)}, bf16[2,528,128]{2,1,0:T(8,128)(2,1)S(1)}, u32[]{:S(2)}, u32[]{:S(2)}) %collective-permute-start.31) | collective-permute-done | bytes 270368 | tf_op jit(solution)/shard_map/ppermute | solution.py:878
  306.7 3.3 add_convert_fusion.2
  310.0 4.1 collective-permute-start.40
  314.1 12.0 %collective-permute-done.32 = bf16[2,528,128]{2,1,0:T(8,128)(2,1)S(1)} collective-permute-done((bf16[2,528,128]{2,1,0:T(8,128)(2,1)S(1)}, bf16[2,528,128]{2,1,0:T(8,128)(2,1)S(1)}, u32[]{:S(2)}, u32[]{:S(2)}) %collective-permute-start.32) | collective-permute-done | bytes 270368 | tf_op jit(solution)/shard_map/ppermute | solution.py:878
  327.0 2.7 collective-permute-done.28
  330.7 12.2 %key_value_gradients.1 = (bf16[4,2,64,1024]{3,2,1,0:T(8,128)(2,1)}, bf16[4,2,64,1024]{3,2,1,0:T(8,128)(2,1)}, bf16[4,2,64,1024]{3,2,1,0:T(8,128)(2,1)}, bf16[4,2...) custom-call(s32[4]{0:T(128)} %pad_add_fusion.3.refs_0_, ...), custom_call_target="tpu_custom_call" | custom-call | flops 1 | bytes 1 | tf_op jit(solution)/shard_map/key_value_gradients/pallas_call | solution.py:164
  343.0 2.9 collective-permute-done.33
  347.5 6.8 %collective-permute-done.40 = bf16[4,3,64,1024]{3,2,1,0:T(8,128)(2,1)} collective-permute-done((bf16[4,3,64,1024]{3,2,1,0:T(8,128)(2,1)}, bf16[4,3,64,1024]{3,2,1,0:T(8,128)(2,1)}, u32[]{:S(2)}, u32[]{:S(2)}) %collective-permute-start.40) | collective-permute-done | bytes 1572896 | tf_op jit(solution)/shard_map/ppermute | solution.py:44
  354.4 3.6 add_convert_fusion
  358.0 5.3 %all-to-all-start.2 = ((bf16[4,3,64,1024]{3,2,1,0:T(8,128)(2,1)}), bf16[4,3,64,1024]{3,2,1,0:T(8,128)(2,1)S(1)}, u32[]{:S(2)}, u32[]{:S(2)}) async-start(bf16[4,3,64,1024]{3,2,1,0:T(8,128)(2,1)} %add_convert_fusion), calls=%async_computation.2 | async-start | bytes 3145728 | tf_op jit(solution)/shard_map/all_to_all | solution.py:109
  365.1 16.2 %entry_back.1 = (f32[512,1024]{1,0:T(8,128)}, f32[1,1024]{1,0:T(1,128)}) custom-call(s32[8]{0:T(128)} %pad_add_fusion.2.refs_0_, bf16[512,1024]{1,0:T(8,128)(2,1)} %bitcast.138, f32[1,1024]{1,0:T(1,128)} %bitcast.178, f32[512,1024]{1,0:T(8,128)} %get-tuple-element.135.refs_3_, bf16[512,1024]{1,0:T(8,128)(2,1)} %get-tuple-element.122.refs_5_.refs_4_, ...), custom_call_target="tpu_custom_call" | custom-call | flops 1 | bytes 1 | tf_op jit(solution)/shard_map/entry_back/pallas_call | solution.py:164
  385.2 2.0 collective-permute-done.35
  387.5 3.5 collective-permute-done.36
  391.0 2.0 collective-permute-start.37
  393.0 2.5 add_convert_fusion.3
  398.2 3.8 collective-permute-start.48
  402.0 8.0 %collective-permute-done.46 = bf16[2,64,1024]{2,1,0:T(8,128)(2,1)} collective-permute-done((bf16[2,64,1024]{2,1,0:T(8,128)(2,1)}, bf16[2,64,1024]{2,1,0:T(8,128)(2,1)}, u32[]{:S(2)}, u32[]{:S(2)}) %collective-permute-start.46) | collective-permute-done | bytes 262176 | tf_op jit(solution)/shard_map/ppermute | solution.py:106
  410.1 4.8 %collective-permute-done.48 = bf16[2,64,1024]{2,1,0:T(8,128)(2,1)} collective-permute-done((bf16[2,64,1024]{2,1,0:T(8,128)(2,1)}, bf16[2,64,1024]{2,1,0:T(8,128)(2,1)}, u32[]{:S(2)}, u32[]{:S(2)}) %collective-permute-start.48) | collective-permute-done | bytes 262176 | tf_op jit(solution)/shard_map/ppermute | solution.py:106
  415.0 8.5 %collective-permute-done.47 = bf16[2,64,1024]{2,1,0:T(8,128)(2,1)} collective-permute-done((bf16[2,64,1024]{2,1,0:T(8,128)(2,1)S(1)}, bf16[2,64,1024]{2,1,0:T(8,128)(2,1)}, u32[]{:S(2)}, u32[]{:S(2)}) %collective-permute-start.47) | collective-permute-done | bytes 262176 | tf_op jit(solution)/shard_map/ppermute | solution.py:106
  428.6 3.0 add_convert_fusion.6
  431.6 2.5 collective-permute-done.49
  435.2 3.0 collective-permute-done.44
  (234 shorter events, 73.1 us)
Async XLA Ops:
  7.2 155.3 %all-gather.3.cloned.1.call-start = ((), (), s32[]{:S(2)}) async-start(), calls=%async_computation.5 | async-start | bytes 4866048 | tf_op jit(solution)/shard_map/all_gather | solution.py:952
  42.2 9.2 %collective-permute-start = (bf16[4,2,32,1024]{3,2,1,0:T(8,128)(2,1)S(1)}, bf16[4,2,32,1024]{3,2,1,0:T(8,128)(2,1)S(1)}, u32[]{:S(2)}, u32[]{:S(2)}) collective-permute-start(bf16[4,2,32,1024]{3,2,1,0:T(8,128)(2,1)S(1)} %all_to_all.15.refs_4_.refs_8_), channel_id=1, source_target_pairs={{0,4},{4,0},{8,12},{12,8},{16,20},{20,16},{24,28},{28,24},{1,5},{5... | collective-permute-start | bytes 1572872 | tf_op jit(solution)/shard_map/ppermute | solution.py:44
  43.9 13.9 %collective-permute-start.1 = (bf16[4,2,32,1024]{3,2,1,0:T(8,128)(2,1)S(1)}, bf16[4,2,32,1024]{3,2,1,0:T(8,128)(2,1)S(1)}, u32[]{:S(2)}, u32[]{:S(2)}) collective-permute-start(bf16[4,2,32,1024]{3,2,1,0:T(8,128)(2,1)S(1)} %all_to_all.15.refs_4_.refs_8_), channel_id=1, source_target_pairs={{0,2},{1,3},{2,0},{3,1},{4,6},{5,7},{6,4},{7,5},{8,10},{9,11},{10,... | collective-permute-start | bytes 1572872 | tf_op jit(solution)/shard_map/ppermute | solution.py:44
  46.5 39.5 %all-to-all-start.1 = ((bf16[4,3,32,1024]{3,2,1,0:T(8,128)(2,1)}), bf16[4,3,32,1024]{3,2,1,0:T(8,128)(2,1)S(1)}, u32[]{:S(2)}, u32[]{:S(2)}) async-start(bf16[4,3,32,1024]{3,2,1,0:T(8,128)(2,1)} %broadcast_in_dim.23), calls=%async_computation.1 | async-start | bytes 1572864 | tf_op jit(solution)/shard_map/all_to_all | solution.py:90
  50.0 345.6 %reduce-scatter.2.cloned.1.call-start = ((), (), s32[]{:S(2)}) async-start(), calls=%async_computation.4 | async-start | bytes 4866048 | tf_op jit(solution)/shard_map/reduce_scatter | solution.py:1011
  51.4 13.0 %collective-permute-start.2 = (bf16[4,2,32,1024]{3,2,1,0:T(8,128)(2,1)S(1)}, bf16[4,2,32,1024]{3,2,1,0:T(8,128)(2,1)S(1)}, u32[]{:S(2)}, u32[]{:S(2)}) collective-permute-start(bf16[4,2,32,1024]{3,2,1,0:T(8,128)(2,1)S(1)} %collective-permute-done.refs_5_.refs_9_), channel_id=1, source_target_pairs={{0,2},{1,3},{2,0},{3,1},{4,6},{5,7},{6,4},{7,5},{8,10},{9,11},{10,... | collective-permute-start | bytes 1572872 | tf_op jit(solution)/shard_map/ppermute | solution.py:44
  53.8 11.7 %collective-permute-start.3 = (bf16[4,2,32,1024]{3,2,1,0:T(8,128)(2,1)S(1)}, bf16[4,2,32,1024]{3,2,1,0:T(8,128)(2,1)S(1)}, u32[]{:S(2)}, u32[]{:S(2)}) collective-permute-start(bf16[4,2,32,1024]{3,2,1,0:T(8,128)(2,1)S(1)} %all_to_all.15.refs_4_.refs_8_), channel_id=1, source_target_pairs={{0,1},{1,0},{2,3},{3,2},{4,5},{5,4},{6,7},{7,6},{8,9},{9,8},{10,11... | collective-permute-start | bytes 1572872 | tf_op jit(solution)/shard_map/ppermute | solution.py:44
  53.8 11.7 %collective-permute-start.4 = (bf16[4,2,32,1024]{3,2,1,0:T(8,128)(2,1)S(1)}, bf16[4,2,32,1024]{3,2,1,0:T(8,128)(2,1)}, u32[]{:S(2)}, u32[]{:S(2)}) collective-permute-start(bf16[4,2,32,1024]{3,2,1,0:T(8,128)(2,1)S(1)} %collective-permute-done.refs_5_.refs_9_), channel_id=1, source_target_pairs={{0,1},{1,0},{2,3},{3,2},{4,5},{5,4},{6,7},{7,6},{8,9},{9,8},{10,11... | collective-permute-start | bytes 1572872 | tf_op jit(solution)/shard_map/ppermute | solution.py:44
  57.8 7.7 %collective-permute-start.5 = (bf16[4,2,32,1024]{3,2,1,0:T(8,128)(2,1)S(1)}, bf16[4,2,32,1024]{3,2,1,0:T(8,128)(2,1)}, u32[]{:S(2)}, u32[]{:S(2)}) collective-permute-start(bf16[4,2,32,1024]{3,2,1,0:T(8,128)(2,1)S(1)} %collective-permute-done.1.refs_6_.refs_10_), channel_id=1, source_target_pairs={{0,1},{1,0},{2,3},{3,2},{4,5},{5,4},{6,7},{7,6},{8,9},{9,8},{10,11... | collective-permute-start | bytes 1572872 | tf_op jit(solution)/shard_map/ppermute | solution.py:44
  85.9 17.4 %collective-permute-start.7 = (bf16[4,3,32,1024]{3,2,1,0:T(8,128)(2,1)S(1)}, bf16[4,3,32,1024]{3,2,1,0:T(8,128)(2,1)S(1)}, u32[]{:S(2)}, u32[]{:S(2)}) collective-permute-start(bf16[4,3,32,1024]{3,2,1,0:T(8,128)(2,1)S(1)} %all-to-all-done.1.refs_2_.refs_11_.refs_16_), channel_id=1, source_target_pairs={{0,4},{4,0},{8,12},{12,8},{16,20},{20,16},{24,28},{28,24},{1,5},{5... | collective-permute-start | bytes 2359304 | tf_op jit(solution)/shard_map/ppermute | solution.py:44
  87.6 14.5 %collective-permute-start.14 = (bf16[2,528,128]{2,1,0:T(8,128)(2,1)S(1)}, bf16[2,528,128]{2,1,0:T(8,128)(2,1)S(1)}, u32[]{:S(2)}, u32[]{:S(2)}) collective-permute-start(bf16[2,528,128]{2,1,0:T(8,128)(2,1)S(1)} %pad_maximum_fusion.2), channel_id=1, source_target_pairs={{0,4},{4,8},{8,12},{12,16},{16,20},{20,24},{24,28},{1,5},{5,9},{9,... | collective-permute-start | bytes 811016 | tf_op jit(solution)/shard_map/ppermute | solution.py:878
  91.3 24.1 %collective-permute-start.8 = (bf16[4,3,32,1024]{3,2,1,0:T(8,128)(2,1)S(1)}, bf16[4,3,32,1024]{3,2,1,0:T(8,128)(2,1)S(1)}, u32[]{:S(2)}, u32[]{:S(2)}) collective-permute-start(bf16[4,3,32,1024]{3,2,1,0:T(8,128)(2,1)S(1)} %all-to-all-done.1.refs_2_.refs_11_.refs_16_), channel_id=1, source_target_pairs={{0,2},{1,3},{2,0},{3,1},{4,6},{5,7},{6,4},{7,5},{8,10},{9,11},{10,... | collective-permute-start | bytes 2359304 | tf_op jit(solution)/shard_map/ppermute | solution.py:44
  103.4 16.8 %collective-permute-start.9 = (bf16[4,3,32,1024]{3,2,1,0:T(8,128)(2,1)S(1)}, bf16[4,3,32,1024]{3,2,1,0:T(8,128)(2,1)S(1)}, u32[]{:S(2)}, u32[]{:S(2)}) collective-permute-start(bf16[4,3,32,1024]{3,2,1,0:T(8,128)(2,1)S(1)} %collective-permute-done.7.refs_3_.refs_12_.refs_17_), channel_id=1, source_target_pairs={{0,2},{1,3},{2,0},{3,1},{4,6},{5,7},{6,4},{7,5},{8,10},{9,11},{10,... | collective-permute-start | bytes 2359304 | tf_op jit(solution)/shard_map/ppermute | solution.py:44
  105.3 7.9 %collective-permute-start.15 = (bf16[2,528,128]{2,1,0:T(8,128)(2,1)S(1)}, bf16[2,528,128]{2,1,0:T(8,128)(2,1)S(1)}, u32[]{:S(2)}, u32[]{:S(2)}) collective-permute-start(bf16[2,528,128]{2,1,0:T(8,128)(2,1)S(1)} %pad_maximum_fusion.3), channel_id=1, source_target_pairs={{0,8},{4,12},{8,16},{12,20},{16,24},{20,28},{1,9},{5,13},{9,17},{1... | collective-permute-start | bytes 811016 | tf_op jit(solution)/shard_map/ppermute | solution.py:878
  109.2 24.1 %collective-permute-start.10 = (bf16[4,3,32,1024]{3,2,1,0:T(8,128)(2,1)S(1)}, bf16[4,3,32,1024]{3,2,1,0:T(8,128)(2,1)}, u32[]{:S(2)}, u32[]{:S(2)}) collective-permute-start(bf16[4,3,32,1024]{3,2,1,0:T(8,128)(2,1)S(1)} %all-to-all-done.1.refs_2_.refs_11_.refs_16_), channel_id=1, source_target_pairs={{0,1},{1,0},{2,3},{3,2},{4,5},{5,4},{6,7},{7,6},{8,9},{9,8},{10,11... | collective-permute-start | bytes 2359304 | tf_op jit(solution)/shard_map/ppermute | solution.py:44
  115.3 19.8 %collective-permute-start.11 = (bf16[4,3,32,1024]{3,2,1,0:T(8,128)(2,1)S(1)}, bf16[4,3,32,1024]{3,2,1,0:T(8,128)(2,1)}, u32[]{:S(2)}, u32[]{:S(2)}) collective-permute-start(bf16[4,3,32,1024]{3,2,1,0:T(8,128)(2,1)S(1)} %collective-permute-done.7.refs_3_.refs_12_.refs_17_), channel_id=1, source_target_pairs={{0,1},{1,0},{2,3},{3,2},{4,5},{5,4},{6,7},{7,6},{8,9},{9,8},{10,11... | collective-permute-start | bytes 2359304 | tf_op jit(solution)/shard_map/ppermute | solution.py:44
  115.4 19.7 %collective-permute-start.12 = (bf16[4,3,32,1024]{3,2,1,0:T(8,128)(2,1)S(1)}, bf16[4,3,32,1024]{3,2,1,0:T(8,128)(2,1)}, u32[]{:S(2)}, u32[]{:S(2)}) collective-permute-start(bf16[4,3,32,1024]{3,2,1,0:T(8,128)(2,1)S(1)} %collective-permute-done.8.refs_4_.refs_13_.refs_18_), channel_id=1, source_target_pairs={{0,1},{1,0},{2,3},{3,2},{4,5},{5,4},{6,7},{7,6},{8,9},{9,8},{10,11... | collective-permute-start | bytes 2359304 | tf_op jit(solution)/shard_map/ppermute | solution.py:44
  120.2 14.9 %collective-permute-start.13 = (bf16[4,3,32,1024]{3,2,1,0:T(8,128)(2,1)S(1)}, bf16[4,3,32,1024]{3,2,1,0:T(8,128)(2,1)}, u32[]{:S(2)}, u32[]{:S(2)}) collective-permute-start(bf16[4,3,32,1024]{3,2,1,0:T(8,128)(2,1)S(1)} %collective-permute-done.9.refs_5_.refs_14_.refs_19_), channel_id=1, source_target_pairs={{0,1},{1,0},{2,3},{3,2},{4,5},{5,4},{6,7},{7,6},{8,9},{9,8},{10,11... | collective-permute-start | bytes 2359304 | tf_op jit(solution)/shard_map/ppermute | solution.py:44
  121.1 10.3 %collective-permute-start.16 = (bf16[2,528,128]{2,1,0:T(8,128)(2,1)}, bf16[2,528,128]{2,1,0:T(8,128)(2,1)}, u32[]{:S(2)}, u32[]{:S(2)}) collective-permute-start(bf16[2,528,128]{2,1,0:T(8,128)(2,1)} %pad_maximum_fusion.4), channel_id=1, source_target_pairs={{0,16},{4,20},{8,24},{12,28},{1,17},{5,21},{9,25},{13,29},{2,18},{... | collective-permute-start | bytes 811016 | tf_op jit(solution)/shard_map/ppermute | solution.py:878
  131.4 28.8 %collective-permute-start.18 = (bf16[512,1024]{1,0:T(8,128)(2,1)}, bf16[512,1024]{1,0:T(8,128)(2,1)}, u32[]{:S(2)}, u32[]{:S(2)}) collective-permute-start(bf16[512,1024]{1,0:T(8,128)(2,1)} %bitcast.149), channel_id=1, source_target_pairs={{0,1},{1,0},{2,3},{3,2},{4,5},{5,4},{6,7},{7,6},{8,9},{9,8},{10,11... | collective-permute-start | bytes 3145736 | tf_op jit(solution)/shard_map/ppermute | solution.py:44
  133.3 26.9 %collective-permute-start.17 = (bf16[512,1024]{1,0:T(8,128)(2,1)}, bf16[512,1024]{1,0:T(8,128)(2,1)}, u32[]{:S(2)}, u32[]{:S(2)}) collective-permute-start(bf16[512,1024]{1,0:T(8,128)(2,1)} %bitcast.150), channel_id=1, source_target_pairs={{0,2},{1,3},{2,0},{3,1},{4,6},{5,7},{6,4},{7,5},{8,10},{9,11},{10,... | collective-permute-start | bytes 3145736 | tf_op jit(solution)/shard_map/ppermute | solution.py:44
  159.9 25.6 %collective-permute-start.21 = (bf16[512,1024]{1,0:T(8,128)(2,1)}, bf16[512,1024]{1,0:T(8,128)(2,1)S(1)}, u32[]{:S(2)}, u32[]{:S(2)}) collective-permute-start(bf16[512,1024]{1,0:T(8,128)(2,1)} %get-tuple-element.92.refs_1_), channel_id=1, source_target_pairs={{0,2},{1,3},{2,0},{3,1},{4,6},{5,7},{6,4},{7,5},{8,10},{9,11},{10,... | collective-permute-start | bytes 3145736 | tf_op jit(solution)/shard_map/ppermute | solution.py:44
  180.3 5.1 %collective-permute-start.20 = (bf16[512,1024]{1,0:T(8,128)(2,1)}, bf16[512,1024]{1,0:T(8,128)(2,1)S(1)}, u32[]{:S(2)}, u32[]{:S(2)}) collective-permute-start(bf16[512,1024]{1,0:T(8,128)(2,1)} %get-tuple-element.96), channel_id=1, source_target_pairs={{0,1},{1,0},{2,3},{3,2},{4,5},{5,4},{6,7},{7,6},{8,9},{9,8},{10,11... | collective-permute-start | bytes 3145736 | tf_op jit(solution)/shard_map/ppermute | solution.py:44
  180.6 7.9 %collective-permute-start.23 = (bf16[512,1024]{1,0:T(8,128)(2,1)}, bf16[512,1024]{1,0:T(8,128)(2,1)S(1)}, u32[]{:S(2)}, u32[]{:S(2)}) collective-permute-start(bf16[512,1024]{1,0:T(8,128)(2,1)} %collective-permute-done.17.refs_3_.refs_7_), channel_id=1, source_target_pairs={{0,1},{1,0},{2,3},{3,2},{4,5},{5,4},{6,7},{7,6},{8,9},{9,8},{10,11... | collective-permute-start | bytes 3145736 | tf_op jit(solution)/shard_map/ppermute | solution.py:44
  211.9 25.3 %collective-permute-start.25 = (bf16[512,1024]{1,0:T(8,128)(2,1)S(1)}, bf16[512,1024]{1,0:T(8,128)(2,1)S(1)}, u32[]{:S(2)}, u32[]{:S(2)}) collective-permute-start(bf16[512,1024]{1,0:T(8,128)(2,1)S(1)} %add_convert_fusion.9), channel_id=1, source_target_pairs={{0,2},{1,3},{2,0},{3,1},{4,6},{5,7},{6,4},{7,5},{8,10},{9,11},{10,... | collective-permute-start | bytes 3145736 | tf_op jit(solution)/shard_map/ppermute | solution.py:44
  255.6 18.6 %collective-permute-start.29 = (bf16[2,528,128]{2,1,0:T(8,128)(2,1)S(1)}, bf16[2,528,128]{2,1,0:T(8,128)(2,1)S(1)}, u32[]{:S(2)}, u32[]{:S(2)}) collective-permute-start(bf16[2,528,128]{2,1,0:T(8,128)(2,1)S(1)} %pad_maximum_fusion.1), channel_id=1, source_target_pairs={{4,0},{8,4},{12,8},{16,12},{20,16},{24,20},{28,24},{5,1},{9,5},{13... | collective-permute-start | bytes 811016 | tf_op jit(solution)/shard_map/ppermute | solution.py:878
  256.9 46.1 %collective-permute-start.27 = (bf16[512,1024]{1,0:T(8,128)(2,1)}, bf16[512,1024]{1,0:T(8,128)(2,1)}, u32[]{:S(2)}, u32[]{:S(2)}) collective-permute-start(bf16[512,1024]{1,0:T(8,128)(2,1)} %get-tuple-element.115), channel_id=1, source_target_pairs={{0,1},{1,0},{2,3},{3,2},{4,5},{5,4},{6,7},{7,6},{8,9},{9,8},{10,11... | collective-permute-start | bytes 3145736 | tf_op jit(solution)/shard_map/ppermute | solution.py:44
  284.4 22.2 %collective-permute-start.30 = (bf16[4,3,64,1024]{3,2,1,0:T(8,128)(2,1)}, bf16[4,3,64,1024]{3,2,1,0:T(8,128)(2,1)}, u32[]{:S(2)}, u32[]{:S(2)}) collective-permute-start(bf16[4,3,64,1024]{3,2,1,0:T(8,128)(2,1)} %get-tuple-element.124), channel_id=1, source_target_pairs={{0,1},{1,0},{2,3},{3,2},{4,5},{5,4},{6,7},{7,6},{8,9},{9,8},{10,11... | collective-permute-start | bytes 4718600 | tf_op jit(solution)/shard_map/ppermute | solution.py:44
  285.0 17.1 %collective-permute-start.31 = (bf16[2,528,128]{2,1,0:T(8,128)(2,1)S(1)}, bf16[2,528,128]{2,1,0:T(8,128)(2,1)S(1)}, u32[]{:S(2)}, u32[]{:S(2)}) collective-permute-start(bf16[2,528,128]{2,1,0:T(8,128)(2,1)S(1)} %pad_maximum_fusion.5), channel_id=1, source_target_pairs={{8,0},{12,4},{16,8},{20,12},{24,16},{28,20},{9,1},{13,5},{17,9},{2... | collective-permute-start | bytes 811016 | tf_op jit(solution)/shard_map/ppermute | solution.py:878
  286.3 68.0 %collective-permute-start.39 = (bf16[4,3,64,1024]{3,2,1,0:T(8,128)(2,1)}, bf16[4,3,64,1024]{3,2,1,0:T(8,128)(2,1)S(1)}, u32[]{:S(2)}, u32[]{:S(2)}) collective-permute-start(bf16[4,3,64,1024]{3,2,1,0:T(8,128)(2,1)} %get-tuple-element.141), channel_id=1, source_target_pairs={{0,1},{1,0},{2,3},{3,2},{4,5},{5,4},{6,7},{7,6},{8,9},{9,8},{10,11... | collective-permute-start | bytes 4718600 | tf_op jit(solution)/shard_map/ppermute | solution.py:44
  304.7 25.0 %collective-permute-start.28 = (bf16[512,1024]{1,0:T(8,128)(2,1)S(1)}, bf16[512,1024]{1,0:T(8,128)(2,1)S(1)}, u32[]{:S(2)}, u32[]{:S(2)}) collective-permute-start(bf16[512,1024]{1,0:T(8,128)(2,1)S(1)} %add_convert_fusion.7), channel_id=1, source_target_pairs={{0,2},{1,3},{2,0},{3,1},{4,6},{5,7},{6,4},{7,5},{8,10},{9,11},{10,... | collective-permute-start | bytes 3145736 | tf_op jit(solution)/shard_map/ppermute | solution.py:44
  305.4 20.7 %collective-permute-start.32 = (bf16[2,528,128]{2,1,0:T(8,128)(2,1)S(1)}, bf16[2,528,128]{2,1,0:T(8,128)(2,1)S(1)}, u32[]{:S(2)}, u32[]{:S(2)}) collective-permute-start(bf16[2,528,128]{2,1,0:T(8,128)(2,1)S(1)} %pad_maximum_fusion.6), channel_id=1, source_target_pairs={{16,0},{20,4},{24,8},{28,12},{17,1},{21,5},{25,9},{29,13},{18,2},{... | collective-permute-start | bytes 811016 | tf_op jit(solution)/shard_map/ppermute | solution.py:878
  310.0 44.4 %collective-permute-start.40 = (bf16[4,3,64,1024]{3,2,1,0:T(8,128)(2,1)}, bf16[4,3,64,1024]{3,2,1,0:T(8,128)(2,1)}, u32[]{:S(2)}, u32[]{:S(2)}) collective-permute-start(bf16[4,3,64,1024]{3,2,1,0:T(8,128)(2,1)} %add_convert_fusion.2), channel_id=1, source_target_pairs={{0,4},{4,0},{8,12},{12,8},{16,20},{20,16},{24,28},{28,24},{1,5},{5... | collective-permute-start | bytes 4718600 | tf_op jit(solution)/shard_map/ppermute | solution.py:44
  358.0 67.4 %all-to-all-start.2 = ((bf16[4,3,64,1024]{3,2,1,0:T(8,128)(2,1)}), bf16[4,3,64,1024]{3,2,1,0:T(8,128)(2,1)S(1)}, u32[]{:S(2)}, u32[]{:S(2)}) async-start(bf16[4,3,64,1024]{3,2,1,0:T(8,128)(2,1)} %add_convert_fusion), calls=%async_computation.2 | async-start | bytes 3145728 | tf_op jit(solution)/shard_map/all_to_all | solution.py:109
  363.3 29.6 %collective-permute-start.42 = (bf16[4,2,64,1024]{3,2,1,0:T(8,128)(2,1)S(1)}, bf16[4,2,64,1024]{3,2,1,0:T(8,128)(2,1)}, u32[]{:S(2)}, u32[]{:S(2)}) collective-permute-start(bf16[4,2,64,1024]{3,2,1,0:T(8,128)(2,1)S(1)} %add_convert_fusion.5), channel_id=1, source_target_pairs={{0,4},{4,0},{8,12},{12,8},{16,20},{20,16},{24,28},{28,24},{1,5},{5... | collective-permute-start | bytes 3145736 | tf_op jit(solution)/shard_map/ppermute | solution.py:44
  365.1 27.8 %collective-permute-start.41 = (bf16[4,2,64,1024]{3,2,1,0:T(8,128)(2,1)}, bf16[4,2,64,1024]{3,2,1,0:T(8,128)(2,1)}, u32[]{:S(2)}, u32[]{:S(2)}) collective-permute-start(bf16[4,2,64,1024]{3,2,1,0:T(8,128)(2,1)} %get-tuple-element.145), channel_id=1, source_target_pairs={{0,1},{1,0},{2,3},{3,2},{4,5},{5,4},{6,7},{7,6},{8,9},{9,8},{10,11... | collective-permute-start | bytes 3145736 | tf_op jit(solution)/shard_map/ppermute | solution.py:44
  383.5 3.7 collective-permute-start.35
  387.2 3.7 collective-permute-start.36
  387.5 41.1 %collective-permute-start.26 = (bf16[512,1024]{1,0:T(8,128)(2,1)}, bf16[512,1024]{1,0:T(8,128)(2,1)}, u32[]{:S(2)}, u32[]{:S(2)}) collective-permute-start(bf16[512,1024]{1,0:T(8,128)(2,1)} %get-tuple-element.112), channel_id=1, source_target_pairs={{0,1},{1,0},{2,3},{3,2},{4,5},{5,4},{6,7},{7,6},{8,9},{9,8},{10,11... | collective-permute-start | bytes 3145736 | tf_op jit(solution)/shard_map/ppermute | solution.py:44
  391.0 11.0 %collective-permute-start.37 = (f32[3,1024]{1,0:T(4,128)S(1)}, f32[3,1024]{1,0:T(4,128)S(1)}, u32[]{:S(2)}, u32[]{:S(2)}) collective-permute-start(f32[3,1024]{1,0:T(4,128)S(1)} %add.220), channel_id=1, source_target_pairs={{0,8},{4,12},{8,0},{12,4},{16,24},{20,28},{24,16},{28,20},{1,9},{5... | collective-permute-start | bytes 36872 | tf_op jit(solution)/shard_map/ppermute | solution.py:44
  395.5 30.2 %collective-permute-start.43 = (bf16[3,704,128]{2,1,0:T(8,128)(2,1)}, bf16[3,704,128]{2,1,0:T(8,128)(2,1)}, u32[]{:S(2)}, u32[]{:S(2)}) collective-permute-start(bf16[3,704,128]{2,1,0:T(8,128)(2,1)} %bitcast.162), channel_id=1, source_target_pairs={{0,2},{1,3},{2,0},{3,1},{4,6},{5,7},{6,4},{7,5},{8,10},{9,11},{10,... | collective-permute-start | bytes 1622024 | tf_op jit(solution)/shard_map/ppermute | solution.py:44
  398.2 11.9 %collective-permute-start.46 = (bf16[2,64,1024]{2,1,0:T(8,128)(2,1)}, bf16[2,64,1024]{2,1,0:T(8,128)(2,1)}, u32[]{:S(2)}, u32[]{:S(2)}) collective-permute-start(bf16[2,64,1024]{2,1,0:T(8,128)(2,1)} %get-tuple-element.210), channel_id=1, source_target_pairs={{0,8},{4,12},{8,0},{12,4},{16,24},{20,28},{24,16},{28,20},{1,9},{5... | collective-permute-start | bytes 786440 | tf_op jit(solution)/shard_map/ppermute | solution.py:106
  398.2 16.8 %collective-permute-start.48 = (bf16[2,64,1024]{2,1,0:T(8,128)(2,1)}, bf16[2,64,1024]{2,1,0:T(8,128)(2,1)}, u32[]{:S(2)}, u32[]{:S(2)}) collective-permute-start(bf16[2,64,1024]{2,1,0:T(8,128)(2,1)} %get-tuple-element.211), channel_id=1, source_target_pairs={{0,24},{4,28},{8,16},{12,20},{16,8},{20,12},{24,0},{28,4},{1,25},{... | collective-permute-start | bytes 786440 | tf_op jit(solution)/shard_map/ppermute | solution.py:106
  402.0 21.4 %collective-permute-start.47 = (bf16[2,64,1024]{2,1,0:T(8,128)(2,1)S(1)}, bf16[2,64,1024]{2,1,0:T(8,128)(2,1)}, u32[]{:S(2)}, u32[]{:S(2)}) collective-permute-start(bf16[2,64,1024]{2,1,0:T(8,128)(2,1)S(1)} %get-tuple-element.212), channel_id=1, source_target_pairs={{0,16},{4,20},{8,24},{12,28},{16,0},{20,4},{24,8},{28,12},{1,17},{... | collective-permute-start | bytes 786440 | tf_op jit(solution)/shard_map/ppermute | solution.py:106
  410.1 21.5 %collective-permute-start.38 = (f32[3,1024]{1,0:T(4,128)S(1)}, f32[3,1024]{1,0:T(4,128)S(1)}, u32[]{:S(2)}, u32[]{:S(2)}) collective-permute-start(f32[3,1024]{1,0:T(4,128)S(1)} %add.221), channel_id=1, source_target_pairs={{0,16},{4,20},{8,24},{12,28},{16,0},{20,4},{24,8},{28,12},{1,17},{... | collective-permute-start | bytes 36872 | tf_op jit(solution)/shard_map/ppermute | solution.py:44
  424.7 9.4 %collective-permute-start.49 = (bf16[2,64,1024]{2,1,0:T(8,128)(2,1)S(1)}, bf16[2,64,1024]{2,1,0:T(8,128)(2,1)}, u32[]{:S(2)}, u32[]{:S(2)}) collective-permute-start(bf16[2,64,1024]{2,1,0:T(8,128)(2,1)S(1)} %fusion.14), channel_id=1, source_target_pairs={{0,2},{1,3},{2,0},{3,1},{4,6},{5,7},{6,4},{7,5},{8,10},{9,11},{10,... | collective-permute-start | bytes 786440 | tf_op jit(solution)/shard_map/ppermute | solution.py:44
  427.1 11.1 %collective-permute-start.44 = (bf16[3,64,1024]{2,1,0:T(8,128)(2,1)S(1)}, bf16[3,64,1024]{2,1,0:T(8,128)(2,1)S(1)}, u32[]{:S(2)}, u32[]{:S(2)}) collective-permute-start(bf16[3,64,1024]{2,1,0:T(8,128)(2,1)S(1)} %reduce_sum.12), channel_id=1, source_target_pairs={{0,2},{1,3},{2,0},{3,1},{4,6},{5,7},{6,4},{7,5},{8,10},{9,11},{10,... | collective-permute-start | bytes 1179656 | tf_op jit(solution)/shard_map/ppermute | solution.py:44
  435.1 4.3 collective-permute-start.50
  (42 other events, 426.0 us)
Sparse Core Ops, SparseCore 0:
  11.3 90.3 all-gather.2
  237.3 106.4 reduce-scatter.1
